TPU v7x, 256 devices: a whole 4x4x8 slice. The times are simulated.
256 devices in a mesh: row: 32 (over z, x_lo, core), blk: 8 (over x_hi, y).
Axes of the slice: x: 4 (x_hi: 2, x_lo: 2; x = x_hi * 2 + x_lo), y: 4, z: 8, core: 2. Of those that a mesh axis runs over, the one named last changes fastest.
Arguments:
- features: bfloat16 [32768, 256], P(('row', 'blk')), may hold values from -6 to 6
- grad_out: bfloat16 [32768, 256], P(('row', 'blk')), may hold values from -6 to 6
- w_self: bfloat16 [256, 256], replicated, may hold values from -0.375 to 0.375
- w_neigh: bfloat16 [256, 256], replicated, may hold values from -0.375 to 0.375
- tiles: bfloat16 [256, 192, 128, 128], P(('row', 'blk')), may hold values from 0 to 1
- tile_rows: int32 [256, 192], P(('row', 'blk')), may hold values from 0 to 7, as said below
- tile_cols: int32 [256, 192], P(('row', 'blk')), may hold values from 0 to 31, as said below
- tile_counts: int32 [256], P(('row', 'blk')), may hold values from 32 to 192, as said below
- degrees: int32 [32768], P(('row', 'blk')), may hold values from 8 to 127
Outputs:
- grad_x: bfloat16 [32768, 256], P(('row', 'blk'))
- grad_w_self: float32 [256, 256], replicated
- grad_w_neigh: float32 [256, 256], replicated
Inputs may be any that keep to these rules, and one draw needn't show every extreme that they name: `tile_counts`: live tile slots of each device; some device is full in every draw. `tile_rows`: the first 8 slots of each device name every row tile once. `tile_cols`: the first 32 slots of each device name every column tile once.
All inputs are finite; a program needn't handle non-finite values.
Results may differ from a plain program's by a relative error of at most 0.0046.
Values may be sent and summed in bfloat16 or wider, within the bound.
No kernel may reach another device: no remote copies, remote signals or barrier semaphores. Data moves between devices by JAX's collectives and lax.ppermute only.
A program may use at most 128 MiB of HBM per device.

v0:
```python
import jax
import jax.numpy as jnp
from jax import lax
from jax.sharding import PartitionSpec as P


def tile_products(
    tile_data, row_index, col_index, live_count, class_feats, scaled_group, tile_size
):
    feat_width = class_feats.shape[1]
    row_tiles = scaled_group.shape[0] // tile_size
    col_tiles = class_feats.shape[0] // tile_size
    feat_tiles = class_feats.reshape(col_tiles, tile_size, feat_width)
    scaled_tiles = scaled_group.reshape(row_tiles, tile_size, feat_width)
    capacity = tile_data.shape[0]
    block_size = min(64, capacity)

    def compute(accums, block_start):
        agg_acc, column_acc = accums
        tile_block = lax.dynamic_slice_in_dim(tile_data, block_start, block_size, 0)
        row_slot = lax.dynamic_slice_in_dim(row_index, block_start, block_size, 0)
        col_slot = lax.dynamic_slice_in_dim(col_index, block_start, block_size, 0)
        alive_mask = (block_start + jnp.arange(block_size, dtype=jnp.int32) < live_count).astype(
            jnp.float32
        )
        forward_part = jnp.einsum(
            "tij,tjf->tif", tile_block, feat_tiles[col_slot], preferred_element_type=jnp.float32
        )
        agg_acc = agg_acc.at[row_slot].add(forward_part * alive_mask[:, None, None])
        backward_part = jnp.einsum(
            "tij,tif->tjf", tile_block, scaled_tiles[row_slot], preferred_element_type=jnp.float32
        )
        column_acc = column_acc.at[col_slot].add(backward_part * alive_mask[:, None, None])
        return (agg_acc, column_acc)

    def one_block(accums, block_start):
        return (compute(accums, block_start), None)

    start = (
        jnp.zeros((row_tiles, tile_size, feat_width), jnp.float32),
        jnp.zeros((col_tiles, tile_size, feat_width), jnp.float32),
    )
    starts = jnp.arange(capacity // block_size, dtype=jnp.int32) * block_size
    (agg_acc, column_acc), _ = lax.scan(one_block, start, starts)
    return (
        agg_acc.reshape(row_tiles * tile_size, feat_width),
        column_acc.reshape(col_tiles * tile_size, feat_width),
    )


def shards(features, grad_out, w_self, w_neigh, tiles, tile_rows, tile_cols, tile_counts, degrees):
    highest = lax.Precision.HIGHEST
    span_rows = features.shape[0]
    row_count = lax.axis_size("row")
    blk_count = lax.axis_size("blk")
    node_total = span_rows * row_count * blk_count
    tile_size = tiles.shape[2]
    degree_f = degrees.astype(jnp.float32)[:, None]
    class_feats = lax.all_gather(features, "row", axis=0, tiled=True)
    scaled = (jnp.dot(grad_out, w_neigh.T, preferred_element_type=jnp.float32) / degree_f).astype(
        jnp.bfloat16
    )
    scaled_group = lax.all_gather(scaled, "blk", axis=0, tiled=True)
    agg_partial, column_partial = tile_products(
        tiles[0], tile_rows[0], tile_cols[0], tile_counts[0], class_feats, scaled_group, tile_size
    )
    grad_self = jnp.einsum("nf,ng->fg", features, grad_out, preferred_element_type=jnp.float32)
    agg = lax.psum_scatter(agg_partial, "blk", scatter_dimension=0, tiled=True) / degree_f
    grad_neigh = jnp.dot(agg.T, grad_out.astype(jnp.float32), precision=highest)
    grad_self, grad_neigh = lax.psum((grad_self, grad_neigh), ("row", "blk"))
    column_sum = lax.psum_scatter(column_partial, "row", scatter_dimension=0, tiled=True)
    grad_x = (jnp.dot(grad_out, w_self.T, preferred_element_type=jnp.float32) + column_sum).astype(
        jnp.bfloat16
    )
    return (grad_x, grad_self / node_total, grad_neigh / node_total)


def solution(mesh):
    in_specs = (
        P(("row", "blk"), None),
        P(("row", "blk"), None),
        P(),
        P(),
        P(("row", "blk"), None, None, None),
        P(("row", "blk"), None),
        P(("row", "blk"), None),
        P(("row", "blk")),
        P(("row", "blk")),
    )
    out_specs = (P(("row", "blk"), None), P(), P())
    return jax.shard_map(shards, mesh=mesh, in_specs=in_specs, out_specs=out_specs, check_vma=False)
```

profile of v0, /device:TPU:1, one launch (start us, length us, event | category | flops | bytes accessed | tf_op | source)
XLA Modules:
  0.0 718.8 jit_solution(17875996025009958938)
XLA Ops:
  8.6 1.0 fusion.5
  9.7 30.5 %all_gather.7 = bf16[1024,256]{1,0:T(8,128)(2,1)S(1)} all-gather(bf16[128,256]{1,0:T(8,128)(2,1)S(1)} %fusion.5), channel_id=1, replica_groups=mesh['row'=32,'blk'=8] {'blk'}, dimensions={0}, use_global_device_ids=true | all-gather | bytes 589824 | tf_op jit(solution)/shard_map/all_gather | solution.py:63
  40.2 38.7 %all-gather.2.cloned.1.call-done = bf16[4096,256]{1,0:T(8,128)(2,1)} async-done(((bf16[128,256]{1,0:T(8,128)(2,1)}), bf16[4096,256]{1,0:T(8,128)(2,1)}) %all-gather.2.cloned.1.call-update) | async-done | bytes 2097168 | tf_op jit(solution)/shard_map/all_gather | solution.py:59
  78.9 2.4 broadcast_in_dim.18
  81.4 173.1 %while.12 = (s32[]{:T(128)}, f32[8,128,256]{2,1,0:T(8,128)S(1)}, f32[32,128,256]{2,1,0:T(8,128)}, s32[3]{0:T(128)S(1)}, s32[192]{0:T(256)S(1)}, /*index=5*/bf16[...) while((s32[]{:T(128)}, f32[8,128,256]{2,1,0:T(8,128)S(1)}, ...), condition=%wide.region_3.4_spmd, body=%wide.region_0.3_spmd.sunk | while | flops 1082132992 | bytes 96480704 | solution.py:44
  84.0 1.3 compare_convert_fusion.2
  85.3 4.4 gather_fusion
  89.7 7.3 %broadcast_multiply_fusion.6 = f32[64,128,256]{2,1,0:T(8,128)} fusion(f32[64]{0:T(128)S(1)} %compare_convert_fusion.2, bf16[64,128,256]{2,1,0:T(8,128)(2,1)} %gather_fusion, bf16[192,128,128]{2,1,0:T(8,128)(2,1)} %get-tuple-element.180, s32[]{:T(128)S(6)} %select_n.18), kind=kOutput, calls=%fused_computation.5.clone.1 | convolution fusion | flops 538968064 | bytes 14680324 | tf_op jit(solution)/shard_map/while/body/eval_jaxpr/tij,tjf->tif/dot_general | solution.py:26
  97.0 12.4 %scatter_fusion = f32[8,128,256]{2,1,0:T(8,128)S(1)} fusion(f32[8,128,256]{2,1,0:T(8,128)S(1)} %get-tuple-element.163, s32[64]{0:T(128)S(1)} %get-tuple-element.147, f32[64,128,256]{2,1,0:T(8,128)} %broadcast_multiply_fusion.6), kind=kCustom, calls=%fused_computation.2.clone.1 | custom fusion | flops 2097152 | bytes 25166080 | tf_op jit(solution)/shard_map/while/body/eval_jaxpr/scatter-add | solution.py:29
  109.4 2.8 gather_fusion.1
  112.1 7.6 %broadcast_multiply_fusion.7 = f32[64,128,256]{2,1,0:T(8,128)} fusion(f32[64]{0:T(128)S(1)} %compare_convert_fusion.2, bf16[64,128,256]{2,1,0:T(8,128)(2,1)} %gather_fusion.1, bf16[192,128,128]{2,1,0:T(8,128)(2,1)} %get-tuple-element.180, s32[]{:T(128)S(6)} %select_n.18), kind=kOutput, calls=%fused_computation.4.clone.1 | convolution fusion | flops 538968064 | bytes 14680324 | tf_op jit(solution)/shard_map/while/body/eval_jaxpr/tij,tif->tjf/dot_general | solution.py:30
  119.7 19.5 %scatter_fusion.1 = f32[32,128,256]{2,1,0:T(8,128)} fusion(f32[32,128,256]{2,1,0:T(8,128)} %get-tuple-element.164, s32[64]{0:T(128)S(1)} %get-tuple-element.148, f32[64,128,256]{2,1,0:T(8,128)} %broadcast_multiply_fusion.7), kind=kCustom, calls=%fused_computation.3.clone.1 | custom fusion | flops 2097152 | bytes 25166080 | tf_op jit(solution)/shard_map/while/body/eval_jaxpr/scatter-add | solution.py:33
  141.8 1.3 compare_convert_fusion.2
  143.2 4.4 gather_fusion
  147.5 7.3 %broadcast_multiply_fusion.6 = f32[64,128,256]{2,1,0:T(8,128)} fusion(f32[64]{0:T(128)S(1)} %compare_convert_fusion.2, bf16[64,128,256]{2,1,0:T(8,128)(2,1)} %gather_fusion, bf16[192,128,128]{2,1,0:T(8,128)(2,1)} %get-tuple-element.180, s32[]{:T(128)S(6)} %select_n.18), kind=kOutput, calls=%fused_computation.5.clone.1 | convolution fusion | flops 538968064 | bytes 14680324 | tf_op jit(solution)/shard_map/while/body/eval_jaxpr/tij,tjf->tif/dot_general | solution.py:26
  154.8 12.4 %scatter_fusion = f32[8,128,256]{2,1,0:T(8,128)S(1)} fusion(f32[8,128,256]{2,1,0:T(8,128)S(1)} %get-tuple-element.163, s32[64]{0:T(128)S(1)} %get-tuple-element.147, f32[64,128,256]{2,1,0:T(8,128)} %broadcast_multiply_fusion.6), kind=kCustom, calls=%fused_computation.2.clone.1 | custom fusion | flops 2097152 | bytes 25166080 | tf_op jit(solution)/shard_map/while/body/eval_jaxpr/scatter-add | solution.py:29
  167.2 2.8 gather_fusion.1
  170.0 7.6 %broadcast_multiply_fusion.7 = f32[64,128,256]{2,1,0:T(8,128)} fusion(f32[64]{0:T(128)S(1)} %compare_convert_fusion.2, bf16[64,128,256]{2,1,0:T(8,128)(2,1)} %gather_fusion.1, bf16[192,128,128]{2,1,0:T(8,128)(2,1)} %get-tuple-element.180, s32[]{:T(128)S(6)} %select_n.18), kind=kOutput, calls=%fused_computation.4.clone.1 | convolution fusion | flops 538968064 | bytes 14680324 | tf_op jit(solution)/shard_map/while/body/eval_jaxpr/tij,tif->tjf/dot_general | solution.py:30
  177.6 19.3 %scatter_fusion.1 = f32[32,128,256]{2,1,0:T(8,128)} fusion(f32[32,128,256]{2,1,0:T(8,128)} %get-tuple-element.164, s32[64]{0:T(128)S(1)} %get-tuple-element.148, f32[64,128,256]{2,1,0:T(8,128)} %broadcast_multiply_fusion.7), kind=kCustom, calls=%fused_computation.3.clone.1 | custom fusion | flops 2097152 | bytes 25166080 | tf_op jit(solution)/shard_map/while/body/eval_jaxpr/scatter-add | solution.py:33
  199.5 1.3 compare_convert_fusion.2
  200.8 4.4 gather_fusion
  205.2 7.3 %broadcast_multiply_fusion.6 = f32[64,128,256]{2,1,0:T(8,128)} fusion(f32[64]{0:T(128)S(1)} %compare_convert_fusion.2, bf16[64,128,256]{2,1,0:T(8,128)(2,1)} %gather_fusion, bf16[192,128,128]{2,1,0:T(8,128)(2,1)} %get-tuple-element.180, s32[]{:T(128)S(6)} %select_n.18), kind=kOutput, calls=%fused_computation.5.clone.1 | convolution fusion | flops 538968064 | bytes 14680324 | tf_op jit(solution)/shard_map/while/body/eval_jaxpr/tij,tjf->tif/dot_general | solution.py:26
  212.5 12.4 %scatter_fusion = f32[8,128,256]{2,1,0:T(8,128)S(1)} fusion(f32[8,128,256]{2,1,0:T(8,128)S(1)} %get-tuple-element.163, s32[64]{0:T(128)S(1)} %get-tuple-element.147, f32[64,128,256]{2,1,0:T(8,128)} %broadcast_multiply_fusion.6), kind=kCustom, calls=%fused_computation.2.clone.1 | custom fusion | flops 2097152 | bytes 25166080 | tf_op jit(solution)/shard_map/while/body/eval_jaxpr/scatter-add | solution.py:29
  224.9 2.8 gather_fusion.1
  227.6 7.6 %broadcast_multiply_fusion.7 = f32[64,128,256]{2,1,0:T(8,128)} fusion(f32[64]{0:T(128)S(1)} %compare_convert_fusion.2, bf16[64,128,256]{2,1,0:T(8,128)(2,1)} %gather_fusion.1, bf16[192,128,128]{2,1,0:T(8,128)(2,1)} %get-tuple-element.180, s32[]{:T(128)S(6)} %select_n.18), kind=kOutput, calls=%fused_computation.4.clone.1 | convolution fusion | flops 538968064 | bytes 14680324 | tf_op jit(solution)/shard_map/while/body/eval_jaxpr/tij,tif->tjf/dot_general | solution.py:30
  235.2 19.2 %scatter_fusion.1 = f32[32,128,256]{2,1,0:T(8,128)} fusion(f32[32,128,256]{2,1,0:T(8,128)} %get-tuple-element.164, s32[64]{0:T(128)S(1)} %get-tuple-element.148, f32[64,128,256]{2,1,0:T(8,128)} %broadcast_multiply_fusion.7), kind=kCustom, calls=%fused_computation.3.clone.1 | custom fusion | flops 2097152 | bytes 25166080 | tf_op jit(solution)/shard_map/while/body/eval_jaxpr/scatter-add | solution.py:33
  256.4 73.1 %reduce-scatter.5.cloned.1.call-done = f32[128,256]{1,0:T(8,128)} async-done(((f32[1024,256]{1,0:T(8,128)}), f32[128,256]{1,0:T(8,128)}) %reduce-scatter.5.cloned.1.call-update) | async-done | bytes 131088 | tf_op jit(solution)/shard_map/reduce_scatter | solution.py:68
  329.5 2.0 fusion.6
  332.1 256.6 %all-reduce.3.cloned.1.call-done = (f32[256,256]{1,0:T(8,128)}, f32[256,256]{1,0:T(8,128)}) async-done(((f32[256,256]{1,0:T(8,128)}, f32[256,256]{1,0:T(8,128)}), (f32[256,256]{1,0:T(8,128)}, f32[256,256]{1,0:T(8,128)})) %all-reduce.3.cloned.1.call-update) | async-done | bytes 524304 | tf_op jit(solution)/shard_map/psum | solution.py:70
  588.7 1.9 broadcast_multiply_fusion.2
  590.5 120.0 %reduce-scatter.3.cloned.1.call-done = f32[128,256]{1,0:T(8,128)} async-done(((f32[4096,256]{1,0:T(8,128)}), f32[128,256]{1,0:T(8,128)}) %reduce-scatter.3.cloned.1.call-update) | async-done | bytes 131088 | tf_op jit(solution)/shard_map/reduce_scatter | solution.py:71
  710.5 1.7 fusion.4
  (38 shorter events, 6.1 us)
Async XLA Ops:
  7.2 1.5 copy-start
  7.2 74.2 %copy-start.5 = (s32[1,192]{1,0:T(1,128)S(1)}, s32[1,192]{1,0:T(1,128)}, u32[]{:S(2)}) copy-start(s32[1,192]{1,0:T(1,128)} %param.16) | copy-start | bytes 2308
  7.2 74.2 %copy-start.6 = (s32[1,192]{1,0:T(1,128)S(1)}, s32[1,192]{1,0:T(1,128)}, u32[]{:S(2)}) copy-start(s32[1,192]{1,0:T(1,128)} %param.17) | copy-start | bytes 2308
  7.2 71.6 %all-gather.2.cloned.1.call-start = ((), (), s32[]{:S(2)}) async-start(), calls=%async_computation.2 | async-start | bytes 2162688 | tf_op jit(solution)/shard_map/all_gather | solution.py:59
  7.9 321.6 %reduce-scatter.5.cloned.1.call-start = ((), (), s32[]{:S(2)}) async-start(), calls=%async_computation.4 | async-start | bytes 1179648 | tf_op jit(solution)/shard_map/reduce_scatter | solution.py:68
  81.3 174.2 %copy-start.2 = (bf16[128,256]{1,0:T(8,128)(2,1)S(1)}, bf16[128,256]{1,0:T(8,128)(2,1)}, u32[]{:S(2)}) copy-start(bf16[128,256]{1,0:T(8,128)(2,1)} %param.11) | copy-start | bytes 196612
  81.3 174.2 %copy-start.3 = (bf16[128,256]{1,0:T(8,128)(2,1)S(1)}, bf16[128,256]{1,0:T(8,128)(2,1)}, u32[]{:S(2)}) copy-start(bf16[128,256]{1,0:T(8,128)(2,1)} %param.12) | copy-start | bytes 196612
  254.5 1.0 copy-start.1
  254.5 456.0 %copy-start.4 = (bf16[256,256]{1,0:T(8,128)(2,1)S(1)}, bf16[256,256]{1,0:T(8,128)(2,1)}, u32[]{:S(2)}) copy-start(bf16[256,256]{1,0:T(8,128)(2,1)} %param.13) | copy-start | bytes 393220
  255.5 333.2 %all-reduce.3.cloned.1.call-start = ((), (), s32[]{:S(2)}) async-start(), calls=%async_computation.5 | async-start | bytes 1048576 | tf_op jit(solution)/shard_map/psum | solution.py:70
  331.5 379.0 %reduce-scatter.3.cloned.1.call-start = ((), (), s32[]{:S(2)}) async-start(), calls=%async_computation.3 | async-start | bytes 4325376 | tf_op jit(solution)/shard_map/reduce_scatter | solution.py:71
Sparse Core Ops, SparseCore 0:
  9.9 68.8 all-gather.1
  255.6 73.8 reduce-scatter.4
  336.7 251.9 all-reduce.2
  591.2 119.2 reduce-scatter.2
where the time goes:
time: 723 us; the launch traced here: 719 us
  waiting for transfers between devices  490 us (68%)
  other arithmetic  102 us (14%)
  matrix products  50.3 us (7%)
  blocking collectives  30.5 us (4%)
  local copies, waits for them, and re-layouts  26.7 us (4%)
  between operations  13.8 us (2%)
    psum x1, waiting for transfers between devices, shards(): grad_self, grad_neigh = lax.psum((grad_self, grad_neigh), ('row', 'blk'))  257 us
    reduce_scatter x1, waiting for transfers between devices, shards(): lax.psum_scatter(column_partial, 'row', scatter_dimension=0, tiled=True)  120 us
    reduce_scatter x1, waiting for transfers between devices, shards(): lax.psum_scatter(agg_partial, 'blk', scatter_dimension=0, tiled=True)  73.1 us
    scatter-add x3, other arithmetic, compute(): column_acc.at[col_slot].add(backward_part * alive_mask[:, None, None])  58 us
    all_gather x1, waiting for transfers between devices, shards(): class_feats = lax.all_gather(features, 'row', axis=0, tiled=True)  38.7 us
    scatter-add x3, other arithmetic, compute(): agg_acc = agg_acc.at[row_slot].add(forward_part * alive_mask[:, None, None])  37.1 us
    all_gather x1, blocking collectives, shards(): scaled_group = lax.all_gather(scaled, 'blk', axis=0, tiled=True)  30.5 us
    dot_general x3, matrix products, compute(): jnp.einsum('tij,tif->tjf', tile_block, scaled_tiles[row_slot], preferred_...  22.7 us
  transfers between devices with their start and end apart: 4, of which 4 were waited for; matrix products, arithmetic and copies ran while one was open for 1% of the time, Pallas kernels for 0%

commit v1 on v0

v1 whole, which is shorter than its diff:
```python
import itertools

import jax
import jax.numpy as jnp
from jax import lax
from jax.experimental import pallas as pl
from jax.experimental.pallas import tpu as pltpu
from jax.sharding import PartitionSpec as P

PARTS = {"z": 8, "xl": 2, "core": 2, "xh": 2, "y": 4}
CHUNK = 16
DEG_ROWS = 16


def device_id(where):
    row = (where["z"] * 2 + where["xl"]) * 2 + where["core"]
    return row * 8 + where["xh"] * 4 + where["y"]


def groups_of(names):
    rest = [name for name in PARTS if name not in names]
    groups = []
    for fixed in itertools.product(*[range(PARTS[name]) for name in rest]):
        where = dict(zip(rest, fixed))
        group = []
        for moving in itertools.product(*[range(PARTS[name]) for name in names]):
            where.update(zip(names, moving))
            group.append(device_id(where))
        groups.append(group)
    return groups


def exchange(blocks, names):
    return lax.all_to_all(
        blocks, ("row", "blk"), 0, 0, axis_index_groups=groups_of(names), tiled=True
    )


def spread(block, names, count):
    return exchange(jnp.broadcast_to(block[None], (count,) + block.shape), names)


def swap_core(value):
    return lax.ppermute(value, "row", [(row, row ^ 1) for row in range(32)])


def sparse_kernel(rows, cols, meta, grads, tiles, mine, theirs, acc, lhs):
    step = pl.program_id(0)
    live = meta[0]
    core = meta[1]

    @pl.when(step == 0)
    def _():
        for k in range(8):
            grad_t = grads[k, 0:128, :].T.astype(jnp.float32)
            degree = grads[k, 128:129, 0:128].astype(jnp.float32)
            value = grad_t / degree
            high = value.astype(jnp.bfloat16)
            low = (value - high.astype(jnp.float32)).astype(jnp.bfloat16)
            lhs[k, :, 0:128] = high
            lhs[k, :, 128:256] = low
        lhs[8] = jnp.zeros((256, 256), jnp.bfloat16)
        for k in range(32):
            acc[k] = jnp.zeros((256, 128), jnp.float32)

    @pl.when(step * CHUNK < live)
    def _():
        for u in range(CHUNK):
            slot = step * CHUNK + u
            row = jnp.where(slot < live, rows[slot], 8)
            col = cols[slot]
            tile = tiles[u]
            product = jnp.dot(
                lhs[row],
                jnp.concatenate([tile, tile], axis=0),
                preferred_element_type=jnp.float32,
            )
            acc[col] += product

    @pl.when(step == pl.num_programs(0) - 1)
    def _():
        def move(k, carry):
            mine[k] = acc[2 * k + core]
            theirs[k] = acc[2 * k + 1 - core].astype(jnp.bfloat16)
            return carry

        lax.fori_loop(0, 16, move, 0)


def sparse_product(rows, cols, meta, grads, tiles):
    steps = tiles.shape[0] // CHUNK

    def tile_block(i, rows, cols, meta):
        return (jnp.minimum(i, (meta[0] - 1) // CHUNK), 0, 0)

    whole = lambda i, rows, cols, meta: (0, 0, 0)
    return pl.pallas_call(
        sparse_kernel,
        grid_spec=pltpu.PrefetchScalarGridSpec(
            num_scalar_prefetch=3,
            grid=(steps,),
            in_specs=[
                pl.BlockSpec(grads.shape, whole),
                pl.BlockSpec((CHUNK, 128, 128), tile_block),
            ],
            out_specs=[
                pl.BlockSpec((16, 256, 128), whole),
                pl.BlockSpec((16, 256, 128), whole),
            ],
            scratch_shapes=[
                pltpu.VMEM((32, 256, 128), jnp.float32),
                pltpu.VMEM((9, 256, 256), jnp.bfloat16),
            ],
        ),
        out_shape=[
            jax.ShapeDtypeStruct((16, 256, 128), jnp.float32),
            jax.ShapeDtypeStruct((16, 256, 128), jnp.bfloat16),
        ],
        compiler_params=pltpu.CompilerParams(vmem_limit_bytes=40 * 1024 * 1024),
        name="sparse",
    )(rows, cols, meta, grads, tiles)


def dense_kernel(parts, feats, grads, w_self, w_neigh, grad_x, grad_neigh):
    total = parts[0].astype(jnp.float32)
    for k in range(1, 16):
        total += parts[k].astype(jnp.float32)
    high = total.astype(jnp.bfloat16)
    low = (total - high.astype(jnp.float32)).astype(jnp.bfloat16)
    feat = feats[...]
    neigh_t = jnp.dot(
        jnp.concatenate([high, low], axis=1),
        jnp.concatenate([feat, feat], axis=0),
        preferred_element_type=jnp.float32,
    )
    grad_neigh[...] = neigh_t.T
    nt = (((1,), (1,)), ((), ()))
    out = lax.dot_general(w_self[...], grads[...], nt, preferred_element_type=jnp.float32)
    out += jnp.dot(w_neigh[...], high, preferred_element_type=jnp.float32)
    out += jnp.dot(w_neigh[...], low, preferred_element_type=jnp.float32)
    grad_x[...] = out.T.astype(jnp.bfloat16)


def dense_part(parts, feats, grads, w_self, w_neigh):
    return pl.pallas_call(
        dense_kernel,
        out_shape=[
            jax.ShapeDtypeStruct((128, 256), jnp.bfloat16),
            jax.ShapeDtypeStruct((256, 256), jnp.float32),
        ],
        compiler_params=pltpu.CompilerParams(vmem_limit_bytes=32 * 1024 * 1024),
        name="dense",
    )(parts, feats, grads, w_self, w_neigh)


def shards(features, grad_out, w_self, w_neigh, tiles, tile_rows, tile_cols, tile_counts, degrees):
    core = lax.axis_index("row") & 1
    node_total = 128 * 256
    degree_rows = jnp.pad(degrees.astype(jnp.bfloat16)[None], ((0, DEG_ROWS - 1), (0, 128)))
    packed = jnp.concatenate([grad_out, degree_rows], axis=0)
    group = spread(packed, ("xh", "y"), 8)
    meta = jnp.stack([tile_counts[0], core.astype(jnp.int32)])
    mine, theirs = sparse_product(tile_rows[0], tile_cols[0], meta, group, tiles[0])
    halves = (mine + swap_core(theirs).astype(jnp.float32)).astype(jnp.bfloat16)
    parts = exchange(halves, ("z", "xl"))
    grad_x, neigh = dense_part(parts, features, grad_out, w_self, w_neigh)
    own = jnp.einsum("nf,ng->fg", features, grad_out, preferred_element_type=jnp.float32)
    first = core == 0
    kept = jnp.where(first, own, neigh) + swap_core(jnp.where(first, neigh, own))
    pieces = exchange(kept.reshape(16, 16, 256), ("xh", "xl", "y")).sum(axis=0)
    pieces = spread(pieces, ("z",), 8).sum(axis=0) / node_total
    full = spread(pieces, ("xh", "xl", "y"), 16).reshape(256, 256)
    other = swap_core(full)
    return grad_x, jnp.where(first, full, other), jnp.where(first, other, full)


def solution(mesh):
    in_specs = (
        P(("row", "blk"), None),
        P(("row", "blk"), None),
        P(),
        P(),
        P(("row", "blk"), None, None, None),
        P(("row", "blk"), None),
        P(("row", "blk"), None),
        P(("row", "blk")),
        P(("row", "blk")),
    )
    out_specs = (P(("row", "blk"), None), P(), P())
    return jax.shard_map(shards, mesh=mesh, in_specs=in_specs, out_specs=out_specs, check_vma=False)
```

time: 723 us -> 119 us (0.16)
  waiting for transfers between devices: 490 us -> 39 us
  other arithmetic: 102 us -> 3.76 us
  matrix products: 50.3 us -> 0.21 us
  starting transfers between devices: 0.16 us -> 31.3 us
  local copies, waits for them, and re-layouts: 26.7 us -> 5.05 us
  between operations: 13.8 us -> 1.37 us
    psum x1 -> x0, waiting for transfers between devices: 257 us -> none  [shards(): grad_self, grad_neigh = lax.psum((grad_self, grad_neigh), ('row', 'blk'))]
    reduce_scatter x2 -> x0, waiting for transfers between devices: 193 us -> none  [the longest x1 120 us: shards(): lax.psum_scatter(column_partial, 'row', scatter_dimension=0, tiled=True)]
    scatter-add x6 -> x0, other arithmetic: 95.2 us -> none  [the longest x3 58 us: compute(): column_acc.at[col_slot].add(backward_part * alive_mask[:, None, None])]
    dot_general x9 -> x0, matrix products: 49.4 us -> none  [the longest x3 22.7 us: compute(): jnp.einsum('tij,tif->tjf', tile_block, scaled_tiles[row_slot], preferred_...]
    all_gather x1 -> x0, waiting for transfers between devices: 38.7 us -> none  [shards(): class_feats = lax.all_gather(features, 'row', axis=0, tiled=True)]
    all_to_all x0 -> x2, waiting for transfers between devices: none -> 34.4 us  [exchange(): lax.all_to_all(blocks, ('row', 'blk'), 0, 0, axis_index_groups=groups_of(...]
    all_to_all x0 -> x3, blocking collectives: none -> 32.9 us  [exchange(): lax.all_to_all(blocks, ('row', 'blk'), 0, 0, axis_index_groups=groups_of(...]
    all_gather x1 -> x0, blocking collectives: 30.5 us -> none  [shards(): scaled_group = lax.all_gather(scaled, 'blk', axis=0, tiled=True)]
  transfers between devices with their start and end apart: 4 -> 5, of which waited for: 4 -> 5; matrix products, arithmetic and copies ran while one was open for 1% -> 0% of each run, Pallas kernels for 0% -> 0%
where the time goes in v1:
time: 119 us
  waiting for transfers between devices  39 us (33%)
  blocking collectives  32.9 us (28%)
  starting transfers between devices  31.3 us (26%)
  Pallas kernels  5.08 us (4%)
  local copies, waits for them, and re-layouts  5.05 us (4%)
  other arithmetic  3.76 us (3%)
  between operations  1.37 us (1%)
    all_to_all x2, waiting for transfers between devices, exchange(): lax.all_to_all(blocks, ('row', 'blk'), 0, 0, axis_index_groups=groups_of(...  34.4 us
    all_to_all x3, blocking collectives, exchange(): lax.all_to_all(blocks, ('row', 'blk'), 0, 0, axis_index_groups=groups_of(...  32.9 us
    all_to_all x2, starting transfers between devices, exchange(): lax.all_to_all(blocks, ('row', 'blk'), 0, 0, axis_index_groups=groups_of(...  19.3 us
    ppermute x3, starting transfers between devices, swap_core(): return lax.ppermute(value, 'row', [(row, row ^ 1) for row in range(32)])  12 us
    ppermute x3, waiting for transfers between devices, swap_core(): return lax.ppermute(value, 'row', [(row, row ^ 1) for row in range(32)])  4.61 us
    unnamed x14, local copies, waits for them, and re-layouts  4.16 us
    pallas_call x1, Pallas kernels, sparse_product(): pl.pallas_call(sparse_kernel, grid_spec=pltpu.PrefetchScalarGridSpec(num_...  3.96 us
  transfers between devices with their start and end apart: 5, of which 5 were waited for; matrix products, arithmetic and copies ran while one was open for 0% of the time, Pallas kernels for 0%

profile of v1, /device:TPU:1, one launch (start us, length us, event | category | flops | bytes accessed | tf_op | source)
XLA Modules:
  0.0 118.7 jit_solution(15313592293717624634)
XLA Ops:
  0.6 0.7 convert_bitcast_fusion
  1.3 0.8 fusion.1
  2.1 0.9 broadcast_in_dim.9
  3.0 7.5 %all-to-all-start = ((bf16[8,144,256]{2,1,0:T(8,128)(2,1)}), bf16[8,144,256]{2,1,0:T(8,128)(2,1)S(1)}, u32[]{:S(2)}, u32[]{:S(2)}) async-start(bf16[8,144,256]{2,1,0:T(8,128)(2,1)} %broadcast_in_dim.9), calls=%async_computation | async-start | bytes 1179648 | tf_op jit(solution)/shard_map/all_to_all | solution.py:34
  11.1 0.1 pad_add_fusion.meta
  11.2 8.8 %all-to-all-done.grads = bf16[8,144,256]{2,1,0:T(8,128)(2,1)S(1)} async-done(((bf16[8,144,256]{2,1,0:T(8,128)(2,1)}), bf16[8,144,256]{2,1,0:T(8,128)(2,1)S(1)}, u32[]{:S(2)}, u32[]{:S(2)}) %all-to-all-start) | async-done | bytes 589856 | tf_op jit(solution)/shard_map/all_to_all | solution.py:34
  20.0 0.0 copy-start
  20.0 2.8 %copy-done = bf16[1,192,128,128]{3,2,1,0:T(8,128)(2,1)S(1)} copy-done((bf16[1,192,128,128]{3,2,1,0:T(8,128)(2,1)S(1)}, bf16[1,192,128,128]{3,2,1,0:T(8,128)(2,1)}, u32[]{:S(2)}) %copy-start) | copy-done | bytes 6291480
  22.8 0.0 copy-start.5
  22.8 0.7 copy-done.5
  23.4 0.7 copy-done.6
  24.1 4.0 %sparse.1 = (f32[16,256,128]{2,1,0:T(8,128)S(1)}, bf16[16,256,128]{2,1,0:T(8,128)(2,1)S(1)}) custom-call(s32[192]{0:T(256)S(1)} %bitcast.13, s32[192]{0:T(256)S(1)} %bitcast.14, s32[2]{0:T(128)S(1)} %pad_add_fusion.meta, bf16[8,144,256]{2,1,0:T(8,128)(2,1)S(1)} %all-to-all-done.grads, bf16[192,128,128]{2,1,0:T(8,128)(2,1)S(1)} %bitcast.12), custom_call_target="tpu_custom_call" | custom-call | tf_op jit(solution)/shard_map/sparse/pallas_call | solution.py:97
  28.1 3.8 %collective-permute-start = (bf16[16,256,128]{2,1,0:T(8,128)(2,1)S(1)}, bf16[16,256,128]{2,1,0:T(8,128)(2,1)S(1)}, u32[]{:S(2)}, u32[]{:S(2)}) collective-permute-start(bf16[16,256,128]{2,1,0:T(8,128)(2,1)S(1)} %get-tuple-element.8), channel_id=1, source_target_pairs={{0,8},{8,0},{16,24},{24,16},{32,40},{40,32},{48,56},{56,48},{64,72... | collective-permute-start | bytes 3145736 | tf_op jit(solution)/shard_map/ppermute | solution.py:44
  31.9 2.3 %collective-permute-done = bf16[16,256,128]{2,1,0:T(8,128)(2,1)S(1)} collective-permute-done((bf16[16,256,128]{2,1,0:T(8,128)(2,1)S(1)}, bf16[16,256,128]{2,1,0:T(8,128)(2,1)S(1)}, u32[]{:S(2)}, u32[]{:S(2)}) %collective-permute-start) | collective-permute-done | bytes 1048608 | tf_op jit(solution)/shard_map/ppermute | solution.py:44
  34.2 1.3 %add_convert_fusion = bf16[16,256,128]{2,1,0:T(8,128)(2,1)} fusion(f32[16,256,128]{2,1,0:T(8,128)S(1)} %get-tuple-element.7, bf16[16,256,128]{2,1,0:T(8,128)(2,1)S(1)} %collective-permute-done), kind=kLoop, calls=%fused_computation | loop fusion | flops 1572864 | bytes 4194304 | tf_op jit(solution)/shard_map/convert_element_type | solution.py:164
  35.4 11.8 %all-to-all-start.1 = ((bf16[16,256,128]{2,1,0:T(8,128)(2,1)}), bf16[16,256,128]{2,1,0:T(8,128)(2,1)S(1)}, u32[]{:S(2)}, u32[]{:S(2)}) async-start(bf16[16,256,128]{2,1,0:T(8,128)(2,1)} %add_convert_fusion), calls=%async_computation.1 | async-start | bytes 2097152 | tf_op jit(solution)/shard_map/all_to_all | solution.py:34
  47.3 25.7 %all-to-all-done.1.parts = bf16[16,256,128]{2,1,0:T(8,128)(2,1)S(1)} async-done(((bf16[16,256,128]{2,1,0:T(8,128)(2,1)}), bf16[16,256,128]{2,1,0:T(8,128)(2,1)S(1)}, u32[]{:S(2)}, u32[]{:S(2)}) %all-to-all-start.1) | async-done | bytes 1048608 | tf_op jit(solution)/shard_map/all_to_all | solution.py:34
  72.9 0.0 copy-done.1
  72.9 0.0 copy-done.2
  73.0 0.0 copy-done.3
  73.0 0.0 copy-done.4
  73.0 1.1 dense.1
  74.1 0.2 broadcast_select_fusion.2
  74.3 4.1 %collective-permute-start.1 = (f32[256,256]{1,0:T(8,128)S(1)}, f32[256,256]{1,0:T(8,128)S(1)}, u32[]{:S(2)}, u32[]{:S(2)}) collective-permute-start(f32[256,256]{1,0:T(8,128)S(1)} %get-tuple-element.13), channel_id=1, source_target_pairs={{0,8},{8,0},{16,24},{24,16},{32,40},{40,32},{48,56},{56,48},{64,72... | collective-permute-start | bytes 786440 | tf_op jit(solution)/shard_map/ppermute | solution.py:44
  78.4 1.2 collective-permute-done.1
  79.6 0.1 select_add_fusion
  79.6 11.7 %all_to_all.25 = f32[16,16,256]{2,1,0:T(8,128)S(1)} all-to-all(f32[16,16,256]{2,1,0:T(8,128)S(1)} %bitcast.16), channel_id=1, replica_groups={{0,1,2,3,16,17,18,19,4,5,6,7,20,21,22,23},{8,9,10,11,24,25,26,27,12,13,..., dimensions={0} | all-to-all | bytes 524288 | tf_op jit(solution)/shard_map/all_to_all | solution.py:34
  91.4 10.4 %all_to_all.26 = f32[8,16,256]{2,1,0:T(8,128)S(1)} all-to-all(f32[8,16,256]{2,1,0:T(8,128)S(1)} %broadcast_in_dim.10), channel_id=1, replica_groups={{0,32,64,96,128,160,192,224},{1,33,65,97,129,161,193,225},{2,34,66,98,1..., dimensions={0} | all-to-all | bytes 262144 | tf_op jit(solution)/shard_map/all_to_all | solution.py:34
  101.8 10.8 %all_to_all.27 = f32[16,16,256]{2,1,0:T(8,128)S(1)} all-to-all(f32[16,16,256]{2,1,0:T(8,128)S(1)} %broadcast_in_dim.11), channel_id=1, replica_groups={{0,1,2,3,16,17,18,19,4,5,6,7,20,21,22,23},{8,9,10,11,24,25,26,27,12,13,..., dimensions={0} | all-to-all | bytes 524288 | tf_op jit(solution)/shard_map/all_to_all | solution.py:34
  112.6 4.1 %collective-permute-start.2 = (f32[256,256]{1,0:T(8,128)S(1)}, f32[256,256]{1,0:T(8,128)S(1)}, u32[]{:S(2)}, u32[]{:S(2)}) collective-permute-start(f32[256,256]{1,0:T(8,128)S(1)} %bitcast.15), channel_id=1, source_target_pairs={{0,8},{8,0},{16,24},{24,16},{32,40},{40,32},{48,56},{56,48},{64,72... | collective-permute-start | bytes 786440 | tf_op jit(solution)/shard_map/ppermute | solution.py:44
  116.7 1.2 collective-permute-done.2
  117.9 0.8 broadcast_select_fusion
  (10 shorter events, 0.1 us)
Async XLA Ops:
  3.0 17.0 %all-to-all-start = ((bf16[8,144,256]{2,1,0:T(8,128)(2,1)}), bf16[8,144,256]{2,1,0:T(8,128)(2,1)S(1)}, u32[]{:S(2)}, u32[]{:S(2)}) async-start(bf16[8,144,256]{2,1,0:T(8,128)(2,1)} %broadcast_in_dim.9), calls=%async_computation | async-start | bytes 1179648 | tf_op jit(solution)/shard_map/all_to_all | solution.py:34
  20.0 2.8 %copy-start = (bf16[1,192,128,128]{3,2,1,0:T(8,128)(2,1)S(1)}, bf16[1,192,128,128]{3,2,1,0:T(8,128)(2,1)}, u32[]{:S(2)}) copy-start(bf16[1,192,128,128]{3,2,1,0:T(8,128)(2,1)} %param.13) | copy-start | bytes 18874372
  22.8 0.7 copy-start.5
  23.4 0.7 copy-start.6
  28.1 6.1 %collective-permute-start = (bf16[16,256,128]{2,1,0:T(8,128)(2,1)S(1)}, bf16[16,256,128]{2,1,0:T(8,128)(2,1)S(1)}, u32[]{:S(2)}, u32[]{:S(2)}) collective-permute-start(bf16[16,256,128]{2,1,0:T(8,128)(2,1)S(1)} %get-tuple-element.8), channel_id=1, source_target_pairs={{0,8},{8,0},{16,24},{24,16},{32,40},{40,32},{48,56},{56,48},{64,72... | collective-permute-start | bytes 3145736 | tf_op jit(solution)/shard_map/ppermute | solution.py:44
  35.4 37.5 %copy-start.1 = (bf16[128,256]{1,0:T(8,128)(2,1)S(1)}, bf16[128,256]{1,0:T(8,128)(2,1)}, u32[]{:S(2)}) copy-start(bf16[128,256]{1,0:T(8,128)(2,1)} %grads.1) | copy-start | bytes 196612
  35.4 37.5 %copy-start.2 = (bf16[128,256]{1,0:T(8,128)(2,1)S(1)}, bf16[128,256]{1,0:T(8,128)(2,1)}, u32[]{:S(2)}) copy-start(bf16[128,256]{1,0:T(8,128)(2,1)} %feats.1) | copy-start | bytes 196612
  35.4 37.5 %copy-start.3 = (bf16[256,256]{1,0:T(8,128)(2,1)S(1)}, bf16[256,256]{1,0:T(8,128)(2,1)}, u32[]{:S(2)}) copy-start(bf16[256,256]{1,0:T(8,128)(2,1)} %w_self.1) | copy-start | bytes 393220
  35.4 37.5 %copy-start.4 = (bf16[256,256]{1,0:T(8,128)(2,1)S(1)}, bf16[256,256]{1,0:T(8,128)(2,1)}, u32[]{:S(2)}) copy-start(bf16[256,256]{1,0:T(8,128)(2,1)} %w_neigh.1) | copy-start | bytes 393220
  35.4 37.5 %all-to-all-start.1 = ((bf16[16,256,128]{2,1,0:T(8,128)(2,1)}), bf16[16,256,128]{2,1,0:T(8,128)(2,1)S(1)}, u32[]{:S(2)}, u32[]{:S(2)}) async-start(bf16[16,256,128]{2,1,0:T(8,128)(2,1)} %add_convert_fusion), calls=%async_computation.1 | async-start | bytes 2097152 | tf_op jit(solution)/shard_map/all_to_all | solution.py:34
  74.3 5.3 %collective-permute-start.1 = (f32[256,256]{1,0:T(8,128)S(1)}, f32[256,256]{1,0:T(8,128)S(1)}, u32[]{:S(2)}, u32[]{:S(2)}) collective-permute-start(f32[256,256]{1,0:T(8,128)S(1)} %get-tuple-element.13), channel_id=1, source_target_pairs={{0,8},{8,0},{16,24},{24,16},{32,40},{40,32},{48,56},{56,48},{64,72... | collective-permute-start | bytes 786440 | tf_op jit(solution)/shard_map/ppermute | solution.py:44
  112.6 5.3 %collective-permute-start.2 = (f32[256,256]{1,0:T(8,128)S(1)}, f32[256,256]{1,0:T(8,128)S(1)}, u32[]{:S(2)}, u32[]{:S(2)}) collective-permute-start(f32[256,256]{1,0:T(8,128)S(1)} %bitcast.15), channel_id=1, source_target_pairs={{0,8},{8,0},{16,24},{24,16},{32,40},{40,32},{48,56},{56,48},{64,72... | collective-permute-start | bytes 786440 | tf_op jit(solution)/shard_map/ppermute | solution.py:44

commit v2 on v1

v2 whole, which is shorter than its diff:
```python
import functools
import itertools

import jax
import jax.numpy as jnp
from jax import lax
from jax.experimental import pallas as pl
from jax.experimental.pallas import tpu as pltpu
from jax.sharding import PartitionSpec as P

PARTS = {"z": 8, "xl": 2, "core": 2, "xh": 2, "y": 4}
CHUNK = 16
DEG_ROWS = 16
UNROLL = 8
TRASH = 32
ZERO_ROW = 8
MIB = 1024 * 1024
SPARSE_MIB = 48
VMEM = pl.BlockSpec(memory_space=pltpu.VMEM)
SMEM = pl.BlockSpec(memory_space=pltpu.SMEM)
ANY = pl.BlockSpec(memory_space=pl.ANY)


def device_id(where):
    row = (where["z"] * 2 + where["xl"]) * 2 + where["core"]
    return row * 8 + where["xh"] * 4 + where["y"]


def groups_of(names):
    rest = [name for name in PARTS if name not in names]
    groups = []
    for fixed in itertools.product(*[range(PARTS[name]) for name in rest]):
        where = dict(zip(rest, fixed))
        group = []
        for moving in itertools.product(*[range(PARTS[name]) for name in names]):
            where.update(zip(names, moving))
            group.append(device_id(where))
        groups.append(group)
    return groups


def exchange(blocks, names):
    return lax.all_to_all(
        blocks, ("row", "blk"), 0, 0, axis_index_groups=groups_of(names), tiled=True
    )


def spread(block, names, count):
    return exchange(jnp.broadcast_to(block[None], (count,) + block.shape), names)


def swap_core(value):
    return lax.ppermute(value, "row", [(row, row ^ 1) for row in range(32)])


def params(mib):
    return pltpu.CompilerParams(vmem_limit_bytes=mib * MIB)


def head_kernel(grads, degrees, out, degree, sems):
    copies = [pltpu.make_async_copy(degrees, degree, sems.at[8])]
    for k in range(8):
        copies.append(pltpu.make_async_copy(grads, out.at[k, pl.ds(0, 128)], sems.at[k]))
    for copy in copies:
        copy.start()
    copies[0].wait()
    value = jnp.broadcast_to(degree[...], (DEG_ROWS, 128)).astype(jnp.float32)
    for k in range(8):
        out[k, 128 : 128 + DEG_ROWS, 0:128] = value.astype(jnp.bfloat16)
        out[k, 128 : 128 + DEG_ROWS, 128:256] = jnp.zeros((DEG_ROWS, 128), jnp.bfloat16)
    for copy in copies[1:]:
        copy.wait()


def head(grads, degrees):
    return pl.pallas_call(
        head_kernel,
        in_specs=[ANY, ANY],
        out_specs=VMEM,
        out_shape=jax.ShapeDtypeStruct((8, 128 + DEG_ROWS, 256), jnp.bfloat16),
        scratch_shapes=[pltpu.VMEM((1, 128), jnp.int32), pltpu.SemaphoreType.DMA((9,))],
        compiler_params=params(60),
        name="head",
    )(grads, degrees[None])


def prep_kernel(counts, row, rows, cols, feats, grads, plan, own_self):
    own_self[...] = lax.dot_general(
        feats[...], grads[...], (((0,), (0,)), ((), ())), preferred_element_type=jnp.float32
    )
    live = counts[0]
    slots = rows.shape[1]
    narrow = lambda value: value.astype(jnp.float32).astype(jnp.bfloat16)
    slot = lax.broadcasted_iota(jnp.int32, (1, slots), 1)
    lanes = lax.broadcasted_iota(jnp.int32, (8, slots), 0)
    hot = jnp.where((rows[...] == lanes) & (slot < live), 1.0, 0.0)
    earlier = lax.broadcasted_iota(jnp.int32, (slots, slots), 0) < lax.broadcasted_iota(
        jnp.int32, (slots, slots), 1
    )
    rank = jnp.dot(
        hot.astype(jnp.bfloat16),
        jnp.where(earlier, 1.0, 0.0).astype(jnp.bfloat16),
        preferred_element_type=jnp.float32,
    )
    rank = jnp.sum(hot * rank, axis=0, keepdims=True).astype(jnp.int32)
    pairs = (jnp.sum(hot, axis=1, keepdims=True).astype(jnp.int32) + 1) >> 1
    start = jnp.zeros((8, 1), jnp.int32)
    for r in range(7):
        start += jnp.where(lax.broadcasted_iota(jnp.int32, (8, 1), 0) > r, pairs[r : r + 1], 0)
    total = start[7:8] + pairs[7:8]
    start = jnp.sum(hot * start.astype(jnp.float32), axis=0, keepdims=True).astype(jnp.int32)
    pair = jnp.where(slot < live, start + (rank >> 1), -1)
    far = cols[...] ^ row[0]
    place = (far & 1) * 16 + (far & 4) * 2 + (far & 8) // 2 + (far & 2) + (far >> 4)
    values = jnp.where(lanes == 0, slot, 0) + jnp.where(lanes == 1, place, 0)
    values += jnp.where(lanes == 2, rows[...], 0) + jnp.where(lanes == 3, 1, 0)
    mine = lax.broadcasted_iota(jnp.int32, (128, slots), 0) == pair
    nt = (((1,), (1,)), ((), ()))

    def pick(half):
        chosen = jnp.where(mine & ((rank & 1) == half), 1.0, 0.0).astype(jnp.bfloat16)
        picked = lax.dot_general(narrow(values), chosen, nt, preferred_element_type=jnp.float32)
        return picked.astype(jnp.int32)

    first, second = pick(0), pick(1)
    plan[0:1, :] = first[0:1]
    plan[1:2, :] = second[0:1]
    plan[2:3, :] = first[1:2] + (1 - first[3:4]) * TRASH
    plan[3:4, :] = second[1:2] + (1 - second[3:4]) * TRASH
    plan[4:5, :] = first[2:3] + (1 - first[3:4]) * ZERO_ROW
    plan[5:6, :] = jnp.broadcast_to((total + UNROLL - 1) >> 3, (1, 128))
    plan[6:7, :] = jnp.full((1, 128), (live + CHUNK - 1) >> 4, jnp.int32)
    plan[7:8, :] = jnp.zeros((1, 128), jnp.int32)


def prep(counts, row, rows, cols, feats, grads):
    return pl.pallas_call(
        prep_kernel,
        in_specs=[SMEM, SMEM, VMEM, VMEM, VMEM, VMEM],
        out_specs=[VMEM, VMEM],
        out_shape=[
            jax.ShapeDtypeStruct((8, 128), jnp.int32),
            jax.ShapeDtypeStruct((256, 256), jnp.float32),
        ],
        compiler_params=params(10),
        cost_estimate=pl.CostEstimate(flops=0, bytes_accessed=4 * MIB, transcendentals=0),
        name="prep",
    )(counts, row[None], rows, cols, feats, grads)


def join_kernel(first, second, out):
    out[0 : first.shape[0]] = first[...]
    out[first.shape[0] :] = second[...]


def join(first, second):
    return pl.pallas_call(
        join_kernel,
        in_specs=[VMEM, VMEM],
        out_specs=VMEM,
        out_shape=jax.ShapeDtypeStruct((2 * first.shape[0],) + first.shape[1:], first.dtype),
        compiler_params=params(4),
        name="join",
    )(first, second)


def sparse_kernel(plan, grads, tiles, near, away, near_out, away_out, lhs, acc, held, sems):
    chunks = plan[6, 0]

    def piece(k):
        part = pl.ds(k * CHUNK, CHUNK)
        return pltpu.make_async_copy(tiles.at[part], held.at[part], sems.at[k])

    def wait_piece(k, carry):
        piece(k).wait()
        return carry

    for k in range(192 // CHUNK):
        pl.when(k < chunks)(lambda k=k: piece(k).start())
    for k in range(8):
        grad_t = grads[k, 0:128, :].T.astype(jnp.float32)
        degree = grads[k, 128:129, 0:128].astype(jnp.float32)
        value = grad_t / degree
        high = value.astype(jnp.bfloat16)
        low = (value - high.astype(jnp.float32)).astype(jnp.bfloat16)
        lhs[k, :, 0:128] = high
        lhs[k, :, 128:256] = low
    lhs[ZERO_ROW] = jnp.zeros((256, 256), jnp.bfloat16)

    def clear(k, carry):
        acc[k] = jnp.zeros((256, 128), jnp.float32)
        return carry

    lax.fori_loop(0, 33, clear, 0)

    lax.fori_loop(0, chunks, wait_piece, 0)

    def pairs(step, carry):
        for u in range(UNROLL):
            p = step * UNROLL + u
            both = jnp.concatenate([held[plan[0, p]], held[plan[1, p]]], axis=1)
            product = jnp.dot(
                lhs[plan[4, p]],
                jnp.concatenate([both, both], axis=0),
                preferred_element_type=jnp.float32,
            )
            acc[plan[2, p]] += product[:, 0:128]
            acc[plan[3, p]] += product[:, 128:256]
        return carry

    lax.fori_loop(0, plan[5, 0], pairs, 0)

    def move(k, carry):
        near[k] = acc[k]
        away[k] = acc[8 + k]
        near_out[k] = acc[16 + k].astype(jnp.bfloat16)
        away_out[k] = acc[24 + k].astype(jnp.bfloat16)
        return carry

    lax.fori_loop(0, 8, move, 0)


def sparse_product(plan, grads, tiles):
    return pl.pallas_call(
        sparse_kernel,
        in_specs=[SMEM, VMEM, pl.BlockSpec(memory_space=pl.ANY)],
        out_specs=[VMEM] * 4,
        out_shape=[
            jax.ShapeDtypeStruct((8, 256, 128), kind)
            for kind in (jnp.float32, jnp.float32, jnp.bfloat16, jnp.bfloat16)
        ],
        scratch_shapes=[
            pltpu.VMEM((9, 256, 256), jnp.bfloat16),
            pltpu.VMEM((33, 256, 128), jnp.float32),
            pltpu.VMEM((192, 128, 128), jnp.bfloat16),
            pltpu.SemaphoreType.DMA((192 // CHUNK,)),
        ],
        compiler_params=params(SPARSE_MIB),
        cost_estimate=pl.CostEstimate(flops=4 * 10**9, bytes_accessed=12 * MIB, transcendentals=0),
        name="sparse",
    )(plan, grads, tiles)


def neigh_kernel(core, near, core_part, x_part, feats_low, feats_high, own_self, keep, send, kept, sent):
    total_t = jnp.zeros((256, 256), jnp.float32)
    for k in range(8):
        block = near[k] + core_part[k].astype(jnp.float32) + x_part[k].astype(jnp.float32)
        high = block.astype(jnp.bfloat16)
        low = (block - high.astype(jnp.float32)).astype(jnp.bfloat16)
        if k < 4:
            keep[k] = block
        else:
            send[k - 4] = high
        feat = (feats_high if k & 2 else feats_low)[(k & 1) * 2 + (k >> 2)]
        total_t += jnp.dot(
            jnp.concatenate([high, low], axis=1),
            jnp.concatenate([feat, feat], axis=0),
            preferred_element_type=jnp.float32,
        )
    total = total_t.T
    first = core[0] == 0

    @pl.when(first)
    def _():
        kept[...] = own_self[...]
        sent[...] = total

    @pl.when(jnp.logical_not(first))
    def _():
        kept[...] = total
        sent[...] = own_self[...]


def neigh_part(core, near, core_part, x_part, feats_low, feats_high, own_self):
    return pl.pallas_call(
        neigh_kernel,
        in_specs=[SMEM] + [VMEM] * 6,
        out_specs=[VMEM] * 4,
        out_shape=[
            jax.ShapeDtypeStruct((4, 256, 128), jnp.float32),
            jax.ShapeDtypeStruct((4, 256, 128), jnp.bfloat16),
            jax.ShapeDtypeStruct((256, 256), jnp.float32),
            jax.ShapeDtypeStruct((256, 256), jnp.float32),
        ],
        compiler_params=params(16),
        cost_estimate=pl.CostEstimate(flops=10**9, bytes_accessed=4 * MIB, transcendentals=0),
        name="neigh",
    )(core[None], near, core_part, x_part, feats_low, feats_high, own_self)


def fold_kernel(scale, pieces, keep, got, out, *rest):
    total = pieces[0]
    for k in range(1, pieces.shape[0]):
        total += pieces[k]
    total = total * scale
    for k in range(out.shape[0]):
        out[k] = total
    half = keep.shape[0] // 2
    kept, send = rest
    for k in range(half):
        kept[k] = keep[k] + got[k].astype(jnp.float32)
        send[k] = (keep[half + k] + got[half + k].astype(jnp.float32)).astype(jnp.bfloat16)


def fold(scale, pieces, receivers, keep, got):
    half = keep.shape[0] // 2
    return pl.pallas_call(
        functools.partial(fold_kernel, scale),
        in_specs=[VMEM] * 3,
        out_specs=[VMEM] * 3,
        out_shape=[
            jax.ShapeDtypeStruct((receivers, 16, 256), jnp.float32),
            jax.ShapeDtypeStruct((half, 256, 128), jnp.float32),
            jax.ShapeDtypeStruct((half, 256, 128), jnp.bfloat16),
        ],
        compiler_params=params(8),
        name="fold",
    )(pieces, keep, got)


def last_kernel(core, own, part, grads, w_self, w_neigh, full, other, grad_x, grad_self, grad_neigh):
    first = core[0] == 0

    @pl.when(first)
    def _():
        grad_self[...] = full[...]
        grad_neigh[...] = other[...]

    @pl.when(jnp.logical_not(first))
    def _():
        grad_self[...] = other[...]
        grad_neigh[...] = full[...]

    total = own[0] + part[0].astype(jnp.float32)
    high = total.astype(jnp.bfloat16)
    low = (total - high.astype(jnp.float32)).astype(jnp.bfloat16)
    nt = (((1,), (1,)), ((), ()))
    out = lax.dot_general(w_self[...], grads[...], nt, preferred_element_type=jnp.float32)
    out += jnp.dot(w_neigh[...], high, preferred_element_type=jnp.float32)
    out += jnp.dot(w_neigh[...], low, preferred_element_type=jnp.float32)
    grad_x[...] = out.T.astype(jnp.bfloat16)


def last(core, own, part, grads, w_self, w_neigh, full, other):
    return pl.pallas_call(
        last_kernel,
        in_specs=[SMEM] + [VMEM] * 7,
        out_specs=[VMEM] * 3,
        out_shape=[
            jax.ShapeDtypeStruct((128, 256), jnp.bfloat16),
            jax.ShapeDtypeStruct((256, 256), jnp.float32),
            jax.ShapeDtypeStruct((256, 256), jnp.float32),
        ],
        compiler_params=params(8),
        name="last",
    )(core[None], own, part, grads, w_self, w_neigh, full, other)


def swap_z(value, distance):
    return lax.ppermute(value, "row", [(row, row ^ (4 * distance)) for row in range(32)])


def swap_x(value):
    return lax.ppermute(value, "row", [(row, row ^ 2) for row in range(32)])


def shards(features, grad_out, w_self, w_neigh, tiles, tile_rows, tile_cols, tile_counts, degrees):
    row = lax.axis_index("row").astype(jnp.int32)
    core = row & 1
    node_total = 128 * 256
    group = exchange(head(grad_out, degrees), ("xh", "y"))
    plan, own_self = prep(tile_counts, row, tile_rows, tile_cols, features, grad_out)
    feats = features[None]
    feats = join(feats, swap_z(feats, 2))
    feats_far = swap_z(feats, 4)
    group, feats, plan = lax.optimization_barrier((group, feats, plan))
    near, away, near_out, away_out = sparse_product(plan, group, tiles[0])
    away_out, feats_far = lax.optimization_barrier((away_out, feats_far))
    feats = join(feats, feats_far)
    away = (away + swap_core(away_out).astype(jnp.float32)).astype(jnp.bfloat16)
    core_part = swap_core(near_out)
    z_part = swap_z(away, 1)
    feats_x = swap_x(feats)
    keep, send, kept, sent = neigh_part(core, near, core_part, z_part, feats, feats_x, own_self)
    kept = kept + swap_core(sent)
    got = swap_z(send, 2)
    pieces = exchange(kept.reshape(16, 16, 256), ("xh", "xl", "y"))
    pieces, keep, send = fold(1.0, pieces, 8, keep, got)
    got = swap_x(send)
    pieces = exchange(pieces, ("z",))
    pieces, keep, send = fold(1.0 / node_total, pieces, 16, keep, got)
    got = swap_z(send, 4)
    full = exchange(pieces, ("xh", "xl", "y")).reshape(256, 256)
    full, got = lax.optimization_barrier((full, got))
    other = swap_core(full)
    return last(core, keep, got, grad_out, w_self, w_neigh, full, other)


def solution(mesh):
    in_specs = (
        P(("row", "blk"), None),
        P(("row", "blk"), None),
        P(),
        P(),
        P(("row", "blk"), None, None, None),
        P(("row", "blk"), None),
        P(("row", "blk"), None),
        P(("row", "blk")),
        P(("row", "blk")),
    )
    out_specs = (P(("row", "blk"), None), P(), P())
    return jax.shard_map(shards, mesh=mesh, in_specs=in_specs, out_specs=out_specs, check_vma=False)
```

time: 119 us -> 99.6 us (0.84)
  blocking collectives: 32.9 us -> 0 us
  starting transfers between devices: 31.3 us -> 45.9 us
  Pallas kernels: 5.08 us -> 9.98 us
  other arithmetic: 3.76 us -> 0.84 us
  waiting for transfers between devices: 39 us -> 36.8 us
    all_to_all x3 -> x0, blocking collectives: 32.9 us -> none  [exchange(): lax.all_to_all(blocks, ('row', 'blk'), 0, 0, axis_index_groups=groups_of(...]
    all_to_all x2 -> x4, waiting for transfers between devices: 34.4 us -> 6.64 us  [exchange(): lax.all_to_all(blocks, ('row', 'blk'), 0, 0, axis_index_groups=groups_of(...]
    ppermute x0 -> x7, waiting for transfers between devices: none -> 27.6 us  [the longest x5 16.3 us: swap_z(): lax.ppermute(value, 'row', [(row, row ^ 4 * distance) for row in range(32)])]
    ppermute x0 -> x7, starting transfers between devices: none -> 11.5 us  [the longest x5 11.4 us: swap_z(): lax.ppermute(value, 'row', [(row, row ^ 4 * distance) for row in range(32)])]
    pallas_call x2 -> x9, Pallas kernels: 5.08 us -> 9.98 us  [the longest x1 4.51 us: sparse_product(): pl.pallas_call(sparse_kernel, in_specs=[SMEM, VMEM, pl.BlockSpec(memory_s...]
    all_to_all x2 -> x4, starting transfers between devices: 19.3 us -> 23 us  [exchange(): lax.all_to_all(blocks, ('row', 'blk'), 0, 0, axis_index_groups=groups_of(...]
    ppermute x3 -> x4, waiting for transfers between devices: 4.61 us -> 2.6 us  [swap_core(): return lax.ppermute(value, 'row', [(row, row ^ 1) for row in range(32)])]
    ppermute x3 -> x4, starting transfers between devices: 12 us -> 11.4 us  [swap_core(): return lax.ppermute(value, 'row', [(row, row ^ 1) for row in range(32)])]
  transfers between devices with their start and end apart: 5 -> 15, of which waited for: 5 -> 10; matrix products, arithmetic and copies ran while one was open for 0% -> 1% of each run, Pallas kernels for 0% -> 5%
where the time goes in v2:
time: 99.6 us; the launch traced here: 99.3 us
  starting transfers between devices  45.9 us (46%)
  waiting for transfers between devices  36.8 us (37%)
  Pallas kernels  9.98 us (10%)
  local copies, waits for them, and re-layouts  4.28 us (4%)
  between operations  1.44 us (1%)
    all_to_all x4, starting transfers between devices, exchange(): lax.all_to_all(blocks, ('row', 'blk'), 0, 0, axis_index_groups=groups_of(...  23 us
    ppermute x5, waiting for transfers between devices, swap_z(): lax.ppermute(value, 'row', [(row, row ^ 4 * distance) for row in range(32)])  16.3 us
    ppermute x5, starting transfers between devices, swap_z(): lax.ppermute(value, 'row', [(row, row ^ 4 * distance) for row in range(32)])  11.4 us
    ppermute x4, starting transfers between devices, swap_core(): return lax.ppermute(value, 'row', [(row, row ^ 1) for row in range(32)])  11.4 us
    ppermute x2, waiting for transfers between devices, swap_x(): return lax.ppermute(value, 'row', [(row, row ^ 2) for row in range(32)])  11.3 us
    all_to_all x4, waiting for transfers between devices, exchange(): lax.all_to_all(blocks, ('row', 'blk'), 0, 0, axis_index_groups=groups_of(...  6.64 us
    pallas_call x1, Pallas kernels, sparse_product(): pl.pallas_call(sparse_kernel, in_specs=[SMEM, VMEM, pl.BlockSpec(memory_s...  4.51 us
    unnamed x18, local copies, waits for them, and re-layouts  4.28 us
  transfers between devices with their start and end apart: 15, of which 10 were waited for; matrix products, arithmetic and copies ran while one was open for 1% of the time, Pallas kernels for 5%

profile of v2, /device:TPU:1, one launch (start us, length us, event | category | flops | bytes accessed | tf_op | source)
XLA Modules:
  0.0 99.3 jit_solution(10759701200920280906)
XLA Ops:
  0.6 2.1 %head.1 = bf16[8,144,256]{2,1,0:T(8,128)(2,1)} custom-call(bf16[128,256]{1,0:T(8,128)(2,1)} %grads.5, s32[1,128]{1,0:T(1,128)} %bitcast.11), custom_call_target="tpu_custom_call" | custom-call | tf_op jit(solution)/shard_map/head/pallas_call | solution.py:76
  2.8 7.5 %all-to-all-start = ((bf16[8,144,256]{2,1,0:T(8,128)(2,1)}), bf16[8,144,256]{2,1,0:T(8,128)(2,1)S(1)}, u32[]{:S(2)}, u32[]{:S(2)}) async-start(bf16[8,144,256]{2,1,0:T(8,128)(2,1)} %head.1), calls=%async_computation | async-start | bytes 1179648 | tf_op jit(solution)/shard_map/all_to_all | solution.py:43
  10.3 3.0 %collective-permute-start = (bf16[1,128,256]{2,1,0:T(8,128)(2,1)}, bf16[1,128,256]{2,1,0:T(8,128)(2,1)S(1)}, u32[]{:S(2)}, u32[]{:S(2)}) collective-permute-start(bf16[1,128,256]{2,1,0:T(8,128)(2,1)} %bitcast.9), channel_id=1, source_target_pairs={{0,64},{8,72},{16,80},{24,88},{32,96},{40,104},{48,112},{56,120},{... | collective-permute-start | bytes 196616 | tf_op jit(solution)/shard_map/ppermute | solution.py:360
  13.9 0.8 copy-done
  14.7 0.8 copy-done.2
  15.6 0.7 copy-done.5
  16.3 0.7 copy-done.6
  17.3 5.2 %collective-permute-start.2 = (bf16[2,128,256]{2,1,0:T(8,128)(2,1)S(1)}, bf16[2,128,256]{2,1,0:T(8,128)(2,1)S(1)}, u32[]{:S(2)}, u32[]{:S(2)}) collective-permute-start(bf16[2,128,256]{2,1,0:T(8,128)(2,1)S(1)} %join.2.first), channel_id=1, source_target_pairs={{0,128},{8,136},{16,144},{24,152},{32,160},{40,168},{48,176},{56,1... | collective-permute-start | bytes 393224 | tf_op jit(solution)/shard_map/ppermute | solution.py:360
  22.5 4.5 %sparse.1 = (f32[8,256,128]{2,1,0:T(8,128)S(1)}, f32[8,256,128]{2,1,0:T(8,128)S(1)}, bf16[8,256,128]{2,1,0:T(8,128)(2,1)S(1)}, bf16[8,256,128]{2,1,0:T(8,128)(2,1)S(1)}) custom-call(s32[8,128]{1,0:T(8,128)S(1)} %get-tuple-element.27.plan, bf16[8,144,256]{2,1,0:T(8,128)(2,1)S(1)} %all-to-all-done.grads, bf16[192,128,128]{2,1,0:T(8,128)(2,1)} %bitcast.12), custom_call_target="tpu_custom_call" | custom-call | flops 4000000000 | bytes 12582912 | tf_op jit(solution)/shard_map/sparse/pallas_call | solution.py:224
  27.1 6.1 %collective-permute-start.3 = (bf16[8,256,128]{2,1,0:T(8,128)(2,1)S(1)}, bf16[8,256,128]{2,1,0:T(8,128)(2,1)S(1)}, u32[]{:S(2)}, u32[]{:S(2)}) collective-permute-start(bf16[8,256,128]{2,1,0:T(8,128)(2,1)S(1)} %get-tuple-element.33), channel_id=1, source_target_pairs={{0,8},{8,0},{16,24},{24,16},{32,40},{40,32},{48,56},{56,48},{64,72... | collective-permute-start | bytes 1572872 | tf_op jit(solution)/shard_map/ppermute | solution.py:53
  33.3 1.4 %collective-permute-done.3 = bf16[8,256,128]{2,1,0:T(8,128)(2,1)S(1)} collective-permute-done((bf16[8,256,128]{2,1,0:T(8,128)(2,1)S(1)}, bf16[8,256,128]{2,1,0:T(8,128)(2,1)S(1)}, u32[]{:S(2)}, u32[]{:S(2)}) %collective-permute-start.3) | collective-permute-done | bytes 524320 | tf_op jit(solution)/shard_map/ppermute | solution.py:53
  35.1 7.5 %collective-permute-done.5.feats_high = bf16[4,128,256]{2,1,0:T(8,128)(2,1)S(1)} collective-permute-done((bf16[4,128,256]{2,1,0:T(8,128)(2,1)S(1)}, bf16[4,128,256]{2,1,0:T(8,128)(2,1)S(1)}, u32[]{:S(2)}, u32[]{:S(2)}) %collective-permute-start.5) | collective-permute-done | bytes 262176 | tf_op jit(solution)/shard_map/ppermute | solution.py:364
  42.6 5.5 %collective-permute-done.4.x_part = bf16[8,256,128]{2,1,0:T(8,128)(2,1)S(1)} collective-permute-done((bf16[8,256,128]{2,1,0:T(8,128)(2,1)S(1)}, bf16[8,256,128]{2,1,0:T(8,128)(2,1)S(1)}, u32[]{:S(2)}, u32[]{:S(2)}) %collective-permute-start.4) | collective-permute-done | bytes 524320 | tf_op jit(solution)/shard_map/ppermute | solution.py:360
  48.1 1.2 %copy-done.8 = f32[8,256,128]{2,1,0:T(8,128)S(1)} copy-done((f32[8,256,128]{2,1,0:T(8,128)S(1)}, f32[8,256,128]{2,1,0:T(8,128)}, u32[]{:S(2)}) %copy-start.8) | copy-done | bytes 1048600
  49.3 0.5 neigh.1
  49.9 1.3 %collective-permute-start.6 = (f32[256,256]{1,0:T(8,128)S(1)}, f32[256,256]{1,0:T(8,128)S(1)}, u32[]{:S(2)}, u32[]{:S(2)}) collective-permute-start(f32[256,256]{1,0:T(8,128)S(1)} %get-tuple-element.38), channel_id=1, source_target_pairs={{0,8},{8,0},{16,24},{24,16},{32,40},{40,32},{48,56},{56,48},{64,72... | collective-permute-start | bytes 786440 | tf_op jit(solution)/shard_map/ppermute | solution.py:53
  51.1 1.3 %collective-permute-start.7 = (bf16[4,256,128]{2,1,0:T(8,128)(2,1)S(1)}, bf16[4,256,128]{2,1,0:T(8,128)(2,1)S(1)}, u32[]{:S(2)}, u32[]{:S(2)}) collective-permute-start(bf16[4,256,128]{2,1,0:T(8,128)(2,1)S(1)} %get-tuple-element.40), channel_id=1, source_target_pairs={{0,64},{8,72},{16,80},{24,88},{32,96},{40,104},{48,112},{56,120},{... | collective-permute-start | bytes 786440 | tf_op jit(solution)/shard_map/ppermute | solution.py:360
  52.5 0.7 add.7
  53.2 7.1 %all-to-all-start.1 = ((f32[16,16,256]{2,1,0:T(8,128)}), f32[16,16,256]{2,1,0:T(8,128)S(1)}, u32[]{:S(2)}, u32[]{:S(2)}) async-start(f32[16,16,256]{2,1,0:T(8,128)} %bitcast.5), calls=%async_computation.1 | async-start | bytes 524288 | tf_op jit(solution)/shard_map/all_to_all | solution.py:43
  60.3 5.5 %collective-permute-done.7.got = bf16[4,256,128]{2,1,0:T(8,128)(2,1)S(1)} collective-permute-done((bf16[4,256,128]{2,1,0:T(8,128)(2,1)S(1)}, bf16[4,256,128]{2,1,0:T(8,128)(2,1)S(1)}, u32[]{:S(2)}, u32[]{:S(2)}) %collective-permute-start.7) | collective-permute-done | bytes 262176 | tf_op jit(solution)/shard_map/ppermute | solution.py:360
  65.8 2.1 %all-to-all-done.1.pieces = f32[16,16,256]{2,1,0:T(8,128)S(1)} async-done(((f32[16,16,256]{2,1,0:T(8,128)}), f32[16,16,256]{2,1,0:T(8,128)S(1)}, u32[]{:S(2)}, u32[]{:S(2)}) %all-to-all-start.1) | async-done | bytes 262176 | tf_op jit(solution)/shard_map/all_to_all | solution.py:43
  67.9 0.7 fold.2
  68.6 3.6 %all-to-all-start.2 = ((f32[8,16,256]{2,1,0:T(8,128)}), f32[8,16,256]{2,1,0:T(8,128)S(1)}, u32[]{:S(2)}, u32[]{:S(2)}) async-start(f32[8,16,256]{2,1,0:T(8,128)} %get-tuple-element.41), calls=%async_computation.2 | async-start | bytes 262144 | tf_op jit(solution)/shard_map/all_to_all | solution.py:43
  72.2 3.8 %collective-permute-done.8.got = bf16[2,256,128]{2,1,0:T(8,128)(2,1)S(1)} collective-permute-done((bf16[2,256,128]{2,1,0:T(8,128)(2,1)S(1)}, bf16[2,256,128]{2,1,0:T(8,128)(2,1)S(1)}, u32[]{:S(2)}, u32[]{:S(2)}) %collective-permute-start.8) | collective-permute-done | bytes 131104 | tf_op jit(solution)/shard_map/ppermute | solution.py:364
  76.0 4.2 %all-to-all-done.2.pieces = f32[8,16,256]{2,1,0:T(8,128)S(1)} async-done(((f32[8,16,256]{2,1,0:T(8,128)}), f32[8,16,256]{2,1,0:T(8,128)S(1)}, u32[]{:S(2)}, u32[]{:S(2)}) %all-to-all-start.2) | async-done | bytes 131104 | tf_op jit(solution)/shard_map/all_to_all | solution.py:43
  80.2 0.7 fold.3
  80.9 4.8 %all-to-all-start.3 = ((f32[16,16,256]{2,1,0:T(8,128)}), f32[16,16,256]{2,1,0:T(8,128)S(1)}, u32[]{:S(2)}, u32[]{:S(2)}) async-start(f32[16,16,256]{2,1,0:T(8,128)} %get-tuple-element.45), calls=%async_computation.3 | async-start | bytes 524288 | tf_op jit(solution)/shard_map/all_to_all | solution.py:43
  85.8 1.8 %collective-permute-start.9 = (bf16[1,256,128]{2,1,0:T(8,128)(2,1)S(1)}, bf16[1,256,128]{2,1,0:T(8,128)(2,1)S(1)}, u32[]{:S(2)}, u32[]{:S(2)}) collective-permute-start(bf16[1,256,128]{2,1,0:T(8,128)(2,1)S(1)} %get-tuple-element.46), channel_id=1, source_target_pairs={{0,128},{8,136},{16,144},{24,152},{32,160},{40,168},{48,176},{56,1... | collective-permute-start | bytes 196616 | tf_op jit(solution)/shard_map/ppermute | solution.py:360
  87.6 5.3 %collective-permute-done.9.part = bf16[1,256,128]{2,1,0:T(8,128)(2,1)S(1)} collective-permute-done((bf16[1,256,128]{2,1,0:T(8,128)(2,1)S(1)}, bf16[1,256,128]{2,1,0:T(8,128)(2,1)S(1)}, u32[]{:S(2)}, u32[]{:S(2)}) %collective-permute-start.9) | collective-permute-done | bytes 65568 | tf_op jit(solution)/shard_map/ppermute | solution.py:360
  93.2 3.8 %collective-permute-start.10 = (f32[256,256]{1,0:T(8,128)S(1)}, f32[256,256]{1,0:T(8,128)S(1)}, u32[]{:S(2)}, u32[]{:S(2)}) collective-permute-start(f32[256,256]{1,0:T(8,128)S(1)} %bitcast.7), channel_id=1, source_target_pairs={{0,8},{8,0},{16,24},{24,16},{32,40},{40,32},{48,56},{56,48},{64,72... | collective-permute-start | bytes 786440 | tf_op jit(solution)/shard_map/ppermute | solution.py:53
  97.1 1.2 %collective-permute-done.10.other = f32[256,256]{1,0:T(8,128)S(1)} collective-permute-done((f32[256,256]{1,0:T(8,128)S(1)}, f32[256,256]{1,0:T(8,128)S(1)}, u32[]{:S(2)}, u32[]{:S(2)}) %collective-permute-start.10) | collective-permute-done | bytes 262176 | tf_op jit(solution)/shard_map/ppermute | solution.py:53
  98.3 1.0 %last.1 = (bf16[128,256]{1,0:T(8,128)(2,1)}, f32[256,256]{1,0:T(8,128)}, f32[256,256]{1,0:T(8,128)}) custom-call(s32[1]{0:T(128)} %bitcast.core, f32[1,256,128]{2,1,0:T(8,128)S(1)} %get-tuple-element.44.own, bf16[1,256,128]{2,1,0:T(8,128)(2,1)S(1)} %collective-permute-done.9.part, bf16[128,256]{1,0:T(8,128)(2,1)S(1)} %copy-done.1, ...), custom_call_target="tpu_custom_call" | custom-call | tf_op jit(solution)/shard_map/last/pallas_call | solution.py:345
  (27 shorter events, 1.2 us)
Async XLA Ops:
  2.8 19.7 %all-to-all-start = ((bf16[8,144,256]{2,1,0:T(8,128)(2,1)}), bf16[8,144,256]{2,1,0:T(8,128)(2,1)S(1)}, u32[]{:S(2)}, u32[]{:S(2)}) async-start(bf16[8,144,256]{2,1,0:T(8,128)(2,1)} %head.1), calls=%async_computation | async-start | bytes 1179648 | tf_op jit(solution)/shard_map/all_to_all | solution.py:43
  10.3 7.0 %collective-permute-start = (bf16[1,128,256]{2,1,0:T(8,128)(2,1)}, bf16[1,128,256]{2,1,0:T(8,128)(2,1)S(1)}, u32[]{:S(2)}, u32[]{:S(2)}) collective-permute-start(bf16[1,128,256]{2,1,0:T(8,128)(2,1)} %bitcast.9), channel_id=1, source_target_pairs={{0,64},{8,72},{16,80},{24,88},{32,96},{40,104},{48,112},{56,120},{... | collective-permute-start | bytes 196616 | tf_op jit(solution)/shard_map/ppermute | solution.py:360
  13.9 0.8 copy-start
  14.7 0.8 copy-start.2
  15.6 0.7 copy-start.5
  16.3 0.7 copy-start.6
  17.3 9.8 %collective-permute-start.2 = (bf16[2,128,256]{2,1,0:T(8,128)(2,1)S(1)}, bf16[2,128,256]{2,1,0:T(8,128)(2,1)S(1)}, u32[]{:S(2)}, u32[]{:S(2)}) collective-permute-start(bf16[2,128,256]{2,1,0:T(8,128)(2,1)S(1)} %join.2.first), channel_id=1, source_target_pairs={{0,128},{8,136},{16,144},{24,152},{32,160},{40,168},{48,176},{56,1... | collective-permute-start | bytes 393224 | tf_op jit(solution)/shard_map/ppermute | solution.py:360
  27.0 8.0 %copy-start.7 = (f32[8,256,128]{2,1,0:T(8,128)}, f32[8,256,128]{2,1,0:T(8,128)S(1)}, u32[]{:S(2)}) copy-start(f32[8,256,128]{2,1,0:T(8,128)S(1)} %get-tuple-element.29.near) | copy-start | bytes 3145732
  27.0 71.2 %copy-start.1 = (bf16[128,256]{1,0:T(8,128)(2,1)S(1)}, bf16[128,256]{1,0:T(8,128)(2,1)}, u32[]{:S(2)}) copy-start(bf16[128,256]{1,0:T(8,128)(2,1)} %grads.5) | copy-start | bytes 196612
  27.0 71.2 %copy-start.3 = (bf16[256,256]{1,0:T(8,128)(2,1)S(1)}, bf16[256,256]{1,0:T(8,128)(2,1)}, u32[]{:S(2)}) copy-start(bf16[256,256]{1,0:T(8,128)(2,1)} %w_self.1) | copy-start | bytes 393220
  27.0 71.2 %copy-start.4 = (bf16[256,256]{1,0:T(8,128)(2,1)S(1)}, bf16[256,256]{1,0:T(8,128)(2,1)}, u32[]{:S(2)}) copy-start(bf16[256,256]{1,0:T(8,128)(2,1)} %w_neigh.1) | copy-start | bytes 393220
  27.1 7.7 %collective-permute-start.3 = (bf16[8,256,128]{2,1,0:T(8,128)(2,1)S(1)}, bf16[8,256,128]{2,1,0:T(8,128)(2,1)S(1)}, u32[]{:S(2)}, u32[]{:S(2)}) collective-permute-start(bf16[8,256,128]{2,1,0:T(8,128)(2,1)S(1)} %get-tuple-element.33), channel_id=1, source_target_pairs={{0,8},{8,0},{16,24},{24,16},{32,40},{40,32},{48,56},{56,48},{64,72... | collective-permute-start | bytes 1572872 | tf_op jit(solution)/shard_map/ppermute | solution.py:53
  33.2 9.4 %collective-permute-start.1 = (bf16[8,256,128]{2,1,0:T(8,128)(2,1)S(1)}, bf16[8,256,128]{2,1,0:T(8,128)(2,1)S(1)}, u32[]{:S(2)}, u32[]{:S(2)}) collective-permute-start(bf16[8,256,128]{2,1,0:T(8,128)(2,1)S(1)} %get-tuple-element.30), channel_id=1, source_target_pairs={{0,8},{8,0},{16,24},{24,16},{32,40},{40,32},{48,56},{56,48},{64,72... | collective-permute-start | bytes 1572872 | tf_op jit(solution)/shard_map/ppermute | solution.py:53
  34.9 13.2 %collective-permute-start.4 = (bf16[8,256,128]{2,1,0:T(8,128)(2,1)S(1)}, bf16[8,256,128]{2,1,0:T(8,128)(2,1)S(1)}, u32[]{:S(2)}, u32[]{:S(2)}) collective-permute-start(bf16[8,256,128]{2,1,0:T(8,128)(2,1)S(1)} %add_convert_fusion), channel_id=1, source_target_pairs={{0,32},{8,40},{16,48},{24,56},{32,0},{40,8},{48,16},{56,24},{64,96... | collective-permute-start | bytes 1572872 | tf_op jit(solution)/shard_map/ppermute | solution.py:360
  35.0 7.6 %collective-permute-start.5 = (bf16[4,128,256]{2,1,0:T(8,128)(2,1)S(1)}, bf16[4,128,256]{2,1,0:T(8,128)(2,1)S(1)}, u32[]{:S(2)}, u32[]{:S(2)}) collective-permute-start(bf16[4,128,256]{2,1,0:T(8,128)(2,1)S(1)} %join.3.feats_low), channel_id=1, source_target_pairs={{0,16},{8,24},{16,0},{24,8},{32,48},{40,56},{48,32},{56,40},{64,80... | collective-permute-start | bytes 786440 | tf_op jit(solution)/shard_map/ppermute | solution.py:364
  48.1 1.2 %copy-start.8 = (f32[8,256,128]{2,1,0:T(8,128)S(1)}, f32[8,256,128]{2,1,0:T(8,128)}, u32[]{:S(2)}) copy-start(f32[8,256,128]{2,1,0:T(8,128)} %copy-done.7) | copy-start | bytes 3145732
  49.9 2.6 %collective-permute-start.6 = (f32[256,256]{1,0:T(8,128)S(1)}, f32[256,256]{1,0:T(8,128)S(1)}, u32[]{:S(2)}, u32[]{:S(2)}) collective-permute-start(f32[256,256]{1,0:T(8,128)S(1)} %get-tuple-element.38), channel_id=1, source_target_pairs={{0,8},{8,0},{16,24},{24,16},{32,40},{40,32},{48,56},{56,48},{64,72... | collective-permute-start | bytes 786440 | tf_op jit(solution)/shard_map/ppermute | solution.py:53
  51.1 14.6 %collective-permute-start.7 = (bf16[4,256,128]{2,1,0:T(8,128)(2,1)S(1)}, bf16[4,256,128]{2,1,0:T(8,128)(2,1)S(1)}, u32[]{:S(2)}, u32[]{:S(2)}) collective-permute-start(bf16[4,256,128]{2,1,0:T(8,128)(2,1)S(1)} %get-tuple-element.40), channel_id=1, source_target_pairs={{0,64},{8,72},{16,80},{24,88},{32,96},{40,104},{48,112},{56,120},{... | collective-permute-start | bytes 786440 | tf_op jit(solution)/shard_map/ppermute | solution.py:360
  53.2 14.6 %all-to-all-start.1 = ((f32[16,16,256]{2,1,0:T(8,128)}), f32[16,16,256]{2,1,0:T(8,128)S(1)}, u32[]{:S(2)}, u32[]{:S(2)}) async-start(f32[16,16,256]{2,1,0:T(8,128)} %bitcast.5), calls=%async_computation.1 | async-start | bytes 524288 | tf_op jit(solution)/shard_map/all_to_all | solution.py:43
  68.6 11.6 %all-to-all-start.2 = ((f32[8,16,256]{2,1,0:T(8,128)}), f32[8,16,256]{2,1,0:T(8,128)S(1)}, u32[]{:S(2)}, u32[]{:S(2)}) async-start(f32[8,16,256]{2,1,0:T(8,128)} %get-tuple-element.41), calls=%async_computation.2 | async-start | bytes 262144 | tf_op jit(solution)/shard_map/all_to_all | solution.py:43
  72.2 3.8 %collective-permute-start.8 = (bf16[2,256,128]{2,1,0:T(8,128)(2,1)S(1)}, bf16[2,256,128]{2,1,0:T(8,128)(2,1)S(1)}, u32[]{:S(2)}, u32[]{:S(2)}) collective-permute-start(bf16[2,256,128]{2,1,0:T(8,128)(2,1)S(1)} %get-tuple-element.43), channel_id=1, source_target_pairs={{0,16},{8,24},{16,0},{24,8},{32,48},{40,56},{48,32},{56,40},{64,80... | collective-permute-start | bytes 393224 | tf_op jit(solution)/shard_map/ppermute | solution.py:364
  80.9 12.3 %all-to-all-start.3 = ((f32[16,16,256]{2,1,0:T(8,128)}), f32[16,16,256]{2,1,0:T(8,128)S(1)}, u32[]{:S(2)}, u32[]{:S(2)}) async-start(f32[16,16,256]{2,1,0:T(8,128)} %get-tuple-element.45), calls=%async_computation.3 | async-start | bytes 524288 | tf_op jit(solution)/shard_map/all_to_all | solution.py:43
  85.8 7.1 %collective-permute-start.9 = (bf16[1,256,128]{2,1,0:T(8,128)(2,1)S(1)}, bf16[1,256,128]{2,1,0:T(8,128)(2,1)S(1)}, u32[]{:S(2)}, u32[]{:S(2)}) collective-permute-start(bf16[1,256,128]{2,1,0:T(8,128)(2,1)S(1)} %get-tuple-element.46), channel_id=1, source_target_pairs={{0,128},{8,136},{16,144},{24,152},{32,160},{40,168},{48,176},{56,1... | collective-permute-start | bytes 196616 | tf_op jit(solution)/shard_map/ppermute | solution.py:360
  93.2 5.0 %collective-permute-start.10 = (f32[256,256]{1,0:T(8,128)S(1)}, f32[256,256]{1,0:T(8,128)S(1)}, u32[]{:S(2)}, u32[]{:S(2)}) collective-permute-start(f32[256,256]{1,0:T(8,128)S(1)} %bitcast.7), channel_id=1, source_target_pairs={{0,8},{8,0},{16,24},{24,16},{32,40},{40,32},{48,56},{56,48},{64,72... | collective-permute-start | bytes 786440 | tf_op jit(solution)/shard_map/ppermute | solution.py:53

commit v3 on v2

--- a/solution.py
+++ b/solution.py
@@ -90,47 +90,52 @@
     )
     live = counts[0]
     slots = rows.shape[1]
-    narrow = lambda value: value.astype(jnp.float32).astype(jnp.bfloat16)
     slot = lax.broadcasted_iota(jnp.int32, (1, slots), 1)
     lanes = lax.broadcasted_iota(jnp.int32, (8, slots), 0)
     hot = jnp.where((rows[...] == lanes) & (slot < live), 1.0, 0.0)
     earlier = lax.broadcasted_iota(jnp.int32, (slots, slots), 0) < lax.broadcasted_iota(
         jnp.int32, (slots, slots), 1
     )
-    rank = jnp.dot(
-        hot.astype(jnp.bfloat16),
-        jnp.where(earlier, 1.0, 0.0).astype(jnp.bfloat16),
-        preferred_element_type=jnp.float32,
-    )
-    rank = jnp.sum(hot * rank, axis=0, keepdims=True).astype(jnp.int32)
-    pairs = (jnp.sum(hot, axis=1, keepdims=True).astype(jnp.int32) + 1) >> 1
-    start = jnp.zeros((8, 1), jnp.int32)
-    for r in range(7):
-        start += jnp.where(lax.broadcasted_iota(jnp.int32, (8, 1), 0) > r, pairs[r : r + 1], 0)
-    total = start[7:8] + pairs[7:8]
-    start = jnp.sum(hot * start.astype(jnp.float32), axis=0, keepdims=True).astype(jnp.int32)
-    pair = jnp.where(slot < live, start + (rank >> 1), -1)
+    earlier = jnp.where(earlier, 1.0, 0.0).astype(jnp.bfloat16)
+
+    def before(flags):
+        return jnp.dot(flags.astype(jnp.bfloat16), earlier, preferred_element_type=jnp.float32)
+
+    rank = jnp.sum(hot * before(hot), axis=0, keepdims=True).astype(jnp.int32)
+    count = jnp.sum(hot * jnp.sum(hot, axis=1, keepdims=True), axis=0, keepdims=True)
+    second = jnp.where((slot < live) & ((rank & 1) == 1), 1.0, 0.0)
+    single = jnp.where((slot < live) & ((rank & 1) == 0) & (rank + 1 == count.astype(jnp.int32)), 1.0, 0.0)
+    pairs = jnp.sum(second, axis=1, keepdims=True).astype(jnp.int32)
+    total = pairs + jnp.sum(single, axis=1, keepdims=True).astype(jnp.int32)
+    place_of_second = jnp.where(second > 0, before(jnp.broadcast_to(second, (8, slots)))[0:1], -1.0)
+    place_of_single = before(jnp.broadcast_to(single, (8, slots)))[0:1].astype(jnp.int32) + pairs
+    place_of_single = jnp.where(single > 0, place_of_single, -1)
+    key = jnp.where(slot < live, rows[...] * 256 + (rank >> 1), -1).astype(jnp.float32)
+    entry = lax.broadcasted_iota(jnp.int32, (128, slots), 0)
+    is_second = jnp.where(entry == place_of_second.astype(jnp.int32), 1.0, 0.0)
+    entry_key = jnp.sum(is_second * key, axis=1, keepdims=True)
+    is_first = (entry < pairs) & (key == entry_key) & (second == 0)
+    is_first = jnp.where(is_first | (entry == place_of_single), 1.0, 0.0)
     far = cols[...] ^ row[0]
     place = (far & 1) * 16 + (far & 4) * 2 + (far & 8) // 2 + (far & 2) + (far >> 4)
     values = jnp.where(lanes == 0, slot, 0) + jnp.where(lanes == 1, place, 0)
     values += jnp.where(lanes == 2, rows[...], 0) + jnp.where(lanes == 3, 1, 0)
-    mine = lax.broadcasted_iota(jnp.int32, (128, slots), 0) == pair
-    nt = (((1,), (1,)), ((), ()))
-
-    def pick(half):
-        chosen = jnp.where(mine & ((rank & 1) == half), 1.0, 0.0).astype(jnp.bfloat16)
-        picked = lax.dot_general(narrow(values), chosen, nt, preferred_element_type=jnp.float32)
-        return picked.astype(jnp.int32)
-
-    first, second = pick(0), pick(1)
-    plan[0:1, :] = first[0:1]
-    plan[1:2, :] = second[0:1]
-    plan[2:3, :] = first[1:2] + (1 - first[3:4]) * TRASH
-    plan[3:4, :] = second[1:2] + (1 - second[3:4]) * TRASH
-    plan[4:5, :] = first[2:3] + (1 - first[3:4]) * ZERO_ROW
+    values = values.astype(jnp.float32).astype(jnp.bfloat16)
+
+    def pick(chosen):
+        nt = (((1,), (1,)), ((), ()))
+        chosen = chosen.astype(jnp.bfloat16)
+        return lax.dot_general(values, chosen, nt, preferred_element_type=jnp.float32).astype(jnp.int32)
+
+    one, two = pick(is_first), pick(is_second)
+    plan[0:1, :] = one[0:1]
+    plan[1:2, :] = two[0:1]
+    plan[2:3, :] = one[1:2] + (1 - one[3:4]) * TRASH
+    plan[3:4, :] = two[1:2] + (1 - two[3:4]) * TRASH
+    plan[4:5, :] = one[2:3] + (1 - one[3:4]) * ZERO_ROW
     plan[5:6, :] = jnp.broadcast_to((total + UNROLL - 1) >> 3, (1, 128))
-    plan[6:7, :] = jnp.full((1, 128), (live + CHUNK - 1) >> 4, jnp.int32)
-    plan[7:8, :] = jnp.zeros((1, 128), jnp.int32)
+    plan[6:7, :] = (jnp.maximum(one[0:1], two[0:1]) >> 4) + 1
+    plan[7:8, :] = jnp.full((1, 128), (live + CHUNK - 1) >> 4, jnp.int32)
 
 
 def prep(counts, row, rows, cols, feats, grads):
@@ -164,8 +169,8 @@
     )(first, second)
 
 
-def sparse_kernel(plan, grads, tiles, near, away, near_out, away_out, lhs, acc, held, sems):
-    chunks = plan[6, 0]
+def sparse_kernel(plan, z, grads, tiles, near, away_a, away_b, near_out, away_out, lhs, acc, held, sems):
+    chunks = plan[7, 0]
 
     def piece(k):
         part = pl.ds(k * CHUNK, CHUNK)
@@ -193,9 +198,11 @@
 
     lax.fori_loop(0, 33, clear, 0)
 
-    lax.fori_loop(0, chunks, wait_piece, 0)
-
-    def pairs(step, carry):
+    def pairs(step, waited):
+        need = waited
+        for u in range(UNROLL):
+            need = jnp.maximum(need, plan[6, step * UNROLL + u])
+        lax.fori_loop(waited, need, wait_piece, 0)
         for u in range(UNROLL):
             p = step * UNROLL + u
             both = jnp.concatenate([held[plan[0, p]], held[plan[1, p]]], axis=1)
@@ -206,28 +213,36 @@
             )
             acc[plan[2, p]] += product[:, 0:128]
             acc[plan[3, p]] += product[:, 128:256]
-        return carry
-
-    lax.fori_loop(0, plan[5, 0], pairs, 0)
+        return need
+
+    waited = lax.fori_loop(0, plan[5, 0], pairs, jnp.int32(0))
+    lax.fori_loop(waited, chunks, wait_piece, 0)
+
+    turn = 4 ^ (((z[0] + 1) >> 1) + 1 & 1)
 
     def move(k, carry):
         near[k] = acc[k]
-        away[k] = acc[8 + k]
         near_out[k] = acc[16 + k].astype(jnp.bfloat16)
-        away_out[k] = acc[24 + k].astype(jnp.bfloat16)
+        away_a[k] = acc[8 + k, 0:128, :]
+        away_b[k] = acc[8 + (k ^ turn), 128:256, :]
+        away_out[0, k] = acc[24 + k, 0:128, :].astype(jnp.bfloat16)
+        away_out[1, k] = acc[24 + (k ^ turn), 128:256, :].astype(jnp.bfloat16)
         return carry
 
     lax.fori_loop(0, 8, move, 0)
 
 
-def sparse_product(plan, grads, tiles):
+def sparse_product(plan, z, grads, tiles):
     return pl.pallas_call(
         sparse_kernel,
-        in_specs=[SMEM, VMEM, pl.BlockSpec(memory_space=pl.ANY)],
-        out_specs=[VMEM] * 4,
-        out_shape=[
-            jax.ShapeDtypeStruct((8, 256, 128), kind)
-            for kind in (jnp.float32, jnp.float32, jnp.bfloat16, jnp.bfloat16)
+        in_specs=[SMEM, SMEM, VMEM, ANY],
+        out_specs=[VMEM] * 5,
+        out_shape=[
+            jax.ShapeDtypeStruct((8, 256, 128), jnp.float32),
+            jax.ShapeDtypeStruct((8, 128, 128), jnp.float32),
+            jax.ShapeDtypeStruct((8, 128, 128), jnp.float32),
+            jax.ShapeDtypeStruct((8, 256, 128), jnp.bfloat16),
+            jax.ShapeDtypeStruct((2, 8, 128, 128), jnp.bfloat16),
         ],
         scratch_shapes=[
             pltpu.VMEM((9, 256, 256), jnp.bfloat16),
@@ -238,26 +253,78 @@
         compiler_params=params(SPARSE_MIB),
         cost_estimate=pl.CostEstimate(flops=4 * 10**9, bytes_accessed=12 * MIB, transcendentals=0),
         name="sparse",
-    )(plan, grads, tiles)
-
-
-def neigh_kernel(core, near, core_part, x_part, feats_low, feats_high, own_self, keep, send, kept, sent):
-    total_t = jnp.zeros((256, 256), jnp.float32)
-    for k in range(8):
-        block = near[k] + core_part[k].astype(jnp.float32) + x_part[k].astype(jnp.float32)
+    )(plan, z[None], grads, tiles)
+
+
+def mid_kernel(away_a, away_b, part, out_a, out_b):
+    for k in range(8):
+        out_a[k] = (away_a[k] + part[0, k].astype(jnp.float32)).astype(jnp.bfloat16)
+        out_b[k] = (away_b[k] + part[1, k].astype(jnp.float32)).astype(jnp.bfloat16)
+
+
+def mid_part(away_a, away_b, part):
+    return pl.pallas_call(
+        mid_kernel,
+        in_specs=[VMEM] * 3,
+        out_specs=[VMEM] * 2,
+        out_shape=[jax.ShapeDtypeStruct((8, 128, 128), jnp.bfloat16)] * 2,
+        compiler_params=params(8),
+        name="mid",
+    )(away_a, away_b, part)
+
+
+def feat_of(low, high, k):
+    return (high if k & 2 else low)[(k & 1) * 2 + (k >> 2)]
+
+
+def base_kernel(near, core_part, feats_low, feats_high, base, total_t):
+    total = jnp.zeros((256, 256), jnp.float32)
+    for k in range(8):
+        block = near[k] + core_part[k].astype(jnp.float32)
+        base[k] = block
         high = block.astype(jnp.bfloat16)
         low = (block - high.astype(jnp.float32)).astype(jnp.bfloat16)
-        if k < 4:
-            keep[k] = block
-        else:
-            send[k - 4] = high
-        feat = (feats_high if k & 2 else feats_low)[(k & 1) * 2 + (k >> 2)]
-        total_t += jnp.dot(
+        feat = feat_of(feats_low, feats_high, k)
+        total += jnp.dot(
             jnp.concatenate([high, low], axis=1),
             jnp.concatenate([feat, feat], axis=0),
             preferred_element_type=jnp.float32,
         )
-    total = total_t.T
+    total_t[...] = total
+
+
+def base_part(near, core_part, feats_low, feats_high):
+    return pl.pallas_call(
+        base_kernel,
+        in_specs=[VMEM] * 4,
+        out_specs=[VMEM] * 2,
+        out_shape=[
+            jax.ShapeDtypeStruct((8, 256, 128), jnp.float32),
+            jax.ShapeDtypeStruct((256, 256), jnp.float32),
+        ],
+        compiler_params=params(12),
+        cost_estimate=pl.CostEstimate(flops=10**9, bytes_accessed=4 * MIB, transcendentals=0),
+        name="base",
+    )(near, core_part, feats_low, feats_high)
+
+
+def neigh_kernel(core, base, part_a, part_b, feats_low, feats_high, total_t, own_self, keep, send, kept, sent):
+    total = total_t[...]
+    z_part = [jnp.concatenate([part_a[k], part_b[k]], axis=0) for k in range(8)]
+    for k in range(0, 8, 2):
+        pair = [feat_of(feats_low, feats_high, k + u) for u in range(2)]
+        total += jnp.dot(
+            jnp.concatenate([z_part[k], z_part[k + 1]], axis=1),
+            jnp.concatenate(pair, axis=0),
+            preferred_element_type=jnp.float32,
+        )
+    total = total.T
+    for k in range(8):
+        block = base[k] + z_part[k].astype(jnp.float32)
+        if k < 4:
+            keep[k] = block
+        else:
+            send[k - 4] = block.astype(jnp.bfloat16)
     first = core[0] == 0
 
     @pl.when(first)
@@ -271,10 +338,10 @@
         sent[...] = own_self[...]
 
 
-def neigh_part(core, near, core_part, x_part, feats_low, feats_high, own_self):
+def neigh_part(core, base, part_a, part_b, feats_low, feats_high, total_t, own_self):
     return pl.pallas_call(
         neigh_kernel,
-        in_specs=[SMEM] + [VMEM] * 6,
+        in_specs=[SMEM] + [VMEM] * 7,
         out_specs=[VMEM] * 4,
         out_shape=[
             jax.ShapeDtypeStruct((4, 256, 128), jnp.float32),
@@ -282,10 +349,10 @@
             jax.ShapeDtypeStruct((256, 256), jnp.float32),
             jax.ShapeDtypeStruct((256, 256), jnp.float32),
         ],
-        compiler_params=params(16),
+        compiler_params=params(12),
         cost_estimate=pl.CostEstimate(flops=10**9, bytes_accessed=4 * MIB, transcendentals=0),
         name="neigh",
-    )(core[None], near, core_part, x_part, feats_low, feats_high, own_self)
+    )(core[None], base, part_a, part_b, feats_low, feats_high, total_t, own_self)
 
 
 def fold_kernel(scale, pieces, keep, got, out, *rest):
@@ -360,6 +427,15 @@
     return lax.ppermute(value, "row", [(row, row ^ (4 * distance)) for row in range(32)])
 
 
+def swap_z_other(value):
+    pairs = []
+    for row in range(32):
+        z = row >> 2
+        other = (z + 1) % 8 if z & 1 else (z - 1) % 8
+        pairs.append((row, other * 4 + (row & 3)))
+    return lax.ppermute(value, "row", pairs)
+
+
 def swap_x(value):
     return lax.ppermute(value, "row", [(row, row ^ 2) for row in range(32)])
 
@@ -374,14 +450,15 @@
     feats = join(feats, swap_z(feats, 2))
     feats_far = swap_z(feats, 4)
     group, feats, plan = lax.optimization_barrier((group, feats, plan))
-    near, away, near_out, away_out = sparse_product(plan, group, tiles[0])
+    near, away_a, away_b, near_out, away_out = sparse_product(plan, row >> 2, group, tiles[0])
     away_out, feats_far = lax.optimization_barrier((away_out, feats_far))
     feats = join(feats, feats_far)
-    away = (away + swap_core(away_out).astype(jnp.float32)).astype(jnp.bfloat16)
+    away_a, away_b = mid_part(away_a, away_b, swap_core(away_out))
     core_part = swap_core(near_out)
-    z_part = swap_z(away, 1)
+    part_a, part_b = swap_z(away_a, 1), swap_z_other(away_b)
     feats_x = swap_x(feats)
-    keep, send, kept, sent = neigh_part(core, near, core_part, z_part, feats, feats_x, own_self)
+    base, total_t = base_part(near, core_part, feats, feats_x)
+    keep, send, kept, sent = neigh_part(core, base, part_a, part_b, feats, feats_x, total_t, own_self)
     kept = kept + swap_core(sent)
     got = swap_z(send, 2)
     pieces = exchange(kept.reshape(16, 16, 256), ("xh", "xl", "y"))

time: 99.6 us -> 93.7 us (0.941)
  waiting for transfers between devices: 36.8 us -> 29 us
    ppermute x2, waiting for transfers between devices: 11.3 us -> 3.74 us  [swap_x(): return lax.ppermute(value, 'row', [(row, row ^ 2) for row in range(32)])]
    ppermute x5, waiting for transfers between devices: 16.3 us -> 10.9 us  [swap_z(): lax.ppermute(value, 'row', [(row, row ^ 4 * distance) for row in range(32)])]
    ppermute x4, starting transfers between devices: 11.4 us -> 7.14 us  [swap_core(): return lax.ppermute(value, 'row', [(row, row ^ 1) for row in range(32)])]
    ppermute x0 -> x1, starting transfers between devices: none -> 4.17 us  [swap_z_other(): return lax.ppermute(value, 'row', pairs)]
    ppermute x0 -> x1, waiting for transfers between devices: none -> 3.81 us  [swap_z_other(): return lax.ppermute(value, 'row', pairs)]
    pallas_call x2 -> x4, Pallas kernels: 5.06 us -> 5.76 us  [the longest x1 4.81 us: sparse_product(): pl.pallas_call(sparse_kernel, in_specs=[SMEM, SMEM, VMEM, ANY], out_specs...]
  transfers between devices with their start and end apart: 15 -> 16, of which waited for: 10 -> 11; matrix products, arithmetic and copies ran while one was open for 1% -> 1% of each run, Pallas kernels for 5% -> 6%
where the time goes in v3:
time: 93.7 us; the launch traced here: 93 us
  starting transfers between devices  46.6 us (50%)
  waiting for transfers between devices  29 us (31%)
  Pallas kernels  10.9 us (12%)
  local copies, waits for them, and re-layouts  4.27 us (5%)
  between operations  1.39 us (1%)
    all_to_all x4, starting transfers between devices, exchange(): lax.all_to_all(blocks, ('row', 'blk'), 0, 0, axis_index_groups=groups_of(...  22.6 us
    ppermute x5, starting transfers between devices, swap_z(): lax.ppermute(value, 'row', [(row, row ^ 4 * distance) for row in range(32)])  12.2 us
    ppermute x5, waiting for transfers between devices, swap_z(): lax.ppermute(value, 'row', [(row, row ^ 4 * distance) for row in range(32)])  10.9 us
    all_to_all x4, waiting for transfers between devices, exchange(): lax.all_to_all(blocks, ('row', 'blk'), 0, 0, axis_index_groups=groups_of(...  7.28 us
    ppermute x4, starting transfers between devices, swap_core(): return lax.ppermute(value, 'row', [(row, row ^ 1) for row in range(32)])  7.14 us
    pallas_call x1, Pallas kernels, sparse_product(): pl.pallas_call(sparse_kernel, in_specs=[SMEM, SMEM, VMEM, ANY], out_specs...  4.81 us
    unnamed x18, local copies, waits for them, and re-layouts  4.27 us
    ppermute x1, starting transfers between devices, swap_z_other(): return lax.ppermute(value, 'row', pairs)  4.17 us
  transfers between devices with their start and end apart: 16, of which 11 were waited for; matrix products, arithmetic and copies ran while one was open for 1% of the time, Pallas kernels for 6%

profile of v3, /device:TPU:1, one launch (start us, length us, event | category | flops | bytes accessed | tf_op | source)
XLA Modules:
  0.0 93.0 jit_solution(11994948331971936423)
XLA Ops:
  0.6 2.1 %head.1 = bf16[8,144,256]{2,1,0:T(8,128)(2,1)} custom-call(bf16[128,256]{1,0:T(8,128)(2,1)} %grads.5, s32[1,128]{1,0:T(1,128)} %bitcast.12), custom_call_target="tpu_custom_call" | custom-call | tf_op jit(solution)/shard_map/head/pallas_call | solution.py:76
  2.8 7.5 %all-to-all-start = ((bf16[8,144,256]{2,1,0:T(8,128)(2,1)}), bf16[8,144,256]{2,1,0:T(8,128)(2,1)S(1)}, u32[]{:S(2)}, u32[]{:S(2)}) async-start(bf16[8,144,256]{2,1,0:T(8,128)(2,1)} %head.1), calls=%async_computation | async-start | bytes 1179648 | tf_op jit(solution)/shard_map/all_to_all | solution.py:43
  10.2 3.0 %collective-permute-start = (bf16[1,128,256]{2,1,0:T(8,128)(2,1)}, bf16[1,128,256]{2,1,0:T(8,128)(2,1)S(1)}, u32[]{:S(2)}, u32[]{:S(2)}) collective-permute-start(bf16[1,128,256]{2,1,0:T(8,128)(2,1)} %bitcast.10), channel_id=1, source_target_pairs={{0,64},{8,72},{16,80},{24,88},{32,96},{40,104},{48,112},{56,120},{... | collective-permute-start | bytes 196616 | tf_op jit(solution)/shard_map/ppermute | solution.py:427
  13.9 0.8 copy-done
  14.7 0.8 copy-done.2
  15.6 0.7 copy-done.5
  16.3 0.7 copy-done.6
  17.5 5.2 %collective-permute-start.2 = (bf16[2,128,256]{2,1,0:T(8,128)(2,1)S(1)}, bf16[2,128,256]{2,1,0:T(8,128)(2,1)S(1)}, u32[]{:S(2)}, u32[]{:S(2)}) collective-permute-start(bf16[2,128,256]{2,1,0:T(8,128)(2,1)S(1)} %join.2.first), channel_id=1, source_target_pairs={{0,128},{8,136},{16,144},{24,152},{32,160},{40,168},{48,176},{56,1... | collective-permute-start | bytes 393224 | tf_op jit(solution)/shard_map/ppermute | solution.py:427
  22.7 4.8 %sparse.1 = (f32[8,256,128]{2,1,0:T(8,128)S(1)}, f32[8,128,128]{2,1,0:T(8,128)S(1)}, f32[8,128,128]{2,1,0:T(8,128)S(1)}, bf16[8,256,128]{2,1,0:T(8,128)(2,1)S(1)}, bf16[2,8,128,128]{3,2,1,0:T(8,128)(2,1)S(1)}) custom-call(s32[8,128]{1,0:T(8,128)S(1)} %get-tuple-element.32.plan, s32[1]{0:T(128)} %bitcast.4.z, bf16[8,144,256]{2,1,0:T(8,128)(2,1)S(1)} %all-to-all-done.grads, ...), custom_call_target="tpu_custom_call" | custom-call | flops 4000000000 | bytes 12582912 | tf_op jit(solution)/shard_map/sparse/pallas_call | solution.py:236
  27.5 2.0 %collective-permute-start.4 = (bf16[2,8,128,128]{3,2,1,0:T(8,128)(2,1)S(1)}, bf16[2,8,128,128]{3,2,1,0:T(8,128)(2,1)S(1)}, u32[]{:S(2)}, u32[]{:S(2)}) collective-permute-start(bf16[2,8,128,128]{3,2,1,0:T(8,128)(2,1)S(1)} %get-tuple-element.42), channel_id=1, source_target_pairs={{0,8},{8,0},{16,24},{24,16},{32,40},{40,32},{48,56},{56,48},{64,72... | collective-permute-start | bytes 1572872 | tf_op jit(solution)/shard_map/ppermute | solution.py:53
  30.0 1.0 %collective-permute-done.4.part = bf16[2,8,128,128]{3,2,1,0:T(8,128)(2,1)S(1)} collective-permute-done((bf16[2,8,128,128]{3,2,1,0:T(8,128)(2,1)S(1)}, bf16[2,8,128,128]{3,2,1,0:T(8,128)(2,1)S(1)}, u32[]{:S(2)}, u32[]{:S(2)}) %collective-permute-start.4) | collective-permute-done | bytes 524320 | tf_op jit(solution)/shard_map/ppermute | solution.py:53
  31.1 2.5 %collective-permute-start.5 = (bf16[8,128,128]{2,1,0:T(8,128)(2,1)S(1)}, bf16[8,128,128]{2,1,0:T(8,128)(2,1)S(1)}, u32[]{:S(2)}, u32[]{:S(2)}) collective-permute-start(bf16[8,128,128]{2,1,0:T(8,128)(2,1)S(1)} %get-tuple-element.43), channel_id=1, source_target_pairs={{0,32},{8,40},{16,48},{24,56},{32,0},{40,8},{48,16},{56,24},{64,96... | collective-permute-start | bytes 786440 | tf_op jit(solution)/shard_map/ppermute | solution.py:427
  33.6 4.2 %collective-permute-start.6 = (bf16[8,128,128]{2,1,0:T(8,128)(2,1)S(1)}, bf16[8,128,128]{2,1,0:T(8,128)(2,1)S(1)}, u32[]{:S(2)}, u32[]{:S(2)}) collective-permute-start(bf16[8,128,128]{2,1,0:T(8,128)(2,1)S(1)} %get-tuple-element.44), channel_id=1, source_target_pairs={{0,224},{8,232},{16,240},{24,248},{32,64},{40,72},{48,80},{56,88},... | collective-permute-start | bytes 786440 | tf_op jit(solution)/shard_map/ppermute | solution.py:436
  37.8 1.2 %copy-done.8 = f32[8,256,128]{2,1,0:T(8,128)S(1)} copy-done((f32[8,256,128]{2,1,0:T(8,128)S(1)}, f32[8,256,128]{2,1,0:T(8,128)}, u32[]{:S(2)}) %copy-start.8) | copy-done | bytes 1048600
  40.0 3.8 %collective-permute-done.6.part_b = bf16[8,128,128]{2,1,0:T(8,128)(2,1)S(1)} collective-permute-done((bf16[8,128,128]{2,1,0:T(8,128)(2,1)S(1)}, bf16[8,128,128]{2,1,0:T(8,128)(2,1)S(1)}, u32[]{:S(2)}, u32[]{:S(2)}) %collective-permute-start.6) | collective-permute-done | bytes 262176 | tf_op jit(solution)/shard_map/ppermute | solution.py:436
  44.2 1.3 %collective-permute-start.7 = (f32[256,256]{1,0:T(8,128)S(1)}, f32[256,256]{1,0:T(8,128)S(1)}, u32[]{:S(2)}, u32[]{:S(2)}) collective-permute-start(f32[256,256]{1,0:T(8,128)S(1)} %get-tuple-element.48), channel_id=1, source_target_pairs={{0,8},{8,0},{16,24},{24,16},{32,40},{40,32},{48,56},{56,48},{64,72... | collective-permute-start | bytes 786440 | tf_op jit(solution)/shard_map/ppermute | solution.py:53
  45.6 1.2 %collective-permute-done.7 = f32[256,256]{1,0:T(8,128)S(1)} collective-permute-done((f32[256,256]{1,0:T(8,128)S(1)}, f32[256,256]{1,0:T(8,128)S(1)}, u32[]{:S(2)}, u32[]{:S(2)}) %collective-permute-start.7) | collective-permute-done | bytes 262176 | tf_op jit(solution)/shard_map/ppermute | solution.py:53
  46.7 0.7 add.3
  47.4 6.4 %all-to-all-start.1 = ((f32[16,16,256]{2,1,0:T(8,128)}), f32[16,16,256]{2,1,0:T(8,128)S(1)}, u32[]{:S(2)}, u32[]{:S(2)}) async-start(f32[16,16,256]{2,1,0:T(8,128)} %bitcast.6), calls=%async_computation.1 | async-start | bytes 524288 | tf_op jit(solution)/shard_map/all_to_all | solution.py:43
  53.8 4.8 %collective-permute-done.8.got = bf16[4,256,128]{2,1,0:T(8,128)(2,1)S(1)} collective-permute-done((bf16[4,256,128]{2,1,0:T(8,128)(2,1)S(1)}, bf16[4,256,128]{2,1,0:T(8,128)(2,1)S(1)}, u32[]{:S(2)}, u32[]{:S(2)}) %collective-permute-start.8) | collective-permute-done | bytes 262176 | tf_op jit(solution)/shard_map/ppermute | solution.py:427
  58.6 2.8 %all-to-all-done.1.pieces = f32[16,16,256]{2,1,0:T(8,128)S(1)} async-done(((f32[16,16,256]{2,1,0:T(8,128)}), f32[16,16,256]{2,1,0:T(8,128)S(1)}, u32[]{:S(2)}, u32[]{:S(2)}) %all-to-all-start.1) | async-done | bytes 262176 | tf_op jit(solution)/shard_map/all_to_all | solution.py:43
  61.4 0.7 fold.2
  62.1 4.2 %all-to-all-start.2 = ((f32[8,16,256]{2,1,0:T(8,128)}), f32[8,16,256]{2,1,0:T(8,128)S(1)}, u32[]{:S(2)}, u32[]{:S(2)}) async-start(f32[8,16,256]{2,1,0:T(8,128)} %get-tuple-element.51), calls=%async_computation.2 | async-start | bytes 262144 | tf_op jit(solution)/shard_map/all_to_all | solution.py:43
  66.4 3.7 %collective-permute-done.9.got = bf16[2,256,128]{2,1,0:T(8,128)(2,1)S(1)} collective-permute-done((bf16[2,256,128]{2,1,0:T(8,128)(2,1)S(1)}, bf16[2,256,128]{2,1,0:T(8,128)(2,1)S(1)}, u32[]{:S(2)}, u32[]{:S(2)}) %collective-permute-start.9) | collective-permute-done | bytes 131104 | tf_op jit(solution)/shard_map/ppermute | solution.py:440
  70.2 4.2 %all-to-all-done.2.pieces = f32[8,16,256]{2,1,0:T(8,128)S(1)} async-done(((f32[8,16,256]{2,1,0:T(8,128)}), f32[8,16,256]{2,1,0:T(8,128)S(1)}, u32[]{:S(2)}, u32[]{:S(2)}) %all-to-all-start.2) | async-done | bytes 131104 | tf_op jit(solution)/shard_map/all_to_all | solution.py:43
  74.4 0.7 fold.3
  75.1 4.4 %all-to-all-start.3 = ((f32[16,16,256]{2,1,0:T(8,128)}), f32[16,16,256]{2,1,0:T(8,128)S(1)}, u32[]{:S(2)}, u32[]{:S(2)}) async-start(f32[16,16,256]{2,1,0:T(8,128)} %get-tuple-element.55), calls=%async_computation.3 | async-start | bytes 524288 | tf_op jit(solution)/shard_map/all_to_all | solution.py:43
  79.6 1.6 %collective-permute-start.10 = (bf16[1,256,128]{2,1,0:T(8,128)(2,1)S(1)}, bf16[1,256,128]{2,1,0:T(8,128)(2,1)S(1)}, u32[]{:S(2)}, u32[]{:S(2)}) collective-permute-start(bf16[1,256,128]{2,1,0:T(8,128)(2,1)S(1)} %get-tuple-element.56), channel_id=1, source_target_pairs={{0,128},{8,136},{16,144},{24,152},{32,160},{40,168},{48,176},{56,1... | collective-permute-start | bytes 196616 | tf_op jit(solution)/shard_map/ppermute | solution.py:427
  81.2 5.6 %collective-permute-done.10.part = bf16[1,256,128]{2,1,0:T(8,128)(2,1)S(1)} collective-permute-done((bf16[1,256,128]{2,1,0:T(8,128)(2,1)S(1)}, bf16[1,256,128]{2,1,0:T(8,128)(2,1)S(1)}, u32[]{:S(2)}, u32[]{:S(2)}) %collective-permute-start.10) | collective-permute-done | bytes 65568 | tf_op jit(solution)/shard_map/ppermute | solution.py:427
  87.0 3.8 %collective-permute-start.11 = (f32[256,256]{1,0:T(8,128)S(1)}, f32[256,256]{1,0:T(8,128)S(1)}, u32[]{:S(2)}, u32[]{:S(2)}) collective-permute-start(f32[256,256]{1,0:T(8,128)S(1)} %bitcast.8), channel_id=1, source_target_pairs={{0,8},{8,0},{16,24},{24,16},{32,40},{40,32},{48,56},{56,48},{64,72... | collective-permute-start | bytes 786440 | tf_op jit(solution)/shard_map/ppermute | solution.py:53
  90.8 1.2 %collective-permute-done.11.other = f32[256,256]{1,0:T(8,128)S(1)} collective-permute-done((f32[256,256]{1,0:T(8,128)S(1)}, f32[256,256]{1,0:T(8,128)S(1)}, u32[]{:S(2)}, u32[]{:S(2)}) %collective-permute-start.11) | collective-permute-done | bytes 262176 | tf_op jit(solution)/shard_map/ppermute | solution.py:53
  92.0 1.0 %last.1 = (bf16[128,256]{1,0:T(8,128)(2,1)}, f32[256,256]{1,0:T(8,128)}, f32[256,256]{1,0:T(8,128)}) custom-call(s32[1]{0:T(128)} %bitcast.core, f32[1,256,128]{2,1,0:T(8,128)S(1)} %get-tuple-element.54.own, bf16[1,256,128]{2,1,0:T(8,128)(2,1)S(1)} %collective-permute-done.10.part, bf16[128,256]{1,0:T(8,128)(2,1)S(1)} %copy-done.1, ...), custom_call_target="tpu_custom_call" | custom-call | tf_op jit(solution)/shard_map/last/pallas_call | solution.py:412
  (30 shorter events, 3.0 us)
Async XLA Ops:
  2.8 19.9 %all-to-all-start = ((bf16[8,144,256]{2,1,0:T(8,128)(2,1)}), bf16[8,144,256]{2,1,0:T(8,128)(2,1)S(1)}, u32[]{:S(2)}, u32[]{:S(2)}) async-start(bf16[8,144,256]{2,1,0:T(8,128)(2,1)} %head.1), calls=%async_computation | async-start | bytes 1179648 | tf_op jit(solution)/shard_map/all_to_all | solution.py:43
  10.2 7.2 %collective-permute-start = (bf16[1,128,256]{2,1,0:T(8,128)(2,1)}, bf16[1,128,256]{2,1,0:T(8,128)(2,1)S(1)}, u32[]{:S(2)}, u32[]{:S(2)}) collective-permute-start(bf16[1,128,256]{2,1,0:T(8,128)(2,1)} %bitcast.10), channel_id=1, source_target_pairs={{0,64},{8,72},{16,80},{24,88},{32,96},{40,104},{48,112},{56,120},{... | collective-permute-start | bytes 196616 | tf_op jit(solution)/shard_map/ppermute | solution.py:427
  13.9 0.8 copy-start
  14.7 0.8 copy-start.2
  15.6 0.7 copy-start.5
  16.3 0.7 copy-start.6
  17.5 10.0 %collective-permute-start.2 = (bf16[2,128,256]{2,1,0:T(8,128)(2,1)S(1)}, bf16[2,128,256]{2,1,0:T(8,128)(2,1)S(1)}, u32[]{:S(2)}, u32[]{:S(2)}) collective-permute-start(bf16[2,128,256]{2,1,0:T(8,128)(2,1)S(1)} %join.2.first), channel_id=1, source_target_pairs={{0,128},{8,136},{16,144},{24,152},{32,160},{40,168},{48,176},{56,1... | collective-permute-start | bytes 393224 | tf_op jit(solution)/shard_map/ppermute | solution.py:427
  27.5 6.1 %copy-start.7 = (f32[8,256,128]{2,1,0:T(8,128)}, f32[8,256,128]{2,1,0:T(8,128)S(1)}, u32[]{:S(2)}) copy-start(f32[8,256,128]{2,1,0:T(8,128)S(1)} %get-tuple-element.34.near) | copy-start | bytes 3145732
  27.5 3.5 %collective-permute-start.4 = (bf16[2,8,128,128]{3,2,1,0:T(8,128)(2,1)S(1)}, bf16[2,8,128,128]{3,2,1,0:T(8,128)(2,1)S(1)}, u32[]{:S(2)}, u32[]{:S(2)}) collective-permute-start(bf16[2,8,128,128]{3,2,1,0:T(8,128)(2,1)S(1)} %get-tuple-element.42), channel_id=1, source_target_pairs={{0,8},{8,0},{16,24},{24,16},{32,40},{40,32},{48,56},{56,48},{64,72... | collective-permute-start | bytes 1572872 | tf_op jit(solution)/shard_map/ppermute | solution.py:53
  29.5 8.3 %collective-permute-start.1 = (bf16[8,256,128]{2,1,0:T(8,128)(2,1)S(1)}, bf16[8,256,128]{2,1,0:T(8,128)(2,1)S(1)}, u32[]{:S(2)}, u32[]{:S(2)}) collective-permute-start(bf16[8,256,128]{2,1,0:T(8,128)(2,1)S(1)} %get-tuple-element.35), channel_id=1, source_target_pairs={{0,8},{8,0},{16,24},{24,16},{32,40},{40,32},{48,56},{56,48},{64,72... | collective-permute-start | bytes 1572872 | tf_op jit(solution)/shard_map/ppermute | solution.py:53
  29.6 8.2 %collective-permute-start.3 = (bf16[4,128,256]{2,1,0:T(8,128)(2,1)S(1)}, bf16[4,128,256]{2,1,0:T(8,128)(2,1)S(1)}, u32[]{:S(2)}, u32[]{:S(2)}) collective-permute-start(bf16[4,128,256]{2,1,0:T(8,128)(2,1)S(1)} %join.3.feats_low), channel_id=1, source_target_pairs={{0,16},{8,24},{16,0},{24,8},{32,48},{40,56},{48,32},{56,40},{64,80... | collective-permute-start | bytes 786440 | tf_op jit(solution)/shard_map/ppermute | solution.py:440
  31.0 60.9 %copy-start.1 = (bf16[128,256]{1,0:T(8,128)(2,1)S(1)}, bf16[128,256]{1,0:T(8,128)(2,1)}, u32[]{:S(2)}) copy-start(bf16[128,256]{1,0:T(8,128)(2,1)} %grads.5) | copy-start | bytes 196612
  31.0 60.9 %copy-start.3 = (bf16[256,256]{1,0:T(8,128)(2,1)S(1)}, bf16[256,256]{1,0:T(8,128)(2,1)}, u32[]{:S(2)}) copy-start(bf16[256,256]{1,0:T(8,128)(2,1)} %w_self.1) | copy-start | bytes 393220
  31.0 60.9 %copy-start.4 = (bf16[256,256]{1,0:T(8,128)(2,1)S(1)}, bf16[256,256]{1,0:T(8,128)(2,1)}, u32[]{:S(2)}) copy-start(bf16[256,256]{1,0:T(8,128)(2,1)} %w_neigh.1) | copy-start | bytes 393220
  31.1 8.9 %collective-permute-start.5 = (bf16[8,128,128]{2,1,0:T(8,128)(2,1)S(1)}, bf16[8,128,128]{2,1,0:T(8,128)(2,1)S(1)}, u32[]{:S(2)}, u32[]{:S(2)}) collective-permute-start(bf16[8,128,128]{2,1,0:T(8,128)(2,1)S(1)} %get-tuple-element.43), channel_id=1, source_target_pairs={{0,32},{8,40},{16,48},{24,56},{32,0},{40,8},{48,16},{56,24},{64,96... | collective-permute-start | bytes 786440 | tf_op jit(solution)/shard_map/ppermute | solution.py:427
  33.6 10.2 %collective-permute-start.6 = (bf16[8,128,128]{2,1,0:T(8,128)(2,1)S(1)}, bf16[8,128,128]{2,1,0:T(8,128)(2,1)S(1)}, u32[]{:S(2)}, u32[]{:S(2)}) collective-permute-start(bf16[8,128,128]{2,1,0:T(8,128)(2,1)S(1)} %get-tuple-element.44), channel_id=1, source_target_pairs={{0,224},{8,232},{16,240},{24,248},{32,64},{40,72},{48,80},{56,88},... | collective-permute-start | bytes 786440 | tf_op jit(solution)/shard_map/ppermute | solution.py:436
  37.8 1.2 %copy-start.8 = (f32[8,256,128]{2,1,0:T(8,128)S(1)}, f32[8,256,128]{2,1,0:T(8,128)}, u32[]{:S(2)}) copy-start(f32[8,256,128]{2,1,0:T(8,128)} %copy-done.7) | copy-start | bytes 3145732
  44.2 2.5 %collective-permute-start.7 = (f32[256,256]{1,0:T(8,128)S(1)}, f32[256,256]{1,0:T(8,128)S(1)}, u32[]{:S(2)}, u32[]{:S(2)}) collective-permute-start(f32[256,256]{1,0:T(8,128)S(1)} %get-tuple-element.48), channel_id=1, source_target_pairs={{0,8},{8,0},{16,24},{24,16},{32,40},{40,32},{48,56},{56,48},{64,72... | collective-permute-start | bytes 786440 | tf_op jit(solution)/shard_map/ppermute | solution.py:53
  45.5 13.1 %collective-permute-start.8 = (bf16[4,256,128]{2,1,0:T(8,128)(2,1)S(1)}, bf16[4,256,128]{2,1,0:T(8,128)(2,1)S(1)}, u32[]{:S(2)}, u32[]{:S(2)}) collective-permute-start(bf16[4,256,128]{2,1,0:T(8,128)(2,1)S(1)} %get-tuple-element.50), channel_id=1, source_target_pairs={{0,64},{8,72},{16,80},{24,88},{32,96},{40,104},{48,112},{56,120},{... | collective-permute-start | bytes 786440 | tf_op jit(solution)/shard_map/ppermute | solution.py:427
  47.4 13.9 %all-to-all-start.1 = ((f32[16,16,256]{2,1,0:T(8,128)}), f32[16,16,256]{2,1,0:T(8,128)S(1)}, u32[]{:S(2)}, u32[]{:S(2)}) async-start(f32[16,16,256]{2,1,0:T(8,128)} %bitcast.6), calls=%async_computation.1 | async-start | bytes 524288 | tf_op jit(solution)/shard_map/all_to_all | solution.py:43
  62.1 12.3 %all-to-all-start.2 = ((f32[8,16,256]{2,1,0:T(8,128)}), f32[8,16,256]{2,1,0:T(8,128)S(1)}, u32[]{:S(2)}, u32[]{:S(2)}) async-start(f32[8,16,256]{2,1,0:T(8,128)} %get-tuple-element.51), calls=%async_computation.2 | async-start | bytes 262144 | tf_op jit(solution)/shard_map/all_to_all | solution.py:43
  66.3 3.8 %collective-permute-start.9 = (bf16[2,256,128]{2,1,0:T(8,128)(2,1)S(1)}, bf16[2,256,128]{2,1,0:T(8,128)(2,1)S(1)}, u32[]{:S(2)}, u32[]{:S(2)}) collective-permute-start(bf16[2,256,128]{2,1,0:T(8,128)(2,1)S(1)} %get-tuple-element.53), channel_id=1, source_target_pairs={{0,16},{8,24},{16,0},{24,8},{32,48},{40,56},{48,32},{56,40},{64,80... | collective-permute-start | bytes 393224 | tf_op jit(solution)/shard_map/ppermute | solution.py:440
  75.1 11.9 %all-to-all-start.3 = ((f32[16,16,256]{2,1,0:T(8,128)}), f32[16,16,256]{2,1,0:T(8,128)S(1)}, u32[]{:S(2)}, u32[]{:S(2)}) async-start(f32[16,16,256]{2,1,0:T(8,128)} %get-tuple-element.55), calls=%async_computation.3 | async-start | bytes 524288 | tf_op jit(solution)/shard_map/all_to_all | solution.py:43
  79.6 7.1 %collective-permute-start.10 = (bf16[1,256,128]{2,1,0:T(8,128)(2,1)S(1)}, bf16[1,256,128]{2,1,0:T(8,128)(2,1)S(1)}, u32[]{:S(2)}, u32[]{:S(2)}) collective-permute-start(bf16[1,256,128]{2,1,0:T(8,128)(2,1)S(1)} %get-tuple-element.56), channel_id=1, source_target_pairs={{0,128},{8,136},{16,144},{24,152},{32,160},{40,168},{48,176},{56,1... | collective-permute-start | bytes 196616 | tf_op jit(solution)/shard_map/ppermute | solution.py:427
  87.0 4.9 %collective-permute-start.11 = (f32[256,256]{1,0:T(8,128)S(1)}, f32[256,256]{1,0:T(8,128)S(1)}, u32[]{:S(2)}, u32[]{:S(2)}) collective-permute-start(f32[256,256]{1,0:T(8,128)S(1)} %bitcast.8), channel_id=1, source_target_pairs={{0,8},{8,0},{16,24},{24,16},{32,40},{40,32},{48,56},{56,48},{64,72... | collective-permute-start | bytes 786440 | tf_op jit(solution)/shard_map/ppermute | solution.py:53

commit v4 on v3

--- a/solution.py
+++ b/solution.py
@@ -15,6 +15,7 @@
 TRASH = 32
 ZERO_ROW = 8
 MIB = 1024 * 1024
+DENSE_FLOPS = 5 * 10**9
 SPARSE_MIB = 48
 VMEM = pl.BlockSpec(memory_space=pltpu.VMEM)
 SMEM = pl.BlockSpec(memory_space=pltpu.SMEM)
@@ -57,34 +58,52 @@
     return pltpu.CompilerParams(vmem_limit_bytes=mib * MIB)
 
 
-def head_kernel(grads, degrees, out, degree, sems):
-    copies = [pltpu.make_async_copy(degrees, degree, sems.at[8])]
-    for k in range(8):
-        copies.append(pltpu.make_async_copy(grads, out.at[k, pl.ds(0, 128)], sems.at[k]))
-    for copy in copies:
-        copy.start()
-    copies[0].wait()
+def head_kernel(grads, degrees, out, block, degree, sems):
+    loads = [
+        pltpu.make_async_copy(degrees, degree, sems.at[8]),
+        pltpu.make_async_copy(grads, block.at[pl.ds(0, 128)], sems.at[9]),
+    ]
+    for load in loads:
+        load.start()
+    loads[0].wait()
     value = jnp.broadcast_to(degree[...], (DEG_ROWS, 128)).astype(jnp.float32)
-    for k in range(8):
-        out[k, 128 : 128 + DEG_ROWS, 0:128] = value.astype(jnp.bfloat16)
-        out[k, 128 : 128 + DEG_ROWS, 128:256] = jnp.zeros((DEG_ROWS, 128), jnp.bfloat16)
-    for copy in copies[1:]:
-        copy.wait()
+    block[128 : 128 + DEG_ROWS, 0:128] = value.astype(jnp.bfloat16)
+    block[128 : 128 + DEG_ROWS, 128:256] = jnp.zeros((DEG_ROWS, 128), jnp.bfloat16)
+    loads[1].wait()
+    stores = [pltpu.make_async_copy(block, out.at[k], sems.at[k]) for k in range(8)]
+    for store in stores:
+        store.start()
+    for store in stores:
+        store.wait()
 
 
 def head(grads, degrees):
     return pl.pallas_call(
         head_kernel,
         in_specs=[ANY, ANY],
-        out_specs=VMEM,
+        out_specs=ANY,
         out_shape=jax.ShapeDtypeStruct((8, 128 + DEG_ROWS, 256), jnp.bfloat16),
-        scratch_shapes=[pltpu.VMEM((1, 128), jnp.int32), pltpu.SemaphoreType.DMA((9,))],
+        scratch_shapes=[
+            pltpu.VMEM((128 + DEG_ROWS, 256), jnp.bfloat16),
+            pltpu.VMEM((1, 128), jnp.int32),
+            pltpu.SemaphoreType.DMA((10,)),
+        ],
         compiler_params=params(60),
         name="head",
     )(grads, degrees[None])
 
 
-def prep_kernel(counts, row, rows, cols, feats, grads, plan, own_self):
+def prep_kernel(counts, row, *refs):
+    sources, (plan, own_self, own), (rows, cols, grads), sems = refs[:4], refs[4:7], refs[7:10], refs[10]
+    feats = own.at[0]
+    copies = [
+        pltpu.make_async_copy(source, target, sems.at[k])
+        for k, (source, target) in enumerate(zip(sources, (rows, cols, feats, grads)))
+    ]
+    for copy in copies:
+        copy.start()
+    for copy in copies:
+        copy.wait()
     own_self[...] = lax.dot_general(
         feats[...], grads[...], (((0,), (0,)), ((), ())), preferred_element_type=jnp.float32
     )
@@ -141,32 +160,39 @@
 def prep(counts, row, rows, cols, feats, grads):
     return pl.pallas_call(
         prep_kernel,
-        in_specs=[SMEM, SMEM, VMEM, VMEM, VMEM, VMEM],
-        out_specs=[VMEM, VMEM],
+        in_specs=[SMEM, SMEM, ANY, ANY, ANY, ANY],
+        out_specs=[VMEM, VMEM, VMEM],
         out_shape=[
             jax.ShapeDtypeStruct((8, 128), jnp.int32),
             jax.ShapeDtypeStruct((256, 256), jnp.float32),
-        ],
-        compiler_params=params(10),
+            jax.ShapeDtypeStruct((1, 128, 256), jnp.bfloat16),
+        ],
+        scratch_shapes=[
+            pltpu.VMEM(rows.shape, jnp.int32),
+            pltpu.VMEM(cols.shape, jnp.int32),
+            pltpu.VMEM(grads.shape, jnp.bfloat16),
+            pltpu.SemaphoreType.DMA((4,)),
+        ],
+        compiler_params=params(60),
         cost_estimate=pl.CostEstimate(flops=0, bytes_accessed=4 * MIB, transcendentals=0),
         name="prep",
     )(counts, row[None], rows, cols, feats, grads)
 
 
-def join_kernel(first, second, out):
-    out[0 : first.shape[0]] = first[...]
-    out[first.shape[0] :] = second[...]
-
-
-def join(first, second):
+def join_kernel(*refs):
+    for k, ref in enumerate(refs[:-1]):
+        refs[-1][k] = ref[0]
+
+
+def join(*blocks):
     return pl.pallas_call(
         join_kernel,
-        in_specs=[VMEM, VMEM],
+        in_specs=[VMEM] * len(blocks),
         out_specs=VMEM,
-        out_shape=jax.ShapeDtypeStruct((2 * first.shape[0],) + first.shape[1:], first.dtype),
+        out_shape=jax.ShapeDtypeStruct((len(blocks),) + blocks[0].shape[1:], blocks[0].dtype),
         compiler_params=params(4),
         name="join",
-    )(first, second)
+    )(*blocks)
 
 
 def sparse_kernel(plan, z, grads, tiles, near, away_a, away_b, near_out, away_out, lhs, acc, held, sems):
@@ -184,8 +210,8 @@
         pl.when(k < chunks)(lambda k=k: piece(k).start())
     for k in range(8):
         grad_t = grads[k, 0:128, :].T.astype(jnp.float32)
-        degree = grads[k, 128:129, 0:128].astype(jnp.float32)
-        value = grad_t / degree
+        degree = 1.0 / grads[k, 128:129, 0:128].astype(jnp.float32)
+        value = grad_t * degree
         high = value.astype(jnp.bfloat16)
         low = (value - high.astype(jnp.float32)).astype(jnp.bfloat16)
         lhs[k, :, 0:128] = high
@@ -273,18 +299,20 @@
     )(away_a, away_b, part)
 
 
-def feat_of(low, high, k):
-    return (high if k & 2 else low)[(k & 1) * 2 + (k >> 2)]
-
-
-def base_kernel(near, core_part, feats_low, feats_high, base, total_t):
+def feat_of(z, low, high, k):
+    turn = z[0] & 2
+    place = [0, 1 + turn, 2, 3 - turn][(k & 1) * 2 + (k >> 2)]
+    return (high if k & 2 else low)[place]
+
+
+def base_kernel(z, near, core_part, feats_low, feats_high, base, total_t):
     total = jnp.zeros((256, 256), jnp.float32)
     for k in range(8):
         block = near[k] + core_part[k].astype(jnp.float32)
         base[k] = block
         high = block.astype(jnp.bfloat16)
         low = (block - high.astype(jnp.float32)).astype(jnp.bfloat16)
-        feat = feat_of(feats_low, feats_high, k)
+        feat = feat_of(z, feats_low, feats_high, k)
         total += jnp.dot(
             jnp.concatenate([high, low], axis=1),
             jnp.concatenate([feat, feat], axis=0),
@@ -293,10 +321,10 @@
     total_t[...] = total
 
 
-def base_part(near, core_part, feats_low, feats_high):
+def base_part(z, near, core_part, feats_low, feats_high):
     return pl.pallas_call(
         base_kernel,
-        in_specs=[VMEM] * 4,
+        in_specs=[SMEM] + [VMEM] * 4,
         out_specs=[VMEM] * 2,
         out_shape=[
             jax.ShapeDtypeStruct((8, 256, 128), jnp.float32),
@@ -305,14 +333,14 @@
         compiler_params=params(12),
         cost_estimate=pl.CostEstimate(flops=10**9, bytes_accessed=4 * MIB, transcendentals=0),
         name="base",
-    )(near, core_part, feats_low, feats_high)
-
-
-def neigh_kernel(core, base, part_a, part_b, feats_low, feats_high, total_t, own_self, keep, send, kept, sent):
+    )(z[None], near, core_part, feats_low, feats_high)
+
+
+def neigh_kernel(core, z, base, part_a, part_b, feats_low, feats_high, total_t, own_self, keep, send, kept, sent):
     total = total_t[...]
     z_part = [jnp.concatenate([part_a[k], part_b[k]], axis=0) for k in range(8)]
     for k in range(0, 8, 2):
-        pair = [feat_of(feats_low, feats_high, k + u) for u in range(2)]
+        pair = [feat_of(z, feats_low, feats_high, k + u) for u in range(2)]
         total += jnp.dot(
             jnp.concatenate([z_part[k], z_part[k + 1]], axis=1),
             jnp.concatenate(pair, axis=0),
@@ -338,10 +366,10 @@
         sent[...] = own_self[...]
 
 
-def neigh_part(core, base, part_a, part_b, feats_low, feats_high, total_t, own_self):
+def neigh_part(core, z, base, part_a, part_b, feats_low, feats_high, total_t, own_self):
     return pl.pallas_call(
         neigh_kernel,
-        in_specs=[SMEM] + [VMEM] * 7,
+        in_specs=[SMEM] * 2 + [VMEM] * 7,
         out_specs=[VMEM] * 4,
         out_shape=[
             jax.ShapeDtypeStruct((4, 256, 128), jnp.float32),
@@ -352,7 +380,7 @@
         compiler_params=params(12),
         cost_estimate=pl.CostEstimate(flops=10**9, bytes_accessed=4 * MIB, transcendentals=0),
         name="neigh",
-    )(core[None], base, part_a, part_b, feats_low, feats_high, total_t, own_self)
+    )(core[None], z[None], base, part_a, part_b, feats_low, feats_high, total_t, own_self)
 
 
 def fold_kernel(scale, pieces, keep, got, out, *rest):
@@ -385,19 +413,7 @@
     )(pieces, keep, got)
 
 
-def last_kernel(core, own, part, grads, w_self, w_neigh, full, other, grad_x, grad_self, grad_neigh):
-    first = core[0] == 0
-
-    @pl.when(first)
-    def _():
-        grad_self[...] = full[...]
-        grad_neigh[...] = other[...]
-
-    @pl.when(jnp.logical_not(first))
-    def _():
-        grad_self[...] = other[...]
-        grad_neigh[...] = full[...]
-
+def dense_kernel(own, part, grads, w_self, w_neigh, grad_x):
     total = own[0] + part[0].astype(jnp.float32)
     high = total.astype(jnp.bfloat16)
     low = (total - high.astype(jnp.float32)).astype(jnp.bfloat16)
@@ -408,23 +424,50 @@
     grad_x[...] = out.T.astype(jnp.bfloat16)
 
 
-def last(core, own, part, grads, w_self, w_neigh, full, other):
+def dense(own, part, grads, w_self, w_neigh):
+    return pl.pallas_call(
+        dense_kernel,
+        in_specs=[VMEM] * 5,
+        out_specs=VMEM,
+        out_shape=jax.ShapeDtypeStruct((128, 256), jnp.bfloat16),
+        compiler_params=params(8),
+        cost_estimate=pl.CostEstimate(flops=DENSE_FLOPS, bytes_accessed=MIB, transcendentals=0),
+        name="dense",
+    )(own, part, grads, w_self, w_neigh)
+
+
+def last_kernel(core, full, other, grad_self, grad_neigh):
+    first = core[0] == 0
+
+    @pl.when(first)
+    def _():
+        grad_self[...] = full[...]
+        grad_neigh[...] = other[...]
+
+    @pl.when(jnp.logical_not(first))
+    def _():
+        grad_self[...] = other[...]
+        grad_neigh[...] = full[...]
+
+
+def last(core, full, other):
     return pl.pallas_call(
         last_kernel,
-        in_specs=[SMEM] + [VMEM] * 7,
-        out_specs=[VMEM] * 3,
-        out_shape=[
-            jax.ShapeDtypeStruct((128, 256), jnp.bfloat16),
-            jax.ShapeDtypeStruct((256, 256), jnp.float32),
-            jax.ShapeDtypeStruct((256, 256), jnp.float32),
-        ],
+        in_specs=[SMEM] + [VMEM] * 2,
+        out_specs=[VMEM] * 2,
+        out_shape=[jax.ShapeDtypeStruct((256, 256), jnp.float32)] * 2,
         compiler_params=params(8),
         name="last",
-    )(core[None], own, part, grads, w_self, w_neigh, full, other)
+    )(core[None], full, other)
 
 
 def swap_z(value, distance):
     return lax.ppermute(value, "row", [(row, row ^ (4 * distance)) for row in range(32)])
+
+
+def shift_z(value, steps):
+    pairs = [(row, (row + 4 * steps) % 32) for row in range(32)]
+    return lax.ppermute(value, "row", pairs)
 
 
 def swap_z_other(value):
@@ -445,20 +488,20 @@
     core = row & 1
     node_total = 128 * 256
     group = exchange(head(grad_out, degrees), ("xh", "y"))
-    plan, own_self = prep(tile_counts, row, tile_rows, tile_cols, features, grad_out)
-    feats = features[None]
-    feats = join(feats, swap_z(feats, 2))
-    feats_far = swap_z(feats, 4)
-    group, feats, plan = lax.optimization_barrier((group, feats, plan))
-    near, away_a, away_b, near_out, away_out = sparse_product(plan, row >> 2, group, tiles[0])
-    away_out, feats_far = lax.optimization_barrier((away_out, feats_far))
-    feats = join(feats, feats_far)
+    plan, own_self, own = prep(tile_counts, row, tile_rows, tile_cols, features, grad_out)
+    z = row >> 2
+    above, below = shift_z(features[None], 6), shift_z(features[None], 2)
+    opposite = shift_z(above, 6)
+    group, above, below, plan = lax.optimization_barrier((group, above, below, plan))
+    near, away_a, away_b, near_out, away_out = sparse_product(plan, z, group, tiles[0])
+    away_out, opposite = lax.optimization_barrier((away_out, opposite))
+    feats = join(own, above, opposite, below)
     away_a, away_b = mid_part(away_a, away_b, swap_core(away_out))
     core_part = swap_core(near_out)
     part_a, part_b = swap_z(away_a, 1), swap_z_other(away_b)
     feats_x = swap_x(feats)
-    base, total_t = base_part(near, core_part, feats, feats_x)
-    keep, send, kept, sent = neigh_part(core, base, part_a, part_b, feats, feats_x, total_t, own_self)
+    base, total_t = base_part(z, near, core_part, feats, feats_x)
+    keep, send, kept, sent = neigh_part(core, z, base, part_a, part_b, feats, feats_x, total_t, own_self)
     kept = kept + swap_core(sent)
     got = swap_z(send, 2)
     pieces = exchange(kept.reshape(16, 16, 256), ("xh", "xl", "y"))
@@ -468,9 +511,10 @@
     pieces, keep, send = fold(1.0 / node_total, pieces, 16, keep, got)
     got = swap_z(send, 4)
     full = exchange(pieces, ("xh", "xl", "y")).reshape(256, 256)
-    full, got = lax.optimization_barrier((full, got))
     other = swap_core(full)
-    return last(core, keep, got, grad_out, w_self, w_neigh, full, other)
+    grad_x = dense(keep, got, grad_out, w_self, w_neigh)
+    grad_self, grad_neigh = last(core, full, other)
+    return grad_x, grad_self, grad_neigh
 
 
 def solution(mesh):

time: 93.7 us -> 92.8 us (level)
  starting transfers between devices: 46.6 us -> 49.7 us
  local copies, waits for them, and re-layouts: 4.27 us -> 1.93 us
  waiting for transfers between devices: 29 us -> 27.2 us
  Pallas kernels: 10.9 us -> 11.9 us
    ppermute x0 -> x3, starting transfers between devices: none -> 9.67 us  [shift_z(): return lax.ppermute(value, 'row', pairs)]
    ppermute x5 -> x3, starting transfers between devices: 12.2 us -> 3.39 us  [swap_z(): lax.ppermute(value, 'row', [(row, row ^ 4 * distance) for row in range(32)])]
    ppermute x5 -> x3, waiting for transfers between devices: 10.9 us -> 4.19 us  [swap_z(): lax.ppermute(value, 'row', [(row, row ^ 4 * distance) for row in range(32)])]
    all_to_all x4, waiting for transfers between devices: 7.28 us -> 13.2 us  [exchange(): lax.all_to_all(blocks, ('row', 'blk'), 0, 0, axis_index_groups=groups_of(...]
    unnamed x18 -> x16, local copies, waits for them, and re-layouts: 4.27 us -> 1.93 us
    all_to_all x4, starting transfers between devices: 22.6 us -> 24.8 us  [exchange(): lax.all_to_all(blocks, ('row', 'blk'), 0, 0, axis_index_groups=groups_of(...]
    pallas_call x7, Pallas kernels: 4.55 us -> 6.59 us  [the longest x1 2.18 us: prep(): pl.pallas_call(prep_kernel, in_specs=[SMEM, SMEM, ANY, ANY, ANY, ANY], ou...]
    ppermute x4, waiting for transfers between devices: 3.34 us -> 1.71 us  [swap_core(): return lax.ppermute(value, 'row', [(row, row ^ 1) for row in range(32)])]
  transfers between devices with their start and end apart: 16 -> 17, of which waited for: 11 -> 10; matrix products, arithmetic and copies ran while one was open for 1% -> 1% of each run, Pallas kernels for 6% -> 8%
where the time goes in v4:
time: 92.8 us; the launch traced here: 93 us
  starting transfers between devices  49.7 us (54%)
  waiting for transfers between devices  27.2 us (29%)
  Pallas kernels  11.9 us (13%)
  local copies, waits for them, and re-layouts  1.93 us (2%)
  between operations  1.43 us (2%)
    all_to_all x4, starting transfers between devices, exchange(): lax.all_to_all(blocks, ('row', 'blk'), 0, 0, axis_index_groups=groups_of(...  24.8 us
    all_to_all x4, waiting for transfers between devices, exchange(): lax.all_to_all(blocks, ('row', 'blk'), 0, 0, axis_index_groups=groups_of(...  13.2 us
    ppermute x3, starting transfers between devices, shift_z(): return lax.ppermute(value, 'row', pairs)  9.67 us
    ppermute x4, starting transfers between devices, swap_core(): return lax.ppermute(value, 'row', [(row, row ^ 1) for row in range(32)])  7.72 us
    ppermute x2, waiting for transfers between devices, swap_x(): return lax.ppermute(value, 'row', [(row, row ^ 2) for row in range(32)])  4.98 us
    ppermute x3, waiting for transfers between devices, swap_z(): lax.ppermute(value, 'row', [(row, row ^ 4 * distance) for row in range(32)])  4.19 us
    ppermute x1, starting transfers between devices, swap_z_other(): return lax.ppermute(value, 'row', pairs)  3.98 us
    pallas_call x1, Pallas kernels, sparse_product(): pl.pallas_call(sparse_kernel, in_specs=[SMEM, SMEM, VMEM, ANY], out_specs...  3.75 us
  transfers between devices with their start and end apart: 17, of which 10 were waited for; matrix products, arithmetic and copies ran while one was open for 1% of the time, Pallas kernels for 8%

profile of v4, /device:TPU:1, one launch (start us, length us, event | category | flops | bytes accessed | tf_op | source)
XLA Modules:
  0.0 93.0 jit_solution(15828219033238702596)
XLA Ops:
  0.6 1.8 %head.1 = bf16[8,144,256]{2,1,0:T(8,128)(2,1)} custom-call(bf16[128,256]{1,0:T(8,128)(2,1)} %grads.3, s32[1,128]{1,0:T(1,128)} %bitcast.12), custom_call_target="tpu_custom_call" | custom-call | tf_op jit(solution)/shard_map/head/pallas_call | solution.py:81
  2.4 7.5 %all-to-all-start = ((bf16[8,144,256]{2,1,0:T(8,128)(2,1)}), bf16[8,144,256]{2,1,0:T(8,128)(2,1)S(1)}, u32[]{:S(2)}, u32[]{:S(2)}) async-start(bf16[8,144,256]{2,1,0:T(8,128)(2,1)} %head.1), calls=%async_computation | async-start | bytes 1179648 | tf_op jit(solution)/shard_map/all_to_all | solution.py:44
  9.9 6.0 %collective-permute-start = (bf16[1,128,256]{2,1,0:T(8,128)(2,1)}, bf16[1,128,256]{2,1,0:T(8,128)(2,1)S(1)}, u32[]{:S(2)}, u32[]{:S(2)}) collective-permute-start(bf16[1,128,256]{2,1,0:T(8,128)(2,1)} %bitcast.10), channel_id=1, source_target_pairs={{0,192},{8,200},{16,208},{24,216},{32,224},{40,232},{48,240},{56,2... | collective-permute-start | bytes 196616 | tf_op jit(solution)/shard_map/ppermute | solution.py:470
  16.6 2.2 %prep.1 = (s32[8,128]{1,0:T(8,128)}, f32[256,256]{1,0:T(8,128)}, bf16[1,128,256]{2,1,0:T(8,128)(2,1)}) custom-call(s32[1]{0:T(128)S(6)} %copy.12.counts, s32[1]{0:T(128)} %bitcast.4.row, s32[1,192]{1,0:T(1,128)} %refs_0_.1, s32[1,192]{1,0:T(1,128)} %refs_1_.1, bf16[128,256]{1,0:T(8,128)(2,1)} %refs_2_.1, bf16[128,256]{1,0:T(8,128)(2,1)} %grads.3), custom_call_target="tpu_custom_call" | custom-call | bytes 4194304 | tf_op jit(solution)/shard_map/prep/pallas_call | solution.py:161
  18.8 3.6 %collective-permute-start.3 = (bf16[1,128,256]{2,1,0:T(8,128)(2,1)S(1)}, bf16[1,128,256]{2,1,0:T(8,128)(2,1)S(1)}, u32[]{:S(2)}, u32[]{:S(2)}) collective-permute-start(bf16[1,128,256]{2,1,0:T(8,128)(2,1)S(1)} %collective-permute-done.refs_1_), channel_id=1, source_target_pairs={{0,192},{8,200},{16,208},{24,216},{32,224},{40,232},{48,240},{56,2... | collective-permute-start | bytes 196616 | tf_op jit(solution)/shard_map/ppermute | solution.py:470
  22.4 0.7 copy-done.5
  23.1 3.8 %sparse.1 = (f32[8,256,128]{2,1,0:T(8,128)S(1)}, f32[8,128,128]{2,1,0:T(8,128)S(1)}, f32[8,128,128]{2,1,0:T(8,128)S(1)}, bf16[8,256,128]{2,1,0:T(8,128)(2,1)S(1)}, bf16[2,8,128,128]{3,2,1,0:T(8,128)(2,1)S(1)}) custom-call(s32[8,128]{1,0:T(8,128)S(1)} %copy-done.5, s32[1]{0:T(128)} %bitcast.1.z, bf16[8,144,256]{2,1,0:T(8,128)(2,1)S(1)} %all-to-all-done.grads, ...), custom_call_target="tpu_custom_call" | custom-call | flops 4000000000 | bytes 12582912 | tf_op jit(solution)/shard_map/sparse/pallas_call | solution.py:262
  26.9 3.2 %collective-permute-start.5 = (bf16[2,8,128,128]{3,2,1,0:T(8,128)(2,1)S(1)}, bf16[2,8,128,128]{3,2,1,0:T(8,128)(2,1)S(1)}, u32[]{:S(2)}, u32[]{:S(2)}) collective-permute-start(bf16[2,8,128,128]{3,2,1,0:T(8,128)(2,1)S(1)} %get-tuple-element.46), channel_id=1, source_target_pairs={{0,8},{8,0},{16,24},{24,16},{32,40},{40,32},{48,56},{56,48},{64,72... | collective-permute-start | bytes 1572872 | tf_op jit(solution)/shard_map/ppermute | solution.py:54
  30.3 1.3 %collective-permute-done.5.part = bf16[2,8,128,128]{3,2,1,0:T(8,128)(2,1)S(1)} collective-permute-done((bf16[2,8,128,128]{3,2,1,0:T(8,128)(2,1)S(1)}, bf16[2,8,128,128]{3,2,1,0:T(8,128)(2,1)S(1)}, u32[]{:S(2)}, u32[]{:S(2)}) %collective-permute-start.5) | collective-permute-done | bytes 524320 | tf_op jit(solution)/shard_map/ppermute | solution.py:54
  31.7 0.9 collective-permute-start.6
  32.6 4.0 %collective-permute-start.7 = (bf16[8,128,128]{2,1,0:T(8,128)(2,1)S(1)}, bf16[8,128,128]{2,1,0:T(8,128)(2,1)S(1)}, u32[]{:S(2)}, u32[]{:S(2)}) collective-permute-start(bf16[8,128,128]{2,1,0:T(8,128)(2,1)S(1)} %get-tuple-element.48), channel_id=1, source_target_pairs={{0,224},{8,232},{16,240},{24,248},{32,64},{40,72},{48,80},{56,88},... | collective-permute-start | bytes 786440 | tf_op jit(solution)/shard_map/ppermute | solution.py:479
  36.6 1.2 %collective-permute-done.4.feats_high = bf16[4,128,256]{2,1,0:T(8,128)(2,1)S(1)} collective-permute-done((bf16[4,128,256]{2,1,0:T(8,128)(2,1)S(1)}, bf16[4,128,256]{2,1,0:T(8,128)(2,1)S(1)}, u32[]{:S(2)}, u32[]{:S(2)}) %collective-permute-start.4) | collective-permute-done | bytes 262176 | tf_op jit(solution)/shard_map/ppermute | solution.py:483
  37.8 1.2 %copy-done.7 = f32[8,256,128]{2,1,0:T(8,128)S(1)} copy-done((f32[8,256,128]{2,1,0:T(8,128)S(1)}, f32[8,256,128]{2,1,0:T(8,128)}, u32[]{:S(2)}) %copy-start.7) | copy-done | bytes 1048600
  39.0 0.4 base.1
  39.4 3.2 %collective-permute-done.7.part_b = bf16[8,128,128]{2,1,0:T(8,128)(2,1)S(1)} collective-permute-done((bf16[8,128,128]{2,1,0:T(8,128)(2,1)S(1)}, bf16[8,128,128]{2,1,0:T(8,128)(2,1)S(1)}, u32[]{:S(2)}, u32[]{:S(2)}) %collective-permute-start.7) | collective-permute-done | bytes 262176 | tf_op jit(solution)/shard_map/ppermute | solution.py:479
  43.0 1.3 %collective-permute-start.8 = (f32[256,256]{1,0:T(8,128)S(1)}, f32[256,256]{1,0:T(8,128)S(1)}, u32[]{:S(2)}, u32[]{:S(2)}) collective-permute-start(f32[256,256]{1,0:T(8,128)S(1)} %get-tuple-element.52), channel_id=1, source_target_pairs={{0,8},{8,0},{16,24},{24,16},{32,40},{40,32},{48,56},{56,48},{64,72... | collective-permute-start | bytes 786440 | tf_op jit(solution)/shard_map/ppermute | solution.py:54
  44.3 0.9 %collective-permute-start.9 = (bf16[4,256,128]{2,1,0:T(8,128)(2,1)S(1)}, bf16[4,256,128]{2,1,0:T(8,128)(2,1)S(1)}, u32[]{:S(2)}, u32[]{:S(2)}) collective-permute-start(bf16[4,256,128]{2,1,0:T(8,128)(2,1)S(1)} %get-tuple-element.54), channel_id=1, source_target_pairs={{0,64},{8,72},{16,80},{24,88},{32,96},{40,104},{48,112},{56,120},{... | collective-permute-start | bytes 786440 | tf_op jit(solution)/shard_map/ppermute | solution.py:465
  45.5 0.7 add.3
  46.2 8.5 %all-to-all-start.1 = ((f32[16,16,256]{2,1,0:T(8,128)}), f32[16,16,256]{2,1,0:T(8,128)S(1)}, u32[]{:S(2)}, u32[]{:S(2)}) async-start(f32[16,16,256]{2,1,0:T(8,128)} %bitcast.6), calls=%async_computation.1 | async-start | bytes 524288 | tf_op jit(solution)/shard_map/all_to_all | solution.py:44
  54.7 4.2 %collective-permute-done.9.got = bf16[4,256,128]{2,1,0:T(8,128)(2,1)S(1)} collective-permute-done((bf16[4,256,128]{2,1,0:T(8,128)(2,1)S(1)}, bf16[4,256,128]{2,1,0:T(8,128)(2,1)S(1)}, u32[]{:S(2)}, u32[]{:S(2)}) %collective-permute-start.9) | collective-permute-done | bytes 262176 | tf_op jit(solution)/shard_map/ppermute | solution.py:465
  58.8 3.4 %all-to-all-done.1.pieces = f32[16,16,256]{2,1,0:T(8,128)S(1)} async-done(((f32[16,16,256]{2,1,0:T(8,128)}), f32[16,16,256]{2,1,0:T(8,128)S(1)}, u32[]{:S(2)}, u32[]{:S(2)}) %all-to-all-start.1) | async-done | bytes 262176 | tf_op jit(solution)/shard_map/all_to_all | solution.py:44
  62.2 0.7 fold.2
  62.9 3.4 %all-to-all-start.2 = ((f32[8,16,256]{2,1,0:T(8,128)}), f32[8,16,256]{2,1,0:T(8,128)S(1)}, u32[]{:S(2)}, u32[]{:S(2)}) async-start(f32[8,16,256]{2,1,0:T(8,128)} %get-tuple-element.55), calls=%async_computation.2 | async-start | bytes 262144 | tf_op jit(solution)/shard_map/all_to_all | solution.py:44
  66.4 3.8 %collective-permute-done.10.got = bf16[2,256,128]{2,1,0:T(8,128)(2,1)S(1)} collective-permute-done((bf16[2,256,128]{2,1,0:T(8,128)(2,1)S(1)}, bf16[2,256,128]{2,1,0:T(8,128)(2,1)S(1)}, u32[]{:S(2)}, u32[]{:S(2)}) %collective-permute-start.10) | collective-permute-done | bytes 131104 | tf_op jit(solution)/shard_map/ppermute | solution.py:483
  70.2 4.0 %all-to-all-done.2.pieces = f32[8,16,256]{2,1,0:T(8,128)S(1)} async-done(((f32[8,16,256]{2,1,0:T(8,128)}), f32[8,16,256]{2,1,0:T(8,128)S(1)}, u32[]{:S(2)}, u32[]{:S(2)}) %all-to-all-start.2) | async-done | bytes 131104 | tf_op jit(solution)/shard_map/all_to_all | solution.py:44
  74.2 0.7 fold.3
  75.0 5.5 %all-to-all-start.3 = ((f32[16,16,256]{2,1,0:T(8,128)}), f32[16,16,256]{2,1,0:T(8,128)S(1)}, u32[]{:S(2)}, u32[]{:S(2)}) async-start(f32[16,16,256]{2,1,0:T(8,128)} %get-tuple-element.60), calls=%async_computation.3 | async-start | bytes 524288 | tf_op jit(solution)/shard_map/all_to_all | solution.py:44
  80.4 1.6 %collective-permute-start.11 = (bf16[1,256,128]{2,1,0:T(8,128)(2,1)S(1)}, bf16[1,256,128]{2,1,0:T(8,128)(2,1)S(1)}, u32[]{:S(2)}, u32[]{:S(2)}) collective-permute-start(bf16[1,256,128]{2,1,0:T(8,128)(2,1)S(1)} %get-tuple-element.59), channel_id=1, source_target_pairs={{0,128},{8,136},{16,144},{24,152},{32,160},{40,168},{48,176},{56,1... | collective-permute-start | bytes 196616 | tf_op jit(solution)/shard_map/ppermute | solution.py:465
  82.0 5.8 %all-to-all-done.3 = f32[16,16,256]{2,1,0:T(8,128)S(1)} async-done(((f32[16,16,256]{2,1,0:T(8,128)}), f32[16,16,256]{2,1,0:T(8,128)S(1)}, u32[]{:S(2)}, u32[]{:S(2)}) %all-to-all-start.3) | async-done | bytes 262176 | tf_op jit(solution)/shard_map/all_to_all | solution.py:44
  87.8 3.2 %collective-permute-start.12 = (f32[256,256]{1,0:T(8,128)S(1)}, f32[256,256]{1,0:T(8,128)S(1)}, u32[]{:S(2)}, u32[]{:S(2)}) collective-permute-start(f32[256,256]{1,0:T(8,128)S(1)} %bitcast.8), channel_id=1, source_target_pairs={{0,8},{8,0},{16,24},{24,16},{32,40},{40,32},{48,56},{56,48},{64,72... | collective-permute-start | bytes 786440 | tf_op jit(solution)/shard_map/ppermute | solution.py:54
  91.0 1.0 %dense.1 = bf16[128,256]{1,0:T(8,128)(2,1)} custom-call(f32[1,256,128]{2,1,0:T(8,128)S(1)} %get-tuple-element.58.own, bf16[1,256,128]{2,1,0:T(8,128)(2,1)S(1)} %collective-permute-done.11.part, bf16[128,256]{1,0:T(8,128)(2,1)S(1)} %copy-done, bf16[256,256]{1,0:T(8,128)(2,1)S(1)} %copy-done.3, bf16[256,256]{1,0:T(8,128)(2,1)S(1)} %copy-done.4), custom_call_target="tpu_custom_call" | custom-call | flops 5000000000 | bytes 1048576 | tf_op jit(solution)/shard_map/dense/pallas_call | solution.py:428
  92.1 0.8 last.1
  (30 shorter events, 1.3 us)
Async XLA Ops:
  2.4 20.0 %all-to-all-start = ((bf16[8,144,256]{2,1,0:T(8,128)(2,1)}), bf16[8,144,256]{2,1,0:T(8,128)(2,1)S(1)}, u32[]{:S(2)}, u32[]{:S(2)}) async-start(bf16[8,144,256]{2,1,0:T(8,128)(2,1)} %head.1), calls=%async_computation | async-start | bytes 1179648 | tf_op jit(solution)/shard_map/all_to_all | solution.py:44
  9.9 8.9 %collective-permute-start = (bf16[1,128,256]{2,1,0:T(8,128)(2,1)}, bf16[1,128,256]{2,1,0:T(8,128)(2,1)S(1)}, u32[]{:S(2)}, u32[]{:S(2)}) collective-permute-start(bf16[1,128,256]{2,1,0:T(8,128)(2,1)} %bitcast.10), channel_id=1, source_target_pairs={{0,192},{8,200},{16,208},{24,216},{32,224},{40,232},{48,240},{56,2... | collective-permute-start | bytes 196616 | tf_op jit(solution)/shard_map/ppermute | solution.py:470
  15.9 6.5 %collective-permute-start.1 = (bf16[1,128,256]{2,1,0:T(8,128)(2,1)}, bf16[1,128,256]{2,1,0:T(8,128)(2,1)S(1)}, u32[]{:S(2)}, u32[]{:S(2)}) collective-permute-start(bf16[1,128,256]{2,1,0:T(8,128)(2,1)} %bitcast.11), channel_id=1, source_target_pairs={{0,64},{8,72},{16,80},{24,88},{32,96},{40,104},{48,112},{56,120},{... | collective-permute-start | bytes 196616 | tf_op jit(solution)/shard_map/ppermute | solution.py:470
  18.8 8.1 %collective-permute-start.3 = (bf16[1,128,256]{2,1,0:T(8,128)(2,1)S(1)}, bf16[1,128,256]{2,1,0:T(8,128)(2,1)S(1)}, u32[]{:S(2)}, u32[]{:S(2)}) collective-permute-start(bf16[1,128,256]{2,1,0:T(8,128)(2,1)S(1)} %collective-permute-done.refs_1_), channel_id=1, source_target_pairs={{0,192},{8,200},{16,208},{24,216},{32,224},{40,232},{48,240},{56,2... | collective-permute-start | bytes 196616 | tf_op jit(solution)/shard_map/ppermute | solution.py:470
  22.4 0.7 copy-start.5
  23.1 7.1 %copy-start.1 = (bf16[1,128,256]{2,1,0:T(8,128)(2,1)S(1)}, bf16[1,128,256]{2,1,0:T(8,128)(2,1)}, u32[]{:S(2)}) copy-start(bf16[1,128,256]{2,1,0:T(8,128)(2,1)} %get-tuple-element.38.refs_0_) | copy-start | bytes 196612
  23.1 19.5 %copy-start.2 = (f32[256,256]{1,0:T(8,128)S(1)}, f32[256,256]{1,0:T(8,128)}, u32[]{:S(2)}) copy-start(f32[256,256]{1,0:T(8,128)} %get-tuple-element.50.own_self) | copy-start | bytes 786436
  26.9 5.7 %copy-start.6 = (f32[8,256,128]{2,1,0:T(8,128)}, f32[8,256,128]{2,1,0:T(8,128)S(1)}, u32[]{:S(2)}) copy-start(f32[8,256,128]{2,1,0:T(8,128)S(1)} %get-tuple-element.36.near) | copy-start | bytes 3145732
  26.9 4.7 %collective-permute-start.5 = (bf16[2,8,128,128]{3,2,1,0:T(8,128)(2,1)S(1)}, bf16[2,8,128,128]{3,2,1,0:T(8,128)(2,1)S(1)}, u32[]{:S(2)}, u32[]{:S(2)}) collective-permute-start(bf16[2,8,128,128]{3,2,1,0:T(8,128)(2,1)S(1)} %get-tuple-element.46), channel_id=1, source_target_pairs={{0,8},{8,0},{16,24},{24,16},{32,40},{40,32},{48,56},{56,48},{64,72... | collective-permute-start | bytes 1572872 | tf_op jit(solution)/shard_map/ppermute | solution.py:54
  30.1 7.7 %collective-permute-start.2 = (bf16[8,256,128]{2,1,0:T(8,128)(2,1)S(1)}, bf16[8,256,128]{2,1,0:T(8,128)(2,1)S(1)}, u32[]{:S(2)}, u32[]{:S(2)}) collective-permute-start(bf16[8,256,128]{2,1,0:T(8,128)(2,1)S(1)} %get-tuple-element.37), channel_id=1, source_target_pairs={{0,8},{8,0},{16,24},{24,16},{32,40},{40,32},{48,56},{56,48},{64,72... | collective-permute-start | bytes 1572872 | tf_op jit(solution)/shard_map/ppermute | solution.py:54
  30.2 7.6 %collective-permute-start.4 = (bf16[4,128,256]{2,1,0:T(8,128)(2,1)S(1)}, bf16[4,128,256]{2,1,0:T(8,128)(2,1)S(1)}, u32[]{:S(2)}, u32[]{:S(2)}) collective-permute-start(bf16[4,128,256]{2,1,0:T(8,128)(2,1)S(1)} %join.1.feats_low), channel_id=1, source_target_pairs={{0,16},{8,24},{16,0},{24,8},{32,48},{40,56},{48,32},{56,40},{64,80... | collective-permute-start | bytes 786440 | tf_op jit(solution)/shard_map/ppermute | solution.py:483
  31.6 59.4 %copy-start = (bf16[128,256]{1,0:T(8,128)(2,1)S(1)}, bf16[128,256]{1,0:T(8,128)(2,1)}, u32[]{:S(2)}) copy-start(bf16[128,256]{1,0:T(8,128)(2,1)} %grads.3) | copy-start | bytes 196612
  31.6 59.4 %copy-start.3 = (bf16[256,256]{1,0:T(8,128)(2,1)S(1)}, bf16[256,256]{1,0:T(8,128)(2,1)}, u32[]{:S(2)}) copy-start(bf16[256,256]{1,0:T(8,128)(2,1)} %w_self.1) | copy-start | bytes 393220
  31.6 59.4 %copy-start.4 = (bf16[256,256]{1,0:T(8,128)(2,1)S(1)}, bf16[256,256]{1,0:T(8,128)(2,1)}, u32[]{:S(2)}) copy-start(bf16[256,256]{1,0:T(8,128)(2,1)} %w_neigh.1) | copy-start | bytes 393220
  31.7 7.7 %collective-permute-start.6 = (bf16[8,128,128]{2,1,0:T(8,128)(2,1)S(1)}, bf16[8,128,128]{2,1,0:T(8,128)(2,1)S(1)}, u32[]{:S(2)}, u32[]{:S(2)}) collective-permute-start(bf16[8,128,128]{2,1,0:T(8,128)(2,1)S(1)} %get-tuple-element.47), channel_id=1, source_target_pairs={{0,32},{8,40},{16,48},{24,56},{32,0},{40,8},{48,16},{56,24},{64,96... | collective-permute-start | bytes 786440 | tf_op jit(solution)/shard_map/ppermute | solution.py:465
  32.6 10.0 %collective-permute-start.7 = (bf16[8,128,128]{2,1,0:T(8,128)(2,1)S(1)}, bf16[8,128,128]{2,1,0:T(8,128)(2,1)S(1)}, u32[]{:S(2)}, u32[]{:S(2)}) collective-permute-start(bf16[8,128,128]{2,1,0:T(8,128)(2,1)S(1)} %get-tuple-element.48), channel_id=1, source_target_pairs={{0,224},{8,232},{16,240},{24,248},{32,64},{40,72},{48,80},{56,88},... | collective-permute-start | bytes 786440 | tf_op jit(solution)/shard_map/ppermute | solution.py:479
  37.8 1.2 %copy-start.7 = (f32[8,256,128]{2,1,0:T(8,128)S(1)}, f32[8,256,128]{2,1,0:T(8,128)}, u32[]{:S(2)}) copy-start(f32[8,256,128]{2,1,0:T(8,128)} %copy-done.6) | copy-start | bytes 3145732
  43.0 2.4 %collective-permute-start.8 = (f32[256,256]{1,0:T(8,128)S(1)}, f32[256,256]{1,0:T(8,128)S(1)}, u32[]{:S(2)}, u32[]{:S(2)}) collective-permute-start(f32[256,256]{1,0:T(8,128)S(1)} %get-tuple-element.52), channel_id=1, source_target_pairs={{0,8},{8,0},{16,24},{24,16},{32,40},{40,32},{48,56},{56,48},{64,72... | collective-permute-start | bytes 786440 | tf_op jit(solution)/shard_map/ppermute | solution.py:54
  44.3 14.6 %collective-permute-start.9 = (bf16[4,256,128]{2,1,0:T(8,128)(2,1)S(1)}, bf16[4,256,128]{2,1,0:T(8,128)(2,1)S(1)}, u32[]{:S(2)}, u32[]{:S(2)}) collective-permute-start(bf16[4,256,128]{2,1,0:T(8,128)(2,1)S(1)} %get-tuple-element.54), channel_id=1, source_target_pairs={{0,64},{8,72},{16,80},{24,88},{32,96},{40,104},{48,112},{56,120},{... | collective-permute-start | bytes 786440 | tf_op jit(solution)/shard_map/ppermute | solution.py:465
  46.2 16.0 %all-to-all-start.1 = ((f32[16,16,256]{2,1,0:T(8,128)}), f32[16,16,256]{2,1,0:T(8,128)S(1)}, u32[]{:S(2)}, u32[]{:S(2)}) async-start(f32[16,16,256]{2,1,0:T(8,128)} %bitcast.6), calls=%async_computation.1 | async-start | bytes 524288 | tf_op jit(solution)/shard_map/all_to_all | solution.py:44
  62.9 11.3 %all-to-all-start.2 = ((f32[8,16,256]{2,1,0:T(8,128)}), f32[8,16,256]{2,1,0:T(8,128)S(1)}, u32[]{:S(2)}, u32[]{:S(2)}) async-start(f32[8,16,256]{2,1,0:T(8,128)} %get-tuple-element.55), calls=%async_computation.2 | async-start | bytes 262144 | tf_op jit(solution)/shard_map/all_to_all | solution.py:44
  66.3 3.9 %collective-permute-start.10 = (bf16[2,256,128]{2,1,0:T(8,128)(2,1)S(1)}, bf16[2,256,128]{2,1,0:T(8,128)(2,1)S(1)}, u32[]{:S(2)}, u32[]{:S(2)}) collective-permute-start(bf16[2,256,128]{2,1,0:T(8,128)(2,1)S(1)} %get-tuple-element.57), channel_id=1, source_target_pairs={{0,16},{8,24},{16,0},{24,8},{32,48},{40,56},{48,32},{56,40},{64,80... | collective-permute-start | bytes 393224 | tf_op jit(solution)/shard_map/ppermute | solution.py:483
  75.0 12.8 %all-to-all-start.3 = ((f32[16,16,256]{2,1,0:T(8,128)}), f32[16,16,256]{2,1,0:T(8,128)S(1)}, u32[]{:S(2)}, u32[]{:S(2)}) async-start(f32[16,16,256]{2,1,0:T(8,128)} %get-tuple-element.60), calls=%async_computation.3 | async-start | bytes 524288 | tf_op jit(solution)/shard_map/all_to_all | solution.py:44
  80.4 10.6 %collective-permute-start.11 = (bf16[1,256,128]{2,1,0:T(8,128)(2,1)S(1)}, bf16[1,256,128]{2,1,0:T(8,128)(2,1)S(1)}, u32[]{:S(2)}, u32[]{:S(2)}) collective-permute-start(bf16[1,256,128]{2,1,0:T(8,128)(2,1)S(1)} %get-tuple-element.59), channel_id=1, source_target_pairs={{0,128},{8,136},{16,144},{24,152},{32,160},{40,168},{48,176},{56,1... | collective-permute-start | bytes 196616 | tf_op jit(solution)/shard_map/ppermute | solution.py:465
  87.8 4.3 %collective-permute-start.12 = (f32[256,256]{1,0:T(8,128)S(1)}, f32[256,256]{1,0:T(8,128)S(1)}, u32[]{:S(2)}, u32[]{:S(2)}) collective-permute-start(f32[256,256]{1,0:T(8,128)S(1)} %bitcast.8), channel_id=1, source_target_pairs={{0,8},{8,0},{16,24},{24,16},{32,40},{40,32},{48,56},{56,48},{64,72... | collective-permute-start | bytes 786440 | tf_op jit(solution)/shard_map/ppermute | solution.py:54

commit v5 on v4

--- a/solution.py
+++ b/solution.py
@@ -93,20 +93,25 @@
     )(grads, degrees[None])
 
 
-def prep_kernel(counts, row, *refs):
-    sources, (plan, own_self, own), (rows, cols, grads), sems = refs[:4], refs[4:7], refs[7:10], refs[10]
-    feats = own.at[0]
-    copies = [
-        pltpu.make_async_copy(source, target, sems.at[k])
-        for k, (source, target) in enumerate(zip(sources, (rows, cols, feats, grads)))
-    ]
-    for copy in copies:
-        copy.start()
-    for copy in copies:
-        copy.wait()
+def self_kernel(feats, grads, own_self):
     own_self[...] = lax.dot_general(
-        feats[...], grads[...], (((0,), (0,)), ((), ())), preferred_element_type=jnp.float32
+        feats[0], grads[...], (((0,), (0,)), ((), ())), preferred_element_type=jnp.float32
     )
+
+
+def self_part(feats, grads):
+    return pl.pallas_call(
+        self_kernel,
+        in_specs=[VMEM, VMEM],
+        out_specs=VMEM,
+        out_shape=jax.ShapeDtypeStruct((256, 256), jnp.float32),
+        compiler_params=params(4),
+        name="self",
+    )(feats, grads)
+
+
+def prep_kernel(counts, row, rows, cols, feats, plan, own):
+    own[0] = feats[...]
     live = counts[0]
     slots = rows.shape[1]
     slot = lax.broadcasted_iota(jnp.int32, (1, slots), 1)
@@ -157,26 +162,19 @@
     plan[7:8, :] = jnp.full((1, 128), (live + CHUNK - 1) >> 4, jnp.int32)
 
 
-def prep(counts, row, rows, cols, feats, grads):
+def prep(counts, row, rows, cols, feats):
     return pl.pallas_call(
         prep_kernel,
-        in_specs=[SMEM, SMEM, ANY, ANY, ANY, ANY],
-        out_specs=[VMEM, VMEM, VMEM],
+        in_specs=[SMEM, SMEM, VMEM, VMEM, VMEM],
+        out_specs=[VMEM, VMEM],
         out_shape=[
             jax.ShapeDtypeStruct((8, 128), jnp.int32),
-            jax.ShapeDtypeStruct((256, 256), jnp.float32),
             jax.ShapeDtypeStruct((1, 128, 256), jnp.bfloat16),
         ],
-        scratch_shapes=[
-            pltpu.VMEM(rows.shape, jnp.int32),
-            pltpu.VMEM(cols.shape, jnp.int32),
-            pltpu.VMEM(grads.shape, jnp.bfloat16),
-            pltpu.SemaphoreType.DMA((4,)),
-        ],
-        compiler_params=params(60),
+        compiler_params=params(10),
         cost_estimate=pl.CostEstimate(flops=0, bytes_accessed=4 * MIB, transcendentals=0),
         name="prep",
-    )(counts, row[None], rows, cols, feats, grads)
+    )(counts, row[None], rows, cols, feats)
 
 
 def join_kernel(*refs):
@@ -218,11 +216,8 @@
         lhs[k, :, 128:256] = low
     lhs[ZERO_ROW] = jnp.zeros((256, 256), jnp.bfloat16)
 
-    def clear(k, carry):
+    for k in range(32):
         acc[k] = jnp.zeros((256, 128), jnp.float32)
-        return carry
-
-    lax.fori_loop(0, 33, clear, 0)
 
     def pairs(step, waited):
         need = waited
@@ -436,8 +431,9 @@
     )(own, part, grads, w_self, w_neigh)
 
 
-def last_kernel(core, full, other, grad_self, grad_neigh):
+def last_kernel(core, full, other, done_x, grad_self, grad_neigh, grad_x):
     first = core[0] == 0
+    grad_x[...] = done_x[...]
 
     @pl.when(first)
     def _():
@@ -450,15 +446,19 @@
         grad_neigh[...] = full[...]
 
 
-def last(core, full, other):
+def last(core, full, other, done_x):
     return pl.pallas_call(
         last_kernel,
-        in_specs=[SMEM] + [VMEM] * 2,
-        out_specs=[VMEM] * 2,
-        out_shape=[jax.ShapeDtypeStruct((256, 256), jnp.float32)] * 2,
+        in_specs=[SMEM] + [VMEM] * 3,
+        out_specs=[VMEM] * 3,
+        out_shape=[
+            jax.ShapeDtypeStruct((256, 256), jnp.float32),
+            jax.ShapeDtypeStruct((256, 256), jnp.float32),
+            jax.ShapeDtypeStruct((128, 256), jnp.bfloat16),
+        ],
         compiler_params=params(8),
         name="last",
-    )(core[None], full, other)
+    )(core[None], full, other, done_x)
 
 
 def swap_z(value, distance):
@@ -488,18 +488,19 @@
     core = row & 1
     node_total = 128 * 256
     group = exchange(head(grad_out, degrees), ("xh", "y"))
-    plan, own_self, own = prep(tile_counts, row, tile_rows, tile_cols, features, grad_out)
+    plan, own = prep(tile_counts, row, tile_rows, tile_cols, features)
     z = row >> 2
     above, below = shift_z(features[None], 6), shift_z(features[None], 2)
     opposite = shift_z(above, 6)
     group, above, below, plan = lax.optimization_barrier((group, above, below, plan))
     near, away_a, away_b, near_out, away_out = sparse_product(plan, z, group, tiles[0])
-    away_out, opposite = lax.optimization_barrier((away_out, opposite))
+    away_out, opposite, late = lax.optimization_barrier((away_out, opposite, grad_out))
     feats = join(own, above, opposite, below)
     away_a, away_b = mid_part(away_a, away_b, swap_core(away_out))
     core_part = swap_core(near_out)
     part_a, part_b = swap_z(away_a, 1), swap_z_other(away_b)
     feats_x = swap_x(feats)
+    own_self = self_part(own, late)
     base, total_t = base_part(z, near, core_part, feats, feats_x)
     keep, send, kept, sent = neigh_part(core, z, base, part_a, part_b, feats, feats_x, total_t, own_self)
     kept = kept + swap_core(sent)
@@ -513,7 +514,7 @@
     full = exchange(pieces, ("xh", "xl", "y")).reshape(256, 256)
     other = swap_core(full)
     grad_x = dense(keep, got, grad_out, w_self, w_neigh)
-    grad_self, grad_neigh = last(core, full, other)
+    grad_self, grad_neigh, grad_x = last(core, full, other, grad_x)
     return grad_x, grad_self, grad_neigh
 
 

time: 92.8 us -> 93.2 us (level); the launches traced: 93 us -> 91.8 us
  starting transfers between devices: 49.7 us -> 42.8 us
  Pallas kernels: 11.9 us -> 15.1 us
  local copies, waits for them, and re-layouts: 1.93 us -> 3.43 us
  waiting for transfers between devices: 27.2 us -> 28.3 us
    pallas_call x1, Pallas kernels: 3.75 us -> 9.07 us  [sparse_product(): pl.pallas_call(sparse_kernel, in_specs=[SMEM, SMEM, VMEM, ANY], out_specs...]
    all_to_all x4, starting transfers between devices: 24.8 us -> 22.2 us  [exchange(): lax.all_to_all(blocks, ('row', 'blk'), 0, 0, axis_index_groups=groups_of(...]
    ppermute x4, starting transfers between devices: 7.72 us -> 5.36 us  [swap_core(): return lax.ppermute(value, 'row', [(row, row ^ 1) for row in range(32)])]
    ppermute x1, starting transfers between devices: 3.98 us -> 2.14 us  [swap_z_other(): return lax.ppermute(value, 'row', pairs)]
    ppermute x1, waiting for transfers between devices: 3.17 us -> 1.42 us  [swap_z_other(): return lax.ppermute(value, 'row', pairs)]
    ppermute x4, waiting for transfers between devices: 1.71 us -> 3.26 us  [swap_core(): return lax.ppermute(value, 'row', [(row, row ^ 1) for row in range(32)])]
    unnamed x16, local copies, waits for them, and re-layouts: 1.93 us -> 3.43 us
    pallas_call x2 -> x3, Pallas kernels: 3.01 us -> 1.57 us  [the longest x1 0.84 us: last(): pl.pallas_call(last_kernel, in_specs=[SMEM] + [VMEM] * 3, out_specs=[VMEM...]
  transfers between devices with their start and end apart: 17 -> 17, of which waited for: 10 -> 10; matrix products, arithmetic and copies ran while one was open for 1% -> 1% of each run, Pallas kernels for 8% -> 12%
where the time goes in v5:
time: 93.2 us; the launch traced here: 91.8 us
  starting transfers between devices  42.8 us (46%)
  waiting for transfers between devices  28.3 us (30%)
  Pallas kernels  15.1 us (16%)
  local copies, waits for them, and re-layouts  3.43 us (4%)
  between operations  1.43 us (2%)
    all_to_all x4, starting transfers between devices, exchange(): lax.all_to_all(blocks, ('row', 'blk'), 0, 0, axis_index_groups=groups_of(...  22.2 us
    all_to_all x4, waiting for transfers between devices, exchange(): lax.all_to_all(blocks, ('row', 'blk'), 0, 0, axis_index_groups=groups_of(...  11.8 us
    ppermute x3, starting transfers between devices, shift_z(): return lax.ppermute(value, 'row', pairs)  9.65 us
    pallas_call x1, Pallas kernels, sparse_product(): pl.pallas_call(sparse_kernel, in_specs=[SMEM, SMEM, VMEM, ANY], out_specs...  9.07 us
    ppermute x2, waiting for transfers between devices, swap_x(): return lax.ppermute(value, 'row', [(row, row ^ 2) for row in range(32)])  6.27 us
    ppermute x3, waiting for transfers between devices, swap_z(): lax.ppermute(value, 'row', [(row, row ^ 4 * distance) for row in range(32)])  5.55 us
    ppermute x4, starting transfers between devices, swap_core(): return lax.ppermute(value, 'row', [(row, row ^ 1) for row in range(32)])  5.36 us
    unnamed x16, local copies, waits for them, and re-layouts  3.43 us
  transfers between devices with their start and end apart: 17, of which 10 were waited for; matrix products, arithmetic and copies ran while one was open for 1% of the time, Pallas kernels for 12%

profile of v5, /device:TPU:1, one launch (start us, length us, event | category | flops | bytes accessed | tf_op | source)
XLA Modules:
  0.0 91.8 jit_solution(6819853451755238212)
XLA Ops:
  0.6 1.8 %head.1 = bf16[8,144,256]{2,1,0:T(8,128)(2,1)} custom-call(bf16[128,256]{1,0:T(8,128)(2,1)} %grads.4, s32[1,128]{1,0:T(1,128)} %bitcast.12), custom_call_target="tpu_custom_call" | custom-call | tf_op jit(solution)/shard_map/head/pallas_call | solution.py:81
  2.4 7.5 %all-to-all-start = ((bf16[8,144,256]{2,1,0:T(8,128)(2,1)}), bf16[8,144,256]{2,1,0:T(8,128)(2,1)S(1)}, u32[]{:S(2)}, u32[]{:S(2)}) async-start(bf16[8,144,256]{2,1,0:T(8,128)(2,1)} %head.1), calls=%async_computation | async-start | bytes 1179648 | tf_op jit(solution)/shard_map/all_to_all | solution.py:44
  9.9 6.0 %collective-permute-start = (bf16[1,128,256]{2,1,0:T(8,128)(2,1)}, bf16[1,128,256]{2,1,0:T(8,128)(2,1)S(1)}, u32[]{:S(2)}, u32[]{:S(2)}) collective-permute-start(bf16[1,128,256]{2,1,0:T(8,128)(2,1)} %bitcast.10), channel_id=1, source_target_pairs={{0,192},{8,200},{16,208},{24,216},{32,224},{40,232},{48,240},{56,2... | collective-permute-start | bytes 196616 | tf_op jit(solution)/shard_map/ppermute | solution.py:470
  16.6 0.8 copy-done.1
  17.4 0.7 copy-done.2
  18.1 0.7 copy-done.3
  19.3 3.6 %collective-permute-start.3 = (bf16[1,128,256]{2,1,0:T(8,128)(2,1)S(1)}, bf16[1,128,256]{2,1,0:T(8,128)(2,1)S(1)}, u32[]{:S(2)}, u32[]{:S(2)}) collective-permute-start(bf16[1,128,256]{2,1,0:T(8,128)(2,1)S(1)} %collective-permute-done.refs_1_), channel_id=1, source_target_pairs={{0,192},{8,200},{16,208},{24,216},{32,224},{40,232},{48,240},{56,2... | collective-permute-start | bytes 196616 | tf_op jit(solution)/shard_map/ppermute | solution.py:470
  22.9 9.1 %sparse.1 = (f32[8,256,128]{2,1,0:T(8,128)S(1)}, f32[8,128,128]{2,1,0:T(8,128)S(1)}, f32[8,128,128]{2,1,0:T(8,128)S(1)}, bf16[8,256,128]{2,1,0:T(8,128)(2,1)S(1)}, bf16[2,8,128,128]{3,2,1,0:T(8,128)(2,1)S(1)}) custom-call(s32[8,128]{1,0:T(8,128)S(1)} %get-tuple-element.35.plan, s32[1]{0:T(128)} %bitcast.1.z, bf16[8,144,256]{2,1,0:T(8,128)(2,1)S(1)} %all-to-all-done.grads, ...), custom_call_target="tpu_custom_call" | custom-call | flops 4000000000 | bytes 12582912 | tf_op jit(solution)/shard_map/sparse/pallas_call | solution.py:257
  32.8 1.3 %collective-permute-done.5.part = bf16[2,8,128,128]{3,2,1,0:T(8,128)(2,1)S(1)} collective-permute-done((bf16[2,8,128,128]{3,2,1,0:T(8,128)(2,1)S(1)}, bf16[2,8,128,128]{3,2,1,0:T(8,128)(2,1)S(1)}, u32[]{:S(2)}, u32[]{:S(2)}) %collective-permute-start.5) | collective-permute-done | bytes 524320 | tf_op jit(solution)/shard_map/ppermute | solution.py:54
  34.1 1.2 %collective-permute-start.6 = (bf16[8,128,128]{2,1,0:T(8,128)(2,1)S(1)}, bf16[8,128,128]{2,1,0:T(8,128)(2,1)S(1)}, u32[]{:S(2)}, u32[]{:S(2)}) collective-permute-start(bf16[8,128,128]{2,1,0:T(8,128)(2,1)S(1)} %get-tuple-element.48), channel_id=1, source_target_pairs={{0,32},{8,40},{16,48},{24,56},{32,0},{40,8},{48,16},{56,24},{64,96... | collective-permute-start | bytes 786440 | tf_op jit(solution)/shard_map/ppermute | solution.py:465
  35.3 2.1 %collective-permute-start.7 = (bf16[8,128,128]{2,1,0:T(8,128)(2,1)S(1)}, bf16[8,128,128]{2,1,0:T(8,128)(2,1)S(1)}, u32[]{:S(2)}, u32[]{:S(2)}) collective-permute-start(bf16[8,128,128]{2,1,0:T(8,128)(2,1)S(1)} %get-tuple-element.49), channel_id=1, source_target_pairs={{0,224},{8,232},{16,240},{24,248},{32,64},{40,72},{48,80},{56,88},... | collective-permute-start | bytes 786440 | tf_op jit(solution)/shard_map/ppermute | solution.py:479
  37.7 3.0 %collective-permute-done.4.feats_high = bf16[4,128,256]{2,1,0:T(8,128)(2,1)S(1)} collective-permute-done((bf16[4,128,256]{2,1,0:T(8,128)(2,1)S(1)}, bf16[4,128,256]{2,1,0:T(8,128)(2,1)S(1)}, u32[]{:S(2)}, u32[]{:S(2)}) %collective-permute-start.4) | collective-permute-done | bytes 262176 | tf_op jit(solution)/shard_map/ppermute | solution.py:483
  40.6 1.2 %copy-done.7 = f32[8,256,128]{2,1,0:T(8,128)S(1)} copy-done((f32[8,256,128]{2,1,0:T(8,128)S(1)}, f32[8,256,128]{2,1,0:T(8,128)}, u32[]{:S(2)}) %copy-start.7) | copy-done | bytes 1048600
  42.3 1.4 %collective-permute-done.7.part_b = bf16[8,128,128]{2,1,0:T(8,128)(2,1)S(1)} collective-permute-done((bf16[8,128,128]{2,1,0:T(8,128)(2,1)S(1)}, bf16[8,128,128]{2,1,0:T(8,128)(2,1)S(1)}, u32[]{:S(2)}, u32[]{:S(2)}) %collective-permute-start.7) | collective-permute-done | bytes 262176 | tf_op jit(solution)/shard_map/ppermute | solution.py:479
  44.1 1.6 %collective-permute-start.8 = (f32[256,256]{1,0:T(8,128)S(1)}, f32[256,256]{1,0:T(8,128)S(1)}, u32[]{:S(2)}, u32[]{:S(2)}) collective-permute-start(f32[256,256]{1,0:T(8,128)S(1)} %get-tuple-element.53), channel_id=1, source_target_pairs={{0,8},{8,0},{16,24},{24,16},{32,40},{40,32},{48,56},{56,48},{64,72... | collective-permute-start | bytes 786440 | tf_op jit(solution)/shard_map/ppermute | solution.py:54
  45.7 1.2 %collective-permute-done.8 = f32[256,256]{1,0:T(8,128)S(1)} collective-permute-done((f32[256,256]{1,0:T(8,128)S(1)}, f32[256,256]{1,0:T(8,128)S(1)}, u32[]{:S(2)}, u32[]{:S(2)}) %collective-permute-start.8) | collective-permute-done | bytes 262176 | tf_op jit(solution)/shard_map/ppermute | solution.py:54
  46.9 0.7 add.3
  47.6 6.2 %all-to-all-start.1 = ((f32[16,16,256]{2,1,0:T(8,128)}), f32[16,16,256]{2,1,0:T(8,128)S(1)}, u32[]{:S(2)}, u32[]{:S(2)}) async-start(f32[16,16,256]{2,1,0:T(8,128)} %bitcast.6), calls=%async_computation.1 | async-start | bytes 524288 | tf_op jit(solution)/shard_map/all_to_all | solution.py:44
  53.9 5.5 %collective-permute-done.9.got = bf16[4,256,128]{2,1,0:T(8,128)(2,1)S(1)} collective-permute-done((bf16[4,256,128]{2,1,0:T(8,128)(2,1)S(1)}, bf16[4,256,128]{2,1,0:T(8,128)(2,1)S(1)}, u32[]{:S(2)}, u32[]{:S(2)}) %collective-permute-start.9) | collective-permute-done | bytes 262176 | tf_op jit(solution)/shard_map/ppermute | solution.py:465
  59.4 2.0 %all-to-all-done.1.pieces = f32[16,16,256]{2,1,0:T(8,128)S(1)} async-done(((f32[16,16,256]{2,1,0:T(8,128)}), f32[16,16,256]{2,1,0:T(8,128)S(1)}, u32[]{:S(2)}, u32[]{:S(2)}) %all-to-all-start.1) | async-done | bytes 262176 | tf_op jit(solution)/shard_map/all_to_all | solution.py:44
  61.4 0.7 fold.2
  62.1 3.4 %all-to-all-start.2 = ((f32[8,16,256]{2,1,0:T(8,128)}), f32[8,16,256]{2,1,0:T(8,128)S(1)}, u32[]{:S(2)}, u32[]{:S(2)}) async-start(f32[8,16,256]{2,1,0:T(8,128)} %get-tuple-element.56), calls=%async_computation.2 | async-start | bytes 262144 | tf_op jit(solution)/shard_map/all_to_all | solution.py:44
  65.5 0.6 collective-permute-start.10
  66.1 3.3 %collective-permute-done.10.got = bf16[2,256,128]{2,1,0:T(8,128)(2,1)S(1)} collective-permute-done((bf16[2,256,128]{2,1,0:T(8,128)(2,1)S(1)}, bf16[2,256,128]{2,1,0:T(8,128)(2,1)S(1)}, u32[]{:S(2)}, u32[]{:S(2)}) %collective-permute-start.10) | collective-permute-done | bytes 131104 | tf_op jit(solution)/shard_map/ppermute | solution.py:483
  69.4 4.0 %all-to-all-done.2.pieces = f32[8,16,256]{2,1,0:T(8,128)S(1)} async-done(((f32[8,16,256]{2,1,0:T(8,128)}), f32[8,16,256]{2,1,0:T(8,128)S(1)}, u32[]{:S(2)}, u32[]{:S(2)}) %all-to-all-start.2) | async-done | bytes 131104 | tf_op jit(solution)/shard_map/all_to_all | solution.py:44
  73.4 0.7 fold.3
  74.2 5.1 %all-to-all-start.3 = ((f32[16,16,256]{2,1,0:T(8,128)}), f32[16,16,256]{2,1,0:T(8,128)S(1)}, u32[]{:S(2)}, u32[]{:S(2)}) async-start(f32[16,16,256]{2,1,0:T(8,128)} %get-tuple-element.59), calls=%async_computation.3 | async-start | bytes 524288 | tf_op jit(solution)/shard_map/all_to_all | solution.py:44
  79.3 1.6 %collective-permute-start.12 = (bf16[1,256,128]{2,1,0:T(8,128)(2,1)S(1)}, bf16[1,256,128]{2,1,0:T(8,128)(2,1)S(1)}, u32[]{:S(2)}, u32[]{:S(2)}) collective-permute-start(bf16[1,256,128]{2,1,0:T(8,128)(2,1)S(1)} %get-tuple-element.61), channel_id=1, source_target_pairs={{0,128},{8,136},{16,144},{24,152},{32,160},{40,168},{48,176},{56,1... | collective-permute-start | bytes 196616 | tf_op jit(solution)/shard_map/ppermute | solution.py:465
  80.8 5.8 %all-to-all-done.3 = f32[16,16,256]{2,1,0:T(8,128)S(1)} async-done(((f32[16,16,256]{2,1,0:T(8,128)}), f32[16,16,256]{2,1,0:T(8,128)S(1)}, u32[]{:S(2)}, u32[]{:S(2)}) %all-to-all-start.3) | async-done | bytes 262176 | tf_op jit(solution)/shard_map/all_to_all | solution.py:44
  86.6 3.2 %collective-permute-start.11 = (f32[256,256]{1,0:T(8,128)S(1)}, f32[256,256]{1,0:T(8,128)S(1)}, u32[]{:S(2)}, u32[]{:S(2)}) collective-permute-start(f32[256,256]{1,0:T(8,128)S(1)} %bitcast.8), channel_id=1, source_target_pairs={{0,8},{8,0},{16,24},{24,16},{32,40},{40,32},{48,56},{56,48},{64,72... | collective-permute-start | bytes 786440 | tf_op jit(solution)/shard_map/ppermute | solution.py:54
  90.2 0.8 collective-permute-done.11.other
  91.0 0.8 last.1
  (31 shorter events, 2.7 us)
Async XLA Ops:
  2.4 20.5 %all-to-all-start = ((bf16[8,144,256]{2,1,0:T(8,128)(2,1)}), bf16[8,144,256]{2,1,0:T(8,128)(2,1)S(1)}, u32[]{:S(2)}, u32[]{:S(2)}) async-start(bf16[8,144,256]{2,1,0:T(8,128)(2,1)} %head.1), calls=%async_computation | async-start | bytes 1179648 | tf_op jit(solution)/shard_map/all_to_all | solution.py:44
  9.9 9.4 %collective-permute-start = (bf16[1,128,256]{2,1,0:T(8,128)(2,1)}, bf16[1,128,256]{2,1,0:T(8,128)(2,1)S(1)}, u32[]{:S(2)}, u32[]{:S(2)}) collective-permute-start(bf16[1,128,256]{2,1,0:T(8,128)(2,1)} %bitcast.10), channel_id=1, source_target_pairs={{0,192},{8,200},{16,208},{24,216},{32,224},{40,232},{48,240},{56,2... | collective-permute-start | bytes 196616 | tf_op jit(solution)/shard_map/ppermute | solution.py:470
  15.9 7.0 %collective-permute-start.1 = (bf16[1,128,256]{2,1,0:T(8,128)(2,1)}, bf16[1,128,256]{2,1,0:T(8,128)(2,1)S(1)}, u32[]{:S(2)}, u32[]{:S(2)}) collective-permute-start(bf16[1,128,256]{2,1,0:T(8,128)(2,1)} %bitcast.11), channel_id=1, source_target_pairs={{0,64},{8,72},{16,80},{24,88},{32,96},{40,104},{48,112},{56,120},{... | collective-permute-start | bytes 196616 | tf_op jit(solution)/shard_map/ppermute | solution.py:470
  16.6 0.8 copy-start.1
  17.4 0.7 copy-start.2
  18.1 0.7 copy-start.3
  19.3 12.7 %collective-permute-start.3 = (bf16[1,128,256]{2,1,0:T(8,128)(2,1)S(1)}, bf16[1,128,256]{2,1,0:T(8,128)(2,1)S(1)}, u32[]{:S(2)}, u32[]{:S(2)}) collective-permute-start(bf16[1,128,256]{2,1,0:T(8,128)(2,1)S(1)} %collective-permute-done.refs_1_), channel_id=1, source_target_pairs={{0,192},{8,200},{16,208},{24,216},{32,224},{40,232},{48,240},{56,2... | collective-permute-start | bytes 196616 | tf_op jit(solution)/shard_map/ppermute | solution.py:470
  22.9 14.5 %copy-start = (bf16[128,256]{1,0:T(8,128)(2,1)S(1)}, bf16[128,256]{1,0:T(8,128)(2,1)}, u32[]{:S(2)}) copy-start(bf16[128,256]{1,0:T(8,128)(2,1)} %grads.4) | copy-start | bytes 196612
  32.0 3.3 %copy-start.6 = (f32[8,256,128]{2,1,0:T(8,128)}, f32[8,256,128]{2,1,0:T(8,128)S(1)}, u32[]{:S(2)}) copy-start(f32[8,256,128]{2,1,0:T(8,128)S(1)} %get-tuple-element.37.near) | copy-start | bytes 3145732
  32.0 2.0 %collective-permute-start.5 = (bf16[2,8,128,128]{3,2,1,0:T(8,128)(2,1)S(1)}, bf16[2,8,128,128]{3,2,1,0:T(8,128)(2,1)S(1)}, u32[]{:S(2)}, u32[]{:S(2)}) collective-permute-start(bf16[2,8,128,128]{3,2,1,0:T(8,128)(2,1)S(1)} %get-tuple-element.47), channel_id=1, source_target_pairs={{0,8},{8,0},{16,24},{24,16},{32,40},{40,32},{48,56},{56,48},{64,72... | collective-permute-start | bytes 1572872 | tf_op jit(solution)/shard_map/ppermute | solution.py:54
  32.1 8.5 %collective-permute-start.2 = (bf16[8,256,128]{2,1,0:T(8,128)(2,1)S(1)}, bf16[8,256,128]{2,1,0:T(8,128)(2,1)S(1)}, u32[]{:S(2)}, u32[]{:S(2)}) collective-permute-start(bf16[8,256,128]{2,1,0:T(8,128)(2,1)S(1)} %get-tuple-element.38), channel_id=1, source_target_pairs={{0,8},{8,0},{16,24},{24,16},{32,40},{40,32},{48,56},{56,48},{64,72... | collective-permute-start | bytes 1572872 | tf_op jit(solution)/shard_map/ppermute | solution.py:54
  32.7 8.0 %collective-permute-start.4 = (bf16[4,128,256]{2,1,0:T(8,128)(2,1)S(1)}, bf16[4,128,256]{2,1,0:T(8,128)(2,1)S(1)}, u32[]{:S(2)}, u32[]{:S(2)}) collective-permute-start(bf16[4,128,256]{2,1,0:T(8,128)(2,1)S(1)} %join.1.feats_low), channel_id=1, source_target_pairs={{0,16},{8,24},{16,0},{24,8},{32,48},{40,56},{48,32},{56,40},{64,80... | collective-permute-start | bytes 786440 | tf_op jit(solution)/shard_map/ppermute | solution.py:483
  34.0 55.8 %copy-start.4 = (bf16[256,256]{1,0:T(8,128)(2,1)S(1)}, bf16[256,256]{1,0:T(8,128)(2,1)}, u32[]{:S(2)}) copy-start(bf16[256,256]{1,0:T(8,128)(2,1)} %w_self.1) | copy-start | bytes 393220
  34.0 55.8 %copy-start.5 = (bf16[256,256]{1,0:T(8,128)(2,1)S(1)}, bf16[256,256]{1,0:T(8,128)(2,1)}, u32[]{:S(2)}) copy-start(bf16[256,256]{1,0:T(8,128)(2,1)} %w_neigh.1) | copy-start | bytes 393220
  34.1 8.2 %collective-permute-start.6 = (bf16[8,128,128]{2,1,0:T(8,128)(2,1)S(1)}, bf16[8,128,128]{2,1,0:T(8,128)(2,1)S(1)}, u32[]{:S(2)}, u32[]{:S(2)}) collective-permute-start(bf16[8,128,128]{2,1,0:T(8,128)(2,1)S(1)} %get-tuple-element.48), channel_id=1, source_target_pairs={{0,32},{8,40},{16,48},{24,56},{32,0},{40,8},{48,16},{56,24},{64,96... | collective-permute-start | bytes 786440 | tf_op jit(solution)/shard_map/ppermute | solution.py:465
  35.3 8.4 %collective-permute-start.7 = (bf16[8,128,128]{2,1,0:T(8,128)(2,1)S(1)}, bf16[8,128,128]{2,1,0:T(8,128)(2,1)S(1)}, u32[]{:S(2)}, u32[]{:S(2)}) collective-permute-start(bf16[8,128,128]{2,1,0:T(8,128)(2,1)S(1)} %get-tuple-element.49), channel_id=1, source_target_pairs={{0,224},{8,232},{16,240},{24,248},{32,64},{40,72},{48,80},{56,88},... | collective-permute-start | bytes 786440 | tf_op jit(solution)/shard_map/ppermute | solution.py:479
  40.6 1.2 %copy-start.7 = (f32[8,256,128]{2,1,0:T(8,128)S(1)}, f32[8,256,128]{2,1,0:T(8,128)}, u32[]{:S(2)}) copy-start(f32[8,256,128]{2,1,0:T(8,128)} %copy-done.6) | copy-start | bytes 3145732
  44.1 2.7 %collective-permute-start.8 = (f32[256,256]{1,0:T(8,128)S(1)}, f32[256,256]{1,0:T(8,128)S(1)}, u32[]{:S(2)}, u32[]{:S(2)}) collective-permute-start(f32[256,256]{1,0:T(8,128)S(1)} %get-tuple-element.53), channel_id=1, source_target_pairs={{0,8},{8,0},{16,24},{24,16},{32,40},{40,32},{48,56},{56,48},{64,72... | collective-permute-start | bytes 786440 | tf_op jit(solution)/shard_map/ppermute | solution.py:54
  45.7 13.7 %collective-permute-start.9 = (bf16[4,256,128]{2,1,0:T(8,128)(2,1)S(1)}, bf16[4,256,128]{2,1,0:T(8,128)(2,1)S(1)}, u32[]{:S(2)}, u32[]{:S(2)}) collective-permute-start(bf16[4,256,128]{2,1,0:T(8,128)(2,1)S(1)} %get-tuple-element.55), channel_id=1, source_target_pairs={{0,64},{8,72},{16,80},{24,88},{32,96},{40,104},{48,112},{56,120},{... | collective-permute-start | bytes 786440 | tf_op jit(solution)/shard_map/ppermute | solution.py:465
  47.6 13.8 %all-to-all-start.1 = ((f32[16,16,256]{2,1,0:T(8,128)}), f32[16,16,256]{2,1,0:T(8,128)S(1)}, u32[]{:S(2)}, u32[]{:S(2)}) async-start(f32[16,16,256]{2,1,0:T(8,128)} %bitcast.6), calls=%async_computation.1 | async-start | bytes 524288 | tf_op jit(solution)/shard_map/all_to_all | solution.py:44
  62.1 11.3 %all-to-all-start.2 = ((f32[8,16,256]{2,1,0:T(8,128)}), f32[8,16,256]{2,1,0:T(8,128)S(1)}, u32[]{:S(2)}, u32[]{:S(2)}) async-start(f32[8,16,256]{2,1,0:T(8,128)} %get-tuple-element.56), calls=%async_computation.2 | async-start | bytes 262144 | tf_op jit(solution)/shard_map/all_to_all | solution.py:44
  65.5 3.9 %collective-permute-start.10 = (bf16[2,256,128]{2,1,0:T(8,128)(2,1)S(1)}, bf16[2,256,128]{2,1,0:T(8,128)(2,1)S(1)}, u32[]{:S(2)}, u32[]{:S(2)}) collective-permute-start(bf16[2,256,128]{2,1,0:T(8,128)(2,1)S(1)} %get-tuple-element.58), channel_id=1, source_target_pairs={{0,16},{8,24},{16,0},{24,8},{32,48},{40,56},{48,32},{56,40},{64,80... | collective-permute-start | bytes 393224 | tf_op jit(solution)/shard_map/ppermute | solution.py:483
  74.2 12.4 %all-to-all-start.3 = ((f32[16,16,256]{2,1,0:T(8,128)}), f32[16,16,256]{2,1,0:T(8,128)S(1)}, u32[]{:S(2)}, u32[]{:S(2)}) async-start(f32[16,16,256]{2,1,0:T(8,128)} %get-tuple-element.59), calls=%async_computation.3 | async-start | bytes 524288 | tf_op jit(solution)/shard_map/all_to_all | solution.py:44
  79.3 10.6 %collective-permute-start.12 = (bf16[1,256,128]{2,1,0:T(8,128)(2,1)S(1)}, bf16[1,256,128]{2,1,0:T(8,128)(2,1)S(1)}, u32[]{:S(2)}, u32[]{:S(2)}) collective-permute-start(bf16[1,256,128]{2,1,0:T(8,128)(2,1)S(1)} %get-tuple-element.61), channel_id=1, source_target_pairs={{0,128},{8,136},{16,144},{24,152},{32,160},{40,168},{48,176},{56,1... | collective-permute-start | bytes 196616 | tf_op jit(solution)/shard_map/ppermute | solution.py:465
  86.6 4.3 %collective-permute-start.11 = (f32[256,256]{1,0:T(8,128)S(1)}, f32[256,256]{1,0:T(8,128)S(1)}, u32[]{:S(2)}, u32[]{:S(2)}) collective-permute-start(f32[256,256]{1,0:T(8,128)S(1)} %bitcast.8), channel_id=1, source_target_pairs={{0,8},{8,0},{16,24},{24,16},{32,40},{40,32},{48,56},{56,48},{64,72... | collective-permute-start | bytes 786440 | tf_op jit(solution)/shard_map/ppermute | solution.py:54

commit v6 on v5

--- a/solution.py
+++ b/solution.py
@@ -11,7 +11,7 @@
 PARTS = {"z": 8, "xl": 2, "core": 2, "xh": 2, "y": 4}
 CHUNK = 16
 DEG_ROWS = 16
-UNROLL = 8
+LARGE, SMALL = 16, 4
 TRASH = 32
 ZERO_ROW = 8
 MIB = 1024 * 1024
@@ -157,7 +157,7 @@
     plan[2:3, :] = one[1:2] + (1 - one[3:4]) * TRASH
     plan[3:4, :] = two[1:2] + (1 - two[3:4]) * TRASH
     plan[4:5, :] = one[2:3] + (1 - one[3:4]) * ZERO_ROW
-    plan[5:6, :] = jnp.broadcast_to((total + UNROLL - 1) >> 3, (1, 128))
+    plan[5:6, :] = jnp.broadcast_to(total, (1, 128))
     plan[6:7, :] = (jnp.maximum(one[0:1], two[0:1]) >> 4) + 1
     plan[7:8, :] = jnp.full((1, 128), (live + CHUNK - 1) >> 4, jnp.int32)
 
@@ -219,13 +219,13 @@
     for k in range(32):
         acc[k] = jnp.zeros((256, 128), jnp.float32)
 
-    def pairs(step, waited):
+    def pairs(first, count, waited):
         need = waited
-        for u in range(UNROLL):
-            need = jnp.maximum(need, plan[6, step * UNROLL + u])
+        for u in range(count):
+            need = jnp.maximum(need, plan[6, first + u])
         lax.fori_loop(waited, need, wait_piece, 0)
-        for u in range(UNROLL):
-            p = step * UNROLL + u
+        for u in range(count):
+            p = first + u
             both = jnp.concatenate([held[plan[0, p]], held[plan[1, p]]], axis=1)
             product = jnp.dot(
                 lhs[plan[4, p]],
@@ -236,7 +236,16 @@
             acc[plan[3, p]] += product[:, 128:256]
         return need
 
-    waited = lax.fori_loop(0, plan[5, 0], pairs, jnp.int32(0))
+    total = plan[5, 0]
+    large = total // LARGE
+    start = large * LARGE
+    small = (total - start + SMALL - 1) // SMALL
+    waited = lax.fori_loop(
+        0, large, lambda step, waited: pairs(step * LARGE, LARGE, waited), jnp.int32(0)
+    )
+    waited = lax.fori_loop(
+        0, small, lambda step, waited: pairs(start + step * SMALL, SMALL, waited), waited
+    )
     lax.fori_loop(waited, chunks, wait_piece, 0)
 
     turn = 4 ^ (((z[0] + 1) >> 1) + 1 & 1)

time: 93.2 us -> 91.3 us (0.980)
  starting transfers between devices: 42.8 us -> 48.4 us
  Pallas kernels: 15.1 us -> 10.4 us
  waiting for transfers between devices: 28.3 us -> 26.4 us
    pallas_call x1, Pallas kernels: 9.07 us -> 4.3 us  [sparse_product(): pl.pallas_call(sparse_kernel, in_specs=[SMEM, SMEM, VMEM, ANY], out_specs...]
    ppermute x2, waiting for transfers between devices: 6.27 us -> 2.68 us  [swap_x(): return lax.ppermute(value, 'row', [(row, row ^ 2) for row in range(32)])]
    ppermute x1, waiting for transfers between devices: 1.42 us -> 3.95 us  [swap_z_other(): return lax.ppermute(value, 'row', pairs)]
    ppermute x1, starting transfers between devices: 2.14 us -> 4.27 us  [swap_z_other(): return lax.ppermute(value, 'row', pairs)]
    ppermute x2, starting transfers between devices: 0.68 us -> 2.43 us  [swap_x(): return lax.ppermute(value, 'row', [(row, row ^ 2) for row in range(32)])]
    ppermute x4, starting transfers between devices: 5.36 us -> 6.97 us  [swap_core(): return lax.ppermute(value, 'row', [(row, row ^ 1) for row in range(32)])]
    ppermute x3, starting transfers between devices: 2.75 us -> 4.02 us  [swap_z(): lax.ppermute(value, 'row', [(row, row ^ 4 * distance) for row in range(32)])]
    ppermute x4, waiting for transfers between devices: 3.26 us -> 2.11 us  [swap_core(): return lax.ppermute(value, 'row', [(row, row ^ 1) for row in range(32)])]
  transfers between devices with their start and end apart: 17 -> 17, of which waited for: 10 -> 10; matrix products, arithmetic and copies ran while one was open for 1% -> 1% of each run, Pallas kernels for 12% -> 7%
where the time goes in v6:
time: 91.3 us; the launch traced here: 90.8 us
  starting transfers between devices  48.4 us (53%)
  waiting for transfers between devices  26.4 us (29%)
  Pallas kernels  10.4 us (11%)
  local copies, waits for them, and re-layouts  3.42 us (4%)
  between operations  1.43 us (2%)
    all_to_all x4, starting transfers between devices, exchange(): lax.all_to_all(blocks, ('row', 'blk'), 0, 0, axis_index_groups=groups_of(...  21.1 us
    all_to_all x4, waiting for transfers between devices, exchange(): lax.all_to_all(blocks, ('row', 'blk'), 0, 0, axis_index_groups=groups_of(...  11.1 us
    ppermute x3, starting transfers between devices, shift_z(): return lax.ppermute(value, 'row', pairs)  9.65 us
    ppermute x4, starting transfers between devices, swap_core(): return lax.ppermute(value, 'row', [(row, row ^ 1) for row in range(32)])  6.97 us
    ppermute x3, waiting for transfers between devices, swap_z(): lax.ppermute(value, 'row', [(row, row ^ 4 * distance) for row in range(32)])  6.6 us
    pallas_call x1, Pallas kernels, sparse_product(): pl.pallas_call(sparse_kernel, in_specs=[SMEM, SMEM, VMEM, ANY], out_specs...  4.3 us
    ppermute x1, starting transfers between devices, swap_z_other(): return lax.ppermute(value, 'row', pairs)  4.27 us
    ppermute x3, starting transfers between devices, swap_z(): lax.ppermute(value, 'row', [(row, row ^ 4 * distance) for row in range(32)])  4.02 us
  transfers between devices with their start and end apart: 17, of which 10 were waited for; matrix products, arithmetic and copies ran while one was open for 1% of the time, Pallas kernels for 7%

profile of v6, /device:TPU:1, one launch (start us, length us, event | category | flops | bytes accessed | tf_op | source)
XLA Modules:
  0.0 90.8 jit_solution(7526346535893695617)
XLA Ops:
  0.6 1.8 %head.1 = bf16[8,144,256]{2,1,0:T(8,128)(2,1)} custom-call(bf16[128,256]{1,0:T(8,128)(2,1)} %grads.4, s32[1,128]{1,0:T(1,128)} %bitcast.12), custom_call_target="tpu_custom_call" | custom-call | tf_op jit(solution)/shard_map/head/pallas_call | solution.py:81
  2.4 7.5 %all-to-all-start = ((bf16[8,144,256]{2,1,0:T(8,128)(2,1)}), bf16[8,144,256]{2,1,0:T(8,128)(2,1)S(1)}, u32[]{:S(2)}, u32[]{:S(2)}) async-start(bf16[8,144,256]{2,1,0:T(8,128)(2,1)} %head.1), calls=%async_computation | async-start | bytes 1179648 | tf_op jit(solution)/shard_map/all_to_all | solution.py:44
  9.9 6.0 %collective-permute-start = (bf16[1,128,256]{2,1,0:T(8,128)(2,1)}, bf16[1,128,256]{2,1,0:T(8,128)(2,1)S(1)}, u32[]{:S(2)}, u32[]{:S(2)}) collective-permute-start(bf16[1,128,256]{2,1,0:T(8,128)(2,1)} %bitcast.10), channel_id=1, source_target_pairs={{0,192},{8,200},{16,208},{24,216},{32,224},{40,232},{48,240},{56,2... | collective-permute-start | bytes 196616 | tf_op jit(solution)/shard_map/ppermute | solution.py:479
  16.6 0.8 copy-done.1
  17.4 0.7 copy-done.2
  18.1 0.7 copy-done.3
  19.3 3.6 %collective-permute-start.3 = (bf16[1,128,256]{2,1,0:T(8,128)(2,1)S(1)}, bf16[1,128,256]{2,1,0:T(8,128)(2,1)S(1)}, u32[]{:S(2)}, u32[]{:S(2)}) collective-permute-start(bf16[1,128,256]{2,1,0:T(8,128)(2,1)S(1)} %collective-permute-done.refs_1_), channel_id=1, source_target_pairs={{0,192},{8,200},{16,208},{24,216},{32,224},{40,232},{48,240},{56,2... | collective-permute-start | bytes 196616 | tf_op jit(solution)/shard_map/ppermute | solution.py:479
  22.9 4.3 %sparse.1 = (f32[8,256,128]{2,1,0:T(8,128)S(1)}, f32[8,128,128]{2,1,0:T(8,128)S(1)}, f32[8,128,128]{2,1,0:T(8,128)S(1)}, bf16[8,256,128]{2,1,0:T(8,128)(2,1)S(1)}, bf16[2,8,128,128]{3,2,1,0:T(8,128)(2,1)S(1)}) custom-call(s32[8,128]{1,0:T(8,128)S(1)} %get-tuple-element.35.plan, s32[1]{0:T(128)} %bitcast.1.z, bf16[8,144,256]{2,1,0:T(8,128)(2,1)S(1)} %all-to-all-done.grads, ...), custom_call_target="tpu_custom_call" | custom-call | flops 4000000000 | bytes 12582912 | tf_op jit(solution)/shard_map/sparse/pallas_call | solution.py:266
  27.3 2.4 %collective-permute-start.5 = (bf16[2,8,128,128]{3,2,1,0:T(8,128)(2,1)S(1)}, bf16[2,8,128,128]{3,2,1,0:T(8,128)(2,1)S(1)}, u32[]{:S(2)}, u32[]{:S(2)}) collective-permute-start(bf16[2,8,128,128]{3,2,1,0:T(8,128)(2,1)S(1)} %get-tuple-element.47), channel_id=1, source_target_pairs={{0,8},{8,0},{16,24},{24,16},{32,40},{40,32},{48,56},{56,48},{64,72... | collective-permute-start | bytes 1572872 | tf_op jit(solution)/shard_map/ppermute | solution.py:54
  29.8 1.3 %collective-permute-start.4 = (bf16[4,128,256]{2,1,0:T(8,128)(2,1)S(1)}, bf16[4,128,256]{2,1,0:T(8,128)(2,1)S(1)}, u32[]{:S(2)}, u32[]{:S(2)}) collective-permute-start(bf16[4,128,256]{2,1,0:T(8,128)(2,1)S(1)} %join.1.feats_low), channel_id=1, source_target_pairs={{0,16},{8,24},{16,0},{24,8},{32,48},{40,56},{48,32},{56,40},{64,80... | collective-permute-start | bytes 786440 | tf_op jit(solution)/shard_map/ppermute | solution.py:492
  31.3 2.5 %collective-permute-start.6 = (bf16[8,128,128]{2,1,0:T(8,128)(2,1)S(1)}, bf16[8,128,128]{2,1,0:T(8,128)(2,1)S(1)}, u32[]{:S(2)}, u32[]{:S(2)}) collective-permute-start(bf16[8,128,128]{2,1,0:T(8,128)(2,1)S(1)} %get-tuple-element.48), channel_id=1, source_target_pairs={{0,32},{8,40},{16,48},{24,56},{32,0},{40,8},{48,16},{56,24},{64,96... | collective-permute-start | bytes 786440 | tf_op jit(solution)/shard_map/ppermute | solution.py:474
  33.8 4.3 %collective-permute-start.7 = (bf16[8,128,128]{2,1,0:T(8,128)(2,1)S(1)}, bf16[8,128,128]{2,1,0:T(8,128)(2,1)S(1)}, u32[]{:S(2)}, u32[]{:S(2)}) collective-permute-start(bf16[8,128,128]{2,1,0:T(8,128)(2,1)S(1)} %get-tuple-element.49), channel_id=1, source_target_pairs={{0,224},{8,232},{16,240},{24,248},{32,64},{40,72},{48,80},{56,88},... | collective-permute-start | bytes 786440 | tf_op jit(solution)/shard_map/ppermute | solution.py:488
  38.3 1.2 %copy-done.7 = f32[8,256,128]{2,1,0:T(8,128)S(1)} copy-done((f32[8,256,128]{2,1,0:T(8,128)S(1)}, f32[8,256,128]{2,1,0:T(8,128)}, u32[]{:S(2)}) %copy-start.7) | copy-done | bytes 1048600
  40.2 4.0 %collective-permute-done.7.part_b = bf16[8,128,128]{2,1,0:T(8,128)(2,1)S(1)} collective-permute-done((bf16[8,128,128]{2,1,0:T(8,128)(2,1)S(1)}, bf16[8,128,128]{2,1,0:T(8,128)(2,1)S(1)}, u32[]{:S(2)}, u32[]{:S(2)}) %collective-permute-start.7) | collective-permute-done | bytes 262176 | tf_op jit(solution)/shard_map/ppermute | solution.py:488
  44.5 1.3 %collective-permute-start.8 = (f32[256,256]{1,0:T(8,128)S(1)}, f32[256,256]{1,0:T(8,128)S(1)}, u32[]{:S(2)}, u32[]{:S(2)}) collective-permute-start(f32[256,256]{1,0:T(8,128)S(1)} %get-tuple-element.53), channel_id=1, source_target_pairs={{0,8},{8,0},{16,24},{24,16},{32,40},{40,32},{48,56},{56,48},{64,72... | collective-permute-start | bytes 786440 | tf_op jit(solution)/shard_map/ppermute | solution.py:54
  45.8 1.2 %collective-permute-done.8 = f32[256,256]{1,0:T(8,128)S(1)} collective-permute-done((f32[256,256]{1,0:T(8,128)S(1)}, f32[256,256]{1,0:T(8,128)S(1)}, u32[]{:S(2)}, u32[]{:S(2)}) %collective-permute-start.8) | collective-permute-done | bytes 262176 | tf_op jit(solution)/shard_map/ppermute | solution.py:54
  47.0 0.7 add.3
  47.7 4.8 %all-to-all-start.1 = ((f32[16,16,256]{2,1,0:T(8,128)}), f32[16,16,256]{2,1,0:T(8,128)S(1)}, u32[]{:S(2)}, u32[]{:S(2)}) async-start(f32[16,16,256]{2,1,0:T(8,128)} %bitcast.6), calls=%async_computation.1 | async-start | bytes 524288 | tf_op jit(solution)/shard_map/all_to_all | solution.py:44
  52.5 6.4 %collective-permute-done.9.got = bf16[4,256,128]{2,1,0:T(8,128)(2,1)S(1)} collective-permute-done((bf16[4,256,128]{2,1,0:T(8,128)(2,1)S(1)}, bf16[4,256,128]{2,1,0:T(8,128)(2,1)S(1)}, u32[]{:S(2)}, u32[]{:S(2)}) %collective-permute-start.9) | collective-permute-done | bytes 262176 | tf_op jit(solution)/shard_map/ppermute | solution.py:474
  58.9 1.2 %all-to-all-done.1.pieces = f32[16,16,256]{2,1,0:T(8,128)S(1)} async-done(((f32[16,16,256]{2,1,0:T(8,128)}), f32[16,16,256]{2,1,0:T(8,128)S(1)}, u32[]{:S(2)}, u32[]{:S(2)}) %all-to-all-start.1) | async-done | bytes 262176 | tf_op jit(solution)/shard_map/all_to_all | solution.py:44
  60.1 0.7 fold.2
  60.8 4.1 %all-to-all-start.2 = ((f32[8,16,256]{2,1,0:T(8,128)}), f32[8,16,256]{2,1,0:T(8,128)S(1)}, u32[]{:S(2)}, u32[]{:S(2)}) async-start(f32[8,16,256]{2,1,0:T(8,128)} %get-tuple-element.56), calls=%async_computation.2 | async-start | bytes 262144 | tf_op jit(solution)/shard_map/all_to_all | solution.py:44
  64.9 1.1 %collective-permute-start.10 = (bf16[2,256,128]{2,1,0:T(8,128)(2,1)S(1)}, bf16[2,256,128]{2,1,0:T(8,128)(2,1)S(1)}, u32[]{:S(2)}, u32[]{:S(2)}) collective-permute-start(bf16[2,256,128]{2,1,0:T(8,128)(2,1)S(1)} %get-tuple-element.58), channel_id=1, source_target_pairs={{0,16},{8,24},{16,0},{24,8},{32,48},{40,56},{48,32},{56,40},{64,80... | collective-permute-start | bytes 393224 | tf_op jit(solution)/shard_map/ppermute | solution.py:492
  66.0 2.7 %collective-permute-done.10.got = bf16[2,256,128]{2,1,0:T(8,128)(2,1)S(1)} collective-permute-done((bf16[2,256,128]{2,1,0:T(8,128)(2,1)S(1)}, bf16[2,256,128]{2,1,0:T(8,128)(2,1)S(1)}, u32[]{:S(2)}, u32[]{:S(2)}) %collective-permute-start.10) | collective-permute-done | bytes 131104 | tf_op jit(solution)/shard_map/ppermute | solution.py:492
  68.7 4.1 %all-to-all-done.2.pieces = f32[8,16,256]{2,1,0:T(8,128)S(1)} async-done(((f32[8,16,256]{2,1,0:T(8,128)}), f32[8,16,256]{2,1,0:T(8,128)S(1)}, u32[]{:S(2)}, u32[]{:S(2)}) %all-to-all-start.2) | async-done | bytes 131104 | tf_op jit(solution)/shard_map/all_to_all | solution.py:44
  72.8 0.7 fold.3
  73.6 4.7 %all-to-all-start.3 = ((f32[16,16,256]{2,1,0:T(8,128)}), f32[16,16,256]{2,1,0:T(8,128)S(1)}, u32[]{:S(2)}, u32[]{:S(2)}) async-start(f32[16,16,256]{2,1,0:T(8,128)} %get-tuple-element.59), calls=%async_computation.3 | async-start | bytes 524288 | tf_op jit(solution)/shard_map/all_to_all | solution.py:44
  78.2 1.6 %collective-permute-start.12 = (bf16[1,256,128]{2,1,0:T(8,128)(2,1)S(1)}, bf16[1,256,128]{2,1,0:T(8,128)(2,1)S(1)}, u32[]{:S(2)}, u32[]{:S(2)}) collective-permute-start(bf16[1,256,128]{2,1,0:T(8,128)(2,1)S(1)} %get-tuple-element.61), channel_id=1, source_target_pairs={{0,128},{8,136},{16,144},{24,152},{32,160},{40,168},{48,176},{56,1... | collective-permute-start | bytes 196616 | tf_op jit(solution)/shard_map/ppermute | solution.py:474
  79.8 5.8 %all-to-all-done.3 = f32[16,16,256]{2,1,0:T(8,128)S(1)} async-done(((f32[16,16,256]{2,1,0:T(8,128)}), f32[16,16,256]{2,1,0:T(8,128)S(1)}, u32[]{:S(2)}, u32[]{:S(2)}) %all-to-all-start.3) | async-done | bytes 262176 | tf_op jit(solution)/shard_map/all_to_all | solution.py:44
  85.6 3.2 %collective-permute-start.11 = (f32[256,256]{1,0:T(8,128)S(1)}, f32[256,256]{1,0:T(8,128)S(1)}, u32[]{:S(2)}, u32[]{:S(2)}) collective-permute-start(f32[256,256]{1,0:T(8,128)S(1)} %bitcast.8), channel_id=1, source_target_pairs={{0,8},{8,0},{16,24},{24,16},{32,40},{40,32},{48,56},{56,48},{64,72... | collective-permute-start | bytes 786440 | tf_op jit(solution)/shard_map/ppermute | solution.py:54
  89.1 0.8 collective-permute-done.11.other
  90.0 0.8 last.1
  (31 shorter events, 2.5 us)
Async XLA Ops:
  2.4 20.5 %all-to-all-start = ((bf16[8,144,256]{2,1,0:T(8,128)(2,1)}), bf16[8,144,256]{2,1,0:T(8,128)(2,1)S(1)}, u32[]{:S(2)}, u32[]{:S(2)}) async-start(bf16[8,144,256]{2,1,0:T(8,128)(2,1)} %head.1), calls=%async_computation | async-start | bytes 1179648 | tf_op jit(solution)/shard_map/all_to_all | solution.py:44
  9.9 9.4 %collective-permute-start = (bf16[1,128,256]{2,1,0:T(8,128)(2,1)}, bf16[1,128,256]{2,1,0:T(8,128)(2,1)S(1)}, u32[]{:S(2)}, u32[]{:S(2)}) collective-permute-start(bf16[1,128,256]{2,1,0:T(8,128)(2,1)} %bitcast.10), channel_id=1, source_target_pairs={{0,192},{8,200},{16,208},{24,216},{32,224},{40,232},{48,240},{56,2... | collective-permute-start | bytes 196616 | tf_op jit(solution)/shard_map/ppermute | solution.py:479
  15.9 7.0 %collective-permute-start.1 = (bf16[1,128,256]{2,1,0:T(8,128)(2,1)}, bf16[1,128,256]{2,1,0:T(8,128)(2,1)S(1)}, u32[]{:S(2)}, u32[]{:S(2)}) collective-permute-start(bf16[1,128,256]{2,1,0:T(8,128)(2,1)} %bitcast.11), channel_id=1, source_target_pairs={{0,64},{8,72},{16,80},{24,88},{32,96},{40,104},{48,112},{56,120},{... | collective-permute-start | bytes 196616 | tf_op jit(solution)/shard_map/ppermute | solution.py:479
  16.6 0.8 copy-start.1
  17.4 0.7 copy-start.2
  18.1 0.7 copy-start.3
  19.3 8.0 %collective-permute-start.3 = (bf16[1,128,256]{2,1,0:T(8,128)(2,1)S(1)}, bf16[1,128,256]{2,1,0:T(8,128)(2,1)S(1)}, u32[]{:S(2)}, u32[]{:S(2)}) collective-permute-start(bf16[1,128,256]{2,1,0:T(8,128)(2,1)S(1)} %collective-permute-done.refs_1_), channel_id=1, source_target_pairs={{0,192},{8,200},{16,208},{24,216},{32,224},{40,232},{48,240},{56,2... | collective-permute-start | bytes 196616 | tf_op jit(solution)/shard_map/ppermute | solution.py:479
  22.9 15.1 %copy-start = (bf16[128,256]{1,0:T(8,128)(2,1)S(1)}, bf16[128,256]{1,0:T(8,128)(2,1)}, u32[]{:S(2)}) copy-start(bf16[128,256]{1,0:T(8,128)(2,1)} %grads.4) | copy-start | bytes 196612
  27.3 6.5 %copy-start.6 = (f32[8,256,128]{2,1,0:T(8,128)}, f32[8,256,128]{2,1,0:T(8,128)S(1)}, u32[]{:S(2)}) copy-start(f32[8,256,128]{2,1,0:T(8,128)S(1)} %get-tuple-element.37.near) | copy-start | bytes 3145732
  27.3 4.0 %collective-permute-start.5 = (bf16[2,8,128,128]{3,2,1,0:T(8,128)(2,1)S(1)}, bf16[2,8,128,128]{3,2,1,0:T(8,128)(2,1)S(1)}, u32[]{:S(2)}, u32[]{:S(2)}) collective-permute-start(bf16[2,8,128,128]{3,2,1,0:T(8,128)(2,1)S(1)} %get-tuple-element.47), channel_id=1, source_target_pairs={{0,8},{8,0},{16,24},{24,16},{32,40},{40,32},{48,56},{56,48},{64,72... | collective-permute-start | bytes 1572872 | tf_op jit(solution)/shard_map/ppermute | solution.py:54
  29.7 8.6 %collective-permute-start.2 = (bf16[8,256,128]{2,1,0:T(8,128)(2,1)S(1)}, bf16[8,256,128]{2,1,0:T(8,128)(2,1)S(1)}, u32[]{:S(2)}, u32[]{:S(2)}) collective-permute-start(bf16[8,256,128]{2,1,0:T(8,128)(2,1)S(1)} %get-tuple-element.38), channel_id=1, source_target_pairs={{0,8},{8,0},{16,24},{24,16},{32,40},{40,32},{48,56},{56,48},{64,72... | collective-permute-start | bytes 1572872 | tf_op jit(solution)/shard_map/ppermute | solution.py:54
  29.8 8.5 %collective-permute-start.4 = (bf16[4,128,256]{2,1,0:T(8,128)(2,1)S(1)}, bf16[4,128,256]{2,1,0:T(8,128)(2,1)S(1)}, u32[]{:S(2)}, u32[]{:S(2)}) collective-permute-start(bf16[4,128,256]{2,1,0:T(8,128)(2,1)S(1)} %join.1.feats_low), channel_id=1, source_target_pairs={{0,16},{8,24},{16,0},{24,8},{32,48},{40,56},{48,32},{56,40},{64,80... | collective-permute-start | bytes 786440 | tf_op jit(solution)/shard_map/ppermute | solution.py:492
  31.2 57.6 %copy-start.4 = (bf16[256,256]{1,0:T(8,128)(2,1)S(1)}, bf16[256,256]{1,0:T(8,128)(2,1)}, u32[]{:S(2)}) copy-start(bf16[256,256]{1,0:T(8,128)(2,1)} %w_self.1) | copy-start | bytes 393220
  31.2 57.6 %copy-start.5 = (bf16[256,256]{1,0:T(8,128)(2,1)S(1)}, bf16[256,256]{1,0:T(8,128)(2,1)}, u32[]{:S(2)}) copy-start(bf16[256,256]{1,0:T(8,128)(2,1)} %w_neigh.1) | copy-start | bytes 393220
  31.3 8.8 %collective-permute-start.6 = (bf16[8,128,128]{2,1,0:T(8,128)(2,1)S(1)}, bf16[8,128,128]{2,1,0:T(8,128)(2,1)S(1)}, u32[]{:S(2)}, u32[]{:S(2)}) collective-permute-start(bf16[8,128,128]{2,1,0:T(8,128)(2,1)S(1)} %get-tuple-element.48), channel_id=1, source_target_pairs={{0,32},{8,40},{16,48},{24,56},{32,0},{40,8},{48,16},{56,24},{64,96... | collective-permute-start | bytes 786440 | tf_op jit(solution)/shard_map/ppermute | solution.py:474
  33.8 10.3 %collective-permute-start.7 = (bf16[8,128,128]{2,1,0:T(8,128)(2,1)S(1)}, bf16[8,128,128]{2,1,0:T(8,128)(2,1)S(1)}, u32[]{:S(2)}, u32[]{:S(2)}) collective-permute-start(bf16[8,128,128]{2,1,0:T(8,128)(2,1)S(1)} %get-tuple-element.49), channel_id=1, source_target_pairs={{0,224},{8,232},{16,240},{24,248},{32,64},{40,72},{48,80},{56,88},... | collective-permute-start | bytes 786440 | tf_op jit(solution)/shard_map/ppermute | solution.py:488
  38.3 1.2 %copy-start.7 = (f32[8,256,128]{2,1,0:T(8,128)S(1)}, f32[8,256,128]{2,1,0:T(8,128)}, u32[]{:S(2)}) copy-start(f32[8,256,128]{2,1,0:T(8,128)} %copy-done.6) | copy-start | bytes 3145732
  44.5 2.4 %collective-permute-start.8 = (f32[256,256]{1,0:T(8,128)S(1)}, f32[256,256]{1,0:T(8,128)S(1)}, u32[]{:S(2)}, u32[]{:S(2)}) collective-permute-start(f32[256,256]{1,0:T(8,128)S(1)} %get-tuple-element.53), channel_id=1, source_target_pairs={{0,8},{8,0},{16,24},{24,16},{32,40},{40,32},{48,56},{56,48},{64,72... | collective-permute-start | bytes 786440 | tf_op jit(solution)/shard_map/ppermute | solution.py:54
  45.8 13.1 %collective-permute-start.9 = (bf16[4,256,128]{2,1,0:T(8,128)(2,1)S(1)}, bf16[4,256,128]{2,1,0:T(8,128)(2,1)S(1)}, u32[]{:S(2)}, u32[]{:S(2)}) collective-permute-start(bf16[4,256,128]{2,1,0:T(8,128)(2,1)S(1)} %get-tuple-element.55), channel_id=1, source_target_pairs={{0,64},{8,72},{16,80},{24,88},{32,96},{40,104},{48,112},{56,120},{... | collective-permute-start | bytes 786440 | tf_op jit(solution)/shard_map/ppermute | solution.py:474
  47.7 12.4 %all-to-all-start.1 = ((f32[16,16,256]{2,1,0:T(8,128)}), f32[16,16,256]{2,1,0:T(8,128)S(1)}, u32[]{:S(2)}, u32[]{:S(2)}) async-start(f32[16,16,256]{2,1,0:T(8,128)} %bitcast.6), calls=%async_computation.1 | async-start | bytes 524288 | tf_op jit(solution)/shard_map/all_to_all | solution.py:44
  60.8 12.0 %all-to-all-start.2 = ((f32[8,16,256]{2,1,0:T(8,128)}), f32[8,16,256]{2,1,0:T(8,128)S(1)}, u32[]{:S(2)}, u32[]{:S(2)}) async-start(f32[8,16,256]{2,1,0:T(8,128)} %get-tuple-element.56), calls=%async_computation.2 | async-start | bytes 262144 | tf_op jit(solution)/shard_map/all_to_all | solution.py:44
  64.9 3.8 %collective-permute-start.10 = (bf16[2,256,128]{2,1,0:T(8,128)(2,1)S(1)}, bf16[2,256,128]{2,1,0:T(8,128)(2,1)S(1)}, u32[]{:S(2)}, u32[]{:S(2)}) collective-permute-start(bf16[2,256,128]{2,1,0:T(8,128)(2,1)S(1)} %get-tuple-element.58), channel_id=1, source_target_pairs={{0,16},{8,24},{16,0},{24,8},{32,48},{40,56},{48,32},{56,40},{64,80... | collective-permute-start | bytes 393224 | tf_op jit(solution)/shard_map/ppermute | solution.py:492
  73.6 12.0 %all-to-all-start.3 = ((f32[16,16,256]{2,1,0:T(8,128)}), f32[16,16,256]{2,1,0:T(8,128)S(1)}, u32[]{:S(2)}, u32[]{:S(2)}) async-start(f32[16,16,256]{2,1,0:T(8,128)} %get-tuple-element.59), calls=%async_computation.3 | async-start | bytes 524288 | tf_op jit(solution)/shard_map/all_to_all | solution.py:44
  78.2 10.6 %collective-permute-start.12 = (bf16[1,256,128]{2,1,0:T(8,128)(2,1)S(1)}, bf16[1,256,128]{2,1,0:T(8,128)(2,1)S(1)}, u32[]{:S(2)}, u32[]{:S(2)}) collective-permute-start(bf16[1,256,128]{2,1,0:T(8,128)(2,1)S(1)} %get-tuple-element.61), channel_id=1, source_target_pairs={{0,128},{8,136},{16,144},{24,152},{32,160},{40,168},{48,176},{56,1... | collective-permute-start | bytes 196616 | tf_op jit(solution)/shard_map/ppermute | solution.py:474
  85.6 4.3 %collective-permute-start.11 = (f32[256,256]{1,0:T(8,128)S(1)}, f32[256,256]{1,0:T(8,128)S(1)}, u32[]{:S(2)}, u32[]{:S(2)}) collective-permute-start(f32[256,256]{1,0:T(8,128)S(1)} %bitcast.8), channel_id=1, source_target_pairs={{0,8},{8,0},{16,24},{24,16},{32,40},{40,32},{48,56},{56,48},{64,72... | collective-permute-start | bytes 786440 | tf_op jit(solution)/shard_map/ppermute | solution.py:54

commit v7 on v6

--- a/solution.py
+++ b/solution.py
@@ -387,18 +387,20 @@
     )(core[None], z[None], base, part_a, part_b, feats_low, feats_high, total_t, own_self)
 
 
-def fold_kernel(scale, pieces, keep, got, out, *rest):
+def fold_kernel(scale, pieces, keep, got, out, kept, send, whole, sems):
     total = pieces[0]
     for k in range(1, pieces.shape[0]):
         total += pieces[k]
-    total = total * scale
-    for k in range(out.shape[0]):
-        out[k] = total
+    whole[...] = total * scale
+    copies = [pltpu.make_async_copy(whole, out.at[k], sems.at[k]) for k in range(out.shape[0])]
+    for copy in copies:
+        copy.start()
     half = keep.shape[0] // 2
-    kept, send = rest
     for k in range(half):
         kept[k] = keep[k] + got[k].astype(jnp.float32)
         send[k] = (keep[half + k] + got[half + k].astype(jnp.float32)).astype(jnp.bfloat16)
+    for copy in copies:
+        copy.wait()
 
 
 def fold(scale, pieces, receivers, keep, got):
@@ -406,11 +408,15 @@
     return pl.pallas_call(
         functools.partial(fold_kernel, scale),
         in_specs=[VMEM] * 3,
-        out_specs=[VMEM] * 3,
+        out_specs=[ANY, VMEM, VMEM],
         out_shape=[
             jax.ShapeDtypeStruct((receivers, 16, 256), jnp.float32),
             jax.ShapeDtypeStruct((half, 256, 128), jnp.float32),
             jax.ShapeDtypeStruct((half, 256, 128), jnp.bfloat16),
+        ],
+        scratch_shapes=[
+            pltpu.VMEM((16, 256), jnp.float32),
+            pltpu.SemaphoreType.DMA((receivers,)),
         ],
         compiler_params=params(8),
         name="fold",

time: 91.3 us -> 92.1 us (level)
  starting transfers between devices: 48.4 us -> 45.3 us
  waiting for transfers between devices: 26.4 us -> 28.3 us
  Pallas kernels: 10.4 us -> 11.8 us
    ppermute x2, starting transfers between devices: 2.43 us -> 0.71 us  [swap_x(): return lax.ppermute(value, 'row', [(row, row ^ 2) for row in range(32)])]
    pallas_call x1, Pallas kernels: 4.3 us -> 5.58 us  [sparse_product(): pl.pallas_call(sparse_kernel, in_specs=[SMEM, SMEM, VMEM, ANY], out_specs...]
    ppermute x4, starting transfers between devices: 6.97 us -> 5.82 us  [swap_core(): return lax.ppermute(value, 'row', [(row, row ^ 1) for row in range(32)])]
    ppermute x2, waiting for transfers between devices: 2.68 us -> 3.68 us  [swap_x(): return lax.ppermute(value, 'row', [(row, row ^ 2) for row in range(32)])]
  transfers between devices with their start and end apart: 17 -> 17, of which waited for: 10 -> 9; matrix products, arithmetic and copies ran while one was open for 1% -> 1% of each run, Pallas kernels for 7% -> 8%
where the time goes in v7:
time: 92.1 us; the launch traced here: 90.9 us
  starting transfers between devices  45.3 us (49%)
  waiting for transfers between devices  28.3 us (31%)
  Pallas kernels  11.8 us (13%)
  local copies, waits for them, and re-layouts  3.42 us (4%)
  between operations  1.45 us (2%)
    all_to_all x4, starting transfers between devices, exchange(): lax.all_to_all(blocks, ('row', 'blk'), 0, 0, axis_index_groups=groups_of(...  20.9 us
    all_to_all x4, waiting for transfers between devices, exchange(): lax.all_to_all(blocks, ('row', 'blk'), 0, 0, axis_index_groups=groups_of(...  10.8 us
    ppermute x3, starting transfers between devices, shift_z(): return lax.ppermute(value, 'row', pairs)  9.65 us
    ppermute x3, waiting for transfers between devices, swap_z(): lax.ppermute(value, 'row', [(row, row ^ 4 * distance) for row in range(32)])  6.56 us
    ppermute x4, starting transfers between devices, swap_core(): return lax.ppermute(value, 'row', [(row, row ^ 1) for row in range(32)])  5.82 us
    pallas_call x1, Pallas kernels, sparse_product(): pl.pallas_call(sparse_kernel, in_specs=[SMEM, SMEM, VMEM, ANY], out_specs...  5.58 us
    ppermute x1, starting transfers between devices, swap_z_other(): return lax.ppermute(value, 'row', pairs)  4.76 us
    ppermute x1, waiting for transfers between devices, swap_z_other(): return lax.ppermute(value, 'row', pairs)  4.46 us
  transfers between devices with their start and end apart: 17, of which 9 were waited for; matrix products, arithmetic and copies ran while one was open for 1% of the time, Pallas kernels for 8%

profile of v7, /device:TPU:1, one launch (start us, length us, event | category | flops | bytes accessed | tf_op | source)
XLA Modules:
  0.0 90.9 jit_solution(6750951750198758799)
XLA Ops:
  0.6 1.8 %head.1 = bf16[8,144,256]{2,1,0:T(8,128)(2,1)} custom-call(bf16[128,256]{1,0:T(8,128)(2,1)} %grads.4, s32[1,128]{1,0:T(1,128)} %bitcast.12), custom_call_target="tpu_custom_call" | custom-call | tf_op jit(solution)/shard_map/head/pallas_call | solution.py:81
  2.4 7.5 %all-to-all-start = ((bf16[8,144,256]{2,1,0:T(8,128)(2,1)}), bf16[8,144,256]{2,1,0:T(8,128)(2,1)S(1)}, u32[]{:S(2)}, u32[]{:S(2)}) async-start(bf16[8,144,256]{2,1,0:T(8,128)(2,1)} %head.1), calls=%async_computation | async-start | bytes 1179648 | tf_op jit(solution)/shard_map/all_to_all | solution.py:44
  9.9 6.0 %collective-permute-start = (bf16[1,128,256]{2,1,0:T(8,128)(2,1)}, bf16[1,128,256]{2,1,0:T(8,128)(2,1)S(1)}, u32[]{:S(2)}, u32[]{:S(2)}) collective-permute-start(bf16[1,128,256]{2,1,0:T(8,128)(2,1)} %bitcast.10), channel_id=1, source_target_pairs={{0,192},{8,200},{16,208},{24,216},{32,224},{40,232},{48,240},{56,2... | collective-permute-start | bytes 196616 | tf_op jit(solution)/shard_map/ppermute | solution.py:485
  16.6 0.8 copy-done.1
  17.4 0.7 copy-done.2
  18.1 0.7 copy-done.3
  19.3 3.6 %collective-permute-start.3 = (bf16[1,128,256]{2,1,0:T(8,128)(2,1)S(1)}, bf16[1,128,256]{2,1,0:T(8,128)(2,1)S(1)}, u32[]{:S(2)}, u32[]{:S(2)}) collective-permute-start(bf16[1,128,256]{2,1,0:T(8,128)(2,1)S(1)} %collective-permute-done.refs_1_), channel_id=1, source_target_pairs={{0,192},{8,200},{16,208},{24,216},{32,224},{40,232},{48,240},{56,2... | collective-permute-start | bytes 196616 | tf_op jit(solution)/shard_map/ppermute | solution.py:485
  22.9 5.6 %sparse.1 = (f32[8,256,128]{2,1,0:T(8,128)S(1)}, f32[8,128,128]{2,1,0:T(8,128)S(1)}, f32[8,128,128]{2,1,0:T(8,128)S(1)}, bf16[8,256,128]{2,1,0:T(8,128)(2,1)S(1)}, bf16[2,8,128,128]{3,2,1,0:T(8,128)(2,1)S(1)}) custom-call(s32[8,128]{1,0:T(8,128)S(1)} %get-tuple-element.35.plan, s32[1]{0:T(128)} %bitcast.1.z, bf16[8,144,256]{2,1,0:T(8,128)(2,1)S(1)} %all-to-all-done.grads, ...), custom_call_target="tpu_custom_call" | custom-call | flops 4000000000 | bytes 12582912 | tf_op jit(solution)/shard_map/sparse/pallas_call | solution.py:266
  28.6 0.6 collective-permute-start.5
  29.3 0.6 collective-permute-start.4
  29.8 0.8 collective-permute-done.5.part
  30.8 1.7 %collective-permute-start.6 = (bf16[8,128,128]{2,1,0:T(8,128)(2,1)S(1)}, bf16[8,128,128]{2,1,0:T(8,128)(2,1)S(1)}, u32[]{:S(2)}, u32[]{:S(2)}) collective-permute-start(bf16[8,128,128]{2,1,0:T(8,128)(2,1)S(1)} %get-tuple-element.48), channel_id=1, source_target_pairs={{0,32},{8,40},{16,48},{24,56},{32,0},{40,8},{48,16},{56,24},{64,96... | collective-permute-start | bytes 786440 | tf_op jit(solution)/shard_map/ppermute | solution.py:480
  32.5 4.8 %collective-permute-start.7 = (bf16[8,128,128]{2,1,0:T(8,128)(2,1)S(1)}, bf16[8,128,128]{2,1,0:T(8,128)(2,1)S(1)}, u32[]{:S(2)}, u32[]{:S(2)}) collective-permute-start(bf16[8,128,128]{2,1,0:T(8,128)(2,1)S(1)} %get-tuple-element.49), channel_id=1, source_target_pairs={{0,224},{8,232},{16,240},{24,248},{32,64},{40,72},{48,80},{56,88},... | collective-permute-start | bytes 786440 | tf_op jit(solution)/shard_map/ppermute | solution.py:494
  37.5 1.2 %copy-done.7 = f32[8,256,128]{2,1,0:T(8,128)S(1)} copy-done((f32[8,256,128]{2,1,0:T(8,128)S(1)}, f32[8,256,128]{2,1,0:T(8,128)}, u32[]{:S(2)}) %copy-start.7) | copy-done | bytes 1048600
  39.2 4.5 %collective-permute-done.7.part_b = bf16[8,128,128]{2,1,0:T(8,128)(2,1)S(1)} collective-permute-done((bf16[8,128,128]{2,1,0:T(8,128)(2,1)S(1)}, bf16[8,128,128]{2,1,0:T(8,128)(2,1)S(1)}, u32[]{:S(2)}, u32[]{:S(2)}) %collective-permute-start.7) | collective-permute-done | bytes 262176 | tf_op jit(solution)/shard_map/ppermute | solution.py:494
  44.1 1.0 %collective-permute-start.8 = (f32[256,256]{1,0:T(8,128)S(1)}, f32[256,256]{1,0:T(8,128)S(1)}, u32[]{:S(2)}, u32[]{:S(2)}) collective-permute-start(f32[256,256]{1,0:T(8,128)S(1)} %get-tuple-element.53), channel_id=1, source_target_pairs={{0,8},{8,0},{16,24},{24,16},{32,40},{40,32},{48,56},{56,48},{64,72... | collective-permute-start | bytes 786440 | tf_op jit(solution)/shard_map/ppermute | solution.py:54
  45.0 1.2 %collective-permute-done.8 = f32[256,256]{1,0:T(8,128)S(1)} collective-permute-done((f32[256,256]{1,0:T(8,128)S(1)}, f32[256,256]{1,0:T(8,128)S(1)}, u32[]{:S(2)}, u32[]{:S(2)}) %collective-permute-start.8) | collective-permute-done | bytes 262176 | tf_op jit(solution)/shard_map/ppermute | solution.py:54
  46.2 0.7 add.3
  46.9 5.1 %all-to-all-start.1 = ((f32[16,16,256]{2,1,0:T(8,128)}), f32[16,16,256]{2,1,0:T(8,128)S(1)}, u32[]{:S(2)}, u32[]{:S(2)}) async-start(f32[16,16,256]{2,1,0:T(8,128)} %bitcast.6), calls=%async_computation.1 | async-start | bytes 524288 | tf_op jit(solution)/shard_map/all_to_all | solution.py:44
  52.0 6.5 %collective-permute-done.9.got = bf16[4,256,128]{2,1,0:T(8,128)(2,1)S(1)} collective-permute-done((bf16[4,256,128]{2,1,0:T(8,128)(2,1)S(1)}, bf16[4,256,128]{2,1,0:T(8,128)(2,1)S(1)}, u32[]{:S(2)}, u32[]{:S(2)}) %collective-permute-start.9) | collective-permute-done | bytes 262176 | tf_op jit(solution)/shard_map/ppermute | solution.py:480
  58.6 1.0 %all-to-all-done.1.pieces = f32[16,16,256]{2,1,0:T(8,128)S(1)} async-done(((f32[16,16,256]{2,1,0:T(8,128)}), f32[16,16,256]{2,1,0:T(8,128)S(1)}, u32[]{:S(2)}, u32[]{:S(2)}) %all-to-all-start.1) | async-done | bytes 262176 | tf_op jit(solution)/shard_map/all_to_all | solution.py:44
  59.6 0.7 fold.2
  60.3 4.8 %all-to-all-start.2 = ((f32[8,16,256]{2,1,0:T(8,128)}), f32[8,16,256]{2,1,0:T(8,128)S(1)}, u32[]{:S(2)}, u32[]{:S(2)}) async-start(f32[8,16,256]{2,1,0:T(8,128)} %get-tuple-element.56), calls=%async_computation.2 | async-start | bytes 262144 | tf_op jit(solution)/shard_map/all_to_all | solution.py:44
  65.3 3.7 %collective-permute-done.10.got = bf16[2,256,128]{2,1,0:T(8,128)(2,1)S(1)} collective-permute-done((bf16[2,256,128]{2,1,0:T(8,128)(2,1)S(1)}, bf16[2,256,128]{2,1,0:T(8,128)(2,1)S(1)}, u32[]{:S(2)}, u32[]{:S(2)}) %collective-permute-start.10) | collective-permute-done | bytes 131104 | tf_op jit(solution)/shard_map/ppermute | solution.py:498
  69.0 4.1 %all-to-all-done.2.pieces = f32[8,16,256]{2,1,0:T(8,128)S(1)} async-done(((f32[8,16,256]{2,1,0:T(8,128)}), f32[8,16,256]{2,1,0:T(8,128)S(1)}, u32[]{:S(2)}, u32[]{:S(2)}) %all-to-all-start.2) | async-done | bytes 131104 | tf_op jit(solution)/shard_map/all_to_all | solution.py:44
  73.1 0.8 fold.3
  73.9 3.5 %all-to-all-start.3 = ((f32[16,16,256]{2,1,0:T(8,128)}), f32[16,16,256]{2,1,0:T(8,128)S(1)}, u32[]{:S(2)}, u32[]{:S(2)}) async-start(f32[16,16,256]{2,1,0:T(8,128)} %get-tuple-element.59), calls=%async_computation.3 | async-start | bytes 524288 | tf_op jit(solution)/shard_map/all_to_all | solution.py:44
  77.5 1.6 %collective-permute-start.12 = (bf16[1,256,128]{2,1,0:T(8,128)(2,1)S(1)}, bf16[1,256,128]{2,1,0:T(8,128)(2,1)S(1)}, u32[]{:S(2)}, u32[]{:S(2)}) collective-permute-start(bf16[1,256,128]{2,1,0:T(8,128)(2,1)S(1)} %get-tuple-element.61), channel_id=1, source_target_pairs={{0,128},{8,136},{16,144},{24,152},{32,160},{40,168},{48,176},{56,1... | collective-permute-start | bytes 196616 | tf_op jit(solution)/shard_map/ppermute | solution.py:480
  79.1 5.7 %all-to-all-done.3 = f32[16,16,256]{2,1,0:T(8,128)S(1)} async-done(((f32[16,16,256]{2,1,0:T(8,128)}), f32[16,16,256]{2,1,0:T(8,128)S(1)}, u32[]{:S(2)}, u32[]{:S(2)}) %all-to-all-start.3) | async-done | bytes 262176 | tf_op jit(solution)/shard_map/all_to_all | solution.py:44
  84.8 4.2 %collective-permute-start.11 = (f32[256,256]{1,0:T(8,128)S(1)}, f32[256,256]{1,0:T(8,128)S(1)}, u32[]{:S(2)}, u32[]{:S(2)}) collective-permute-start(f32[256,256]{1,0:T(8,128)S(1)} %bitcast.8), channel_id=1, source_target_pairs={{0,8},{8,0},{16,24},{24,16},{32,40},{40,32},{48,56},{56,48},{64,72... | collective-permute-start | bytes 786440 | tf_op jit(solution)/shard_map/ppermute | solution.py:54
  89.3 0.8 collective-permute-done.11.other
  90.1 0.8 last.1
  (31 shorter events, 2.3 us)
Async XLA Ops:
  2.4 20.5 %all-to-all-start = ((bf16[8,144,256]{2,1,0:T(8,128)(2,1)}), bf16[8,144,256]{2,1,0:T(8,128)(2,1)S(1)}, u32[]{:S(2)}, u32[]{:S(2)}) async-start(bf16[8,144,256]{2,1,0:T(8,128)(2,1)} %head.1), calls=%async_computation | async-start | bytes 1179648 | tf_op jit(solution)/shard_map/all_to_all | solution.py:44
  9.9 9.4 %collective-permute-start = (bf16[1,128,256]{2,1,0:T(8,128)(2,1)}, bf16[1,128,256]{2,1,0:T(8,128)(2,1)S(1)}, u32[]{:S(2)}, u32[]{:S(2)}) collective-permute-start(bf16[1,128,256]{2,1,0:T(8,128)(2,1)} %bitcast.10), channel_id=1, source_target_pairs={{0,192},{8,200},{16,208},{24,216},{32,224},{40,232},{48,240},{56,2... | collective-permute-start | bytes 196616 | tf_op jit(solution)/shard_map/ppermute | solution.py:485
  15.9 7.0 %collective-permute-start.1 = (bf16[1,128,256]{2,1,0:T(8,128)(2,1)}, bf16[1,128,256]{2,1,0:T(8,128)(2,1)S(1)}, u32[]{:S(2)}, u32[]{:S(2)}) collective-permute-start(bf16[1,128,256]{2,1,0:T(8,128)(2,1)} %bitcast.11), channel_id=1, source_target_pairs={{0,64},{8,72},{16,80},{24,88},{32,96},{40,104},{48,112},{56,120},{... | collective-permute-start | bytes 196616 | tf_op jit(solution)/shard_map/ppermute | solution.py:485
  16.6 0.8 copy-start.1
  17.4 0.7 copy-start.2
  18.1 0.7 copy-start.3
  19.3 9.2 %collective-permute-start.3 = (bf16[1,128,256]{2,1,0:T(8,128)(2,1)S(1)}, bf16[1,128,256]{2,1,0:T(8,128)(2,1)S(1)}, u32[]{:S(2)}, u32[]{:S(2)}) collective-permute-start(bf16[1,128,256]{2,1,0:T(8,128)(2,1)S(1)} %collective-permute-done.refs_1_), channel_id=1, source_target_pairs={{0,192},{8,200},{16,208},{24,216},{32,224},{40,232},{48,240},{56,2... | collective-permute-start | bytes 196616 | tf_op jit(solution)/shard_map/ppermute | solution.py:485
  22.9 14.3 %copy-start = (bf16[128,256]{1,0:T(8,128)(2,1)S(1)}, bf16[128,256]{1,0:T(8,128)(2,1)}, u32[]{:S(2)}) copy-start(bf16[128,256]{1,0:T(8,128)(2,1)} %grads.4) | copy-start | bytes 196612
  28.5 4.0 %copy-start.6 = (f32[8,256,128]{2,1,0:T(8,128)}, f32[8,256,128]{2,1,0:T(8,128)S(1)}, u32[]{:S(2)}) copy-start(f32[8,256,128]{2,1,0:T(8,128)S(1)} %get-tuple-element.37.near) | copy-start | bytes 3145732
  28.6 2.1 %collective-permute-start.5 = (bf16[2,8,128,128]{3,2,1,0:T(8,128)(2,1)S(1)}, bf16[2,8,128,128]{3,2,1,0:T(8,128)(2,1)S(1)}, u32[]{:S(2)}, u32[]{:S(2)}) collective-permute-start(bf16[2,8,128,128]{3,2,1,0:T(8,128)(2,1)S(1)} %get-tuple-element.47), channel_id=1, source_target_pairs={{0,8},{8,0},{16,24},{24,16},{32,40},{40,32},{48,56},{56,48},{64,72... | collective-permute-start | bytes 1572872 | tf_op jit(solution)/shard_map/ppermute | solution.py:54
  29.1 8.4 %collective-permute-start.2 = (bf16[8,256,128]{2,1,0:T(8,128)(2,1)S(1)}, bf16[8,256,128]{2,1,0:T(8,128)(2,1)S(1)}, u32[]{:S(2)}, u32[]{:S(2)}) collective-permute-start(bf16[8,256,128]{2,1,0:T(8,128)(2,1)S(1)} %get-tuple-element.38), channel_id=1, source_target_pairs={{0,8},{8,0},{16,24},{24,16},{32,40},{40,32},{48,56},{56,48},{64,72... | collective-permute-start | bytes 1572872 | tf_op jit(solution)/shard_map/ppermute | solution.py:54
  29.3 8.2 %collective-permute-start.4 = (bf16[4,128,256]{2,1,0:T(8,128)(2,1)S(1)}, bf16[4,128,256]{2,1,0:T(8,128)(2,1)S(1)}, u32[]{:S(2)}, u32[]{:S(2)}) collective-permute-start(bf16[4,128,256]{2,1,0:T(8,128)(2,1)S(1)} %join.1.feats_low), channel_id=1, source_target_pairs={{0,16},{8,24},{16,0},{24,8},{32,48},{40,56},{48,32},{56,40},{64,80... | collective-permute-start | bytes 786440 | tf_op jit(solution)/shard_map/ppermute | solution.py:498
  30.7 58.3 %copy-start.4 = (bf16[256,256]{1,0:T(8,128)(2,1)S(1)}, bf16[256,256]{1,0:T(8,128)(2,1)}, u32[]{:S(2)}) copy-start(bf16[256,256]{1,0:T(8,128)(2,1)} %w_self.1) | copy-start | bytes 393220
  30.7 58.3 %copy-start.5 = (bf16[256,256]{1,0:T(8,128)(2,1)S(1)}, bf16[256,256]{1,0:T(8,128)(2,1)}, u32[]{:S(2)}) copy-start(bf16[256,256]{1,0:T(8,128)(2,1)} %w_neigh.1) | copy-start | bytes 393220
  30.8 8.4 %collective-permute-start.6 = (bf16[8,128,128]{2,1,0:T(8,128)(2,1)S(1)}, bf16[8,128,128]{2,1,0:T(8,128)(2,1)S(1)}, u32[]{:S(2)}, u32[]{:S(2)}) collective-permute-start(bf16[8,128,128]{2,1,0:T(8,128)(2,1)S(1)} %get-tuple-element.48), channel_id=1, source_target_pairs={{0,32},{8,40},{16,48},{24,56},{32,0},{40,8},{48,16},{56,24},{64,96... | collective-permute-start | bytes 786440 | tf_op jit(solution)/shard_map/ppermute | solution.py:480
  32.5 11.1 %collective-permute-start.7 = (bf16[8,128,128]{2,1,0:T(8,128)(2,1)S(1)}, bf16[8,128,128]{2,1,0:T(8,128)(2,1)S(1)}, u32[]{:S(2)}, u32[]{:S(2)}) collective-permute-start(bf16[8,128,128]{2,1,0:T(8,128)(2,1)S(1)} %get-tuple-element.49), channel_id=1, source_target_pairs={{0,224},{8,232},{16,240},{24,248},{32,64},{40,72},{48,80},{56,88},... | collective-permute-start | bytes 786440 | tf_op jit(solution)/shard_map/ppermute | solution.py:494
  37.5 1.2 %copy-start.7 = (f32[8,256,128]{2,1,0:T(8,128)S(1)}, f32[8,256,128]{2,1,0:T(8,128)}, u32[]{:S(2)}) copy-start(f32[8,256,128]{2,1,0:T(8,128)} %copy-done.6) | copy-start | bytes 3145732
  44.1 2.1 %collective-permute-start.8 = (f32[256,256]{1,0:T(8,128)S(1)}, f32[256,256]{1,0:T(8,128)S(1)}, u32[]{:S(2)}, u32[]{:S(2)}) collective-permute-start(f32[256,256]{1,0:T(8,128)S(1)} %get-tuple-element.53), channel_id=1, source_target_pairs={{0,8},{8,0},{16,24},{24,16},{32,40},{40,32},{48,56},{56,48},{64,72... | collective-permute-start | bytes 786440 | tf_op jit(solution)/shard_map/ppermute | solution.py:54
  45.0 13.6 %collective-permute-start.9 = (bf16[4,256,128]{2,1,0:T(8,128)(2,1)S(1)}, bf16[4,256,128]{2,1,0:T(8,128)(2,1)S(1)}, u32[]{:S(2)}, u32[]{:S(2)}) collective-permute-start(bf16[4,256,128]{2,1,0:T(8,128)(2,1)S(1)} %get-tuple-element.55), channel_id=1, source_target_pairs={{0,64},{8,72},{16,80},{24,88},{32,96},{40,104},{48,112},{56,120},{... | collective-permute-start | bytes 786440 | tf_op jit(solution)/shard_map/ppermute | solution.py:480
  46.9 12.7 %all-to-all-start.1 = ((f32[16,16,256]{2,1,0:T(8,128)}), f32[16,16,256]{2,1,0:T(8,128)S(1)}, u32[]{:S(2)}, u32[]{:S(2)}) async-start(f32[16,16,256]{2,1,0:T(8,128)} %bitcast.6), calls=%async_computation.1 | async-start | bytes 524288 | tf_op jit(solution)/shard_map/all_to_all | solution.py:44
  60.3 12.7 %all-to-all-start.2 = ((f32[8,16,256]{2,1,0:T(8,128)}), f32[8,16,256]{2,1,0:T(8,128)S(1)}, u32[]{:S(2)}, u32[]{:S(2)}) async-start(f32[8,16,256]{2,1,0:T(8,128)} %get-tuple-element.56), calls=%async_computation.2 | async-start | bytes 262144 | tf_op jit(solution)/shard_map/all_to_all | solution.py:44
  65.1 3.8 %collective-permute-start.10 = (bf16[2,256,128]{2,1,0:T(8,128)(2,1)S(1)}, bf16[2,256,128]{2,1,0:T(8,128)(2,1)S(1)}, u32[]{:S(2)}, u32[]{:S(2)}) collective-permute-start(bf16[2,256,128]{2,1,0:T(8,128)(2,1)S(1)} %get-tuple-element.58), channel_id=1, source_target_pairs={{0,16},{8,24},{16,0},{24,8},{32,48},{40,56},{48,32},{56,40},{64,80... | collective-permute-start | bytes 393224 | tf_op jit(solution)/shard_map/ppermute | solution.py:498
  73.9 10.9 %all-to-all-start.3 = ((f32[16,16,256]{2,1,0:T(8,128)}), f32[16,16,256]{2,1,0:T(8,128)S(1)}, u32[]{:S(2)}, u32[]{:S(2)}) async-start(f32[16,16,256]{2,1,0:T(8,128)} %get-tuple-element.59), calls=%async_computation.3 | async-start | bytes 524288 | tf_op jit(solution)/shard_map/all_to_all | solution.py:44
  77.5 11.5 %collective-permute-start.12 = (bf16[1,256,128]{2,1,0:T(8,128)(2,1)S(1)}, bf16[1,256,128]{2,1,0:T(8,128)(2,1)S(1)}, u32[]{:S(2)}, u32[]{:S(2)}) collective-permute-start(bf16[1,256,128]{2,1,0:T(8,128)(2,1)S(1)} %get-tuple-element.61), channel_id=1, source_target_pairs={{0,128},{8,136},{16,144},{24,152},{32,160},{40,168},{48,176},{56,1... | collective-permute-start | bytes 196616 | tf_op jit(solution)/shard_map/ppermute | solution.py:480
  84.8 5.3 %collective-permute-start.11 = (f32[256,256]{1,0:T(8,128)S(1)}, f32[256,256]{1,0:T(8,128)S(1)}, u32[]{:S(2)}, u32[]{:S(2)}) collective-permute-start(f32[256,256]{1,0:T(8,128)S(1)} %bitcast.8), channel_id=1, source_target_pairs={{0,8},{8,0},{16,24},{24,16},{32,40},{40,32},{48,56},{56,48},{64,72... | collective-permute-start | bytes 786440 | tf_op jit(solution)/shard_map/ppermute | solution.py:54
